TPU v7x, 32 devices: a whole 2x2x4 slice. The times are simulated.
32 devices in a mesh: gx: 4 (over x, core), gy: 4 (over z), gz: 2 (over y).
Axes of the slice: x: 2, y: 2, z: 4, core: 2. Of those that a mesh axis runs over, the one named last changes fastest.
Arguments:
- bin_mass: float32 [32, 32, 32, 64], P('gx', 'gy', 'gz'), may hold values from 0.02 to 2
- courant: float32 [3, 32, 32, 32], P(None, 'gx', 'gy', 'gz'), may hold values from 0.05 to 0.3
- sub_courant: float32 [64], replicated, may hold values from 0.3 to 0.9
- fall_steps: int32 [64], replicated, may hold values from 1 to 24, as said below
- frag_gain: bfloat16 [4096, 64], replicated, may hold values from -0.01171875 to 0.01171875
- collide: bfloat16 [64, 64], replicated, may hold values from 0.0019989014 to 0.019897461
Outputs:
- updated_mass: float32 [32, 32, 32, 64], P('gx', 'gy', 'gz')
- rainfall: float32 [32, 32, 64], P('gx', ('gy', 'gz'))
Inputs may be any that keep to these rules, and one draw needn't show every extreme that they name: `fall_steps`: some bin takes 24 substeps.
All inputs are finite; a program needn't handle non-finite values.
Results may differ from a plain program's by a relative error of at most 0.003.
Values sent between devices are 32-bit elements; how exact they have to be, the bound alone decides.
No kernel may reach another device: no remote copies, remote signals or barrier semaphores. Data moves between devices by JAX's collectives and lax.ppermute only.
A program may use at most 64 MiB of HBM per device.

v0:
```python
import functools
import itertools

import jax
import jax.numpy as jnp
from jax import lax
from jax.experimental import pallas as pl
from jax.experimental.pallas import tpu as pltpu
from jax.sharding import PartitionSpec as P

SUBS = 24
EPS = 1e-06
LO, HI = 3, 2
PAD_LO, PAD_HI = 2 * LO, 2 * HI
LINES = LO + HI
ROWS, LANES = 8, 128
AHEAD = 4
EARLY = 6
F32 = jnp.float32
VMEM = pl.BlockSpec(memory_space=pltpu.VMEM)


def lane_ids():
    return lax.broadcasted_iota(jnp.int32, (ROWS, LANES), 1)


def pick(tile, ids):
    return jnp.take_along_axis(tile, ids, axis=1, mode="promise_in_bounds")


def turn(tile, lanes):
    lanes %= LANES
    return pltpu.roll(tile, lanes, 1) if lanes else tile


def rows_of(first, count=1):
    return pl.ds(first * ROWS, count * ROWS)


def eight(first, level, step=1):
    return pl.ds(first * ROWS + level, ROWS, stride=step * ROWS)


def order(a, b, straight):
    return jnp.where(straight, a, b), jnp.where(straight, b, a)


def is_even(axis):
    return lax.axis_index(axis) % 2 == 0


def by_quarter(parts):
    quarter = lane_ids() // (LANES // 4)
    return jnp.where(quarter < 2, jnp.where(quarter == 0, parts[0], parts[1]), jnp.where(quarter == 2, parts[2], parts[3]))


def groups(parts):
    width = LANES // (2 * parts)
    return width, width // ROWS, ROWS * ROWS // width


def spread(jobs, parts):
    width, deep, _ = groups(parts)
    place = lane_ids() % width
    rows = [[], []]
    for tile, x, y, _, _ in jobs:
        top = tile.astype(jnp.bfloat16).astype(F32)
        here = place == x % deep * ROWS + y
        for out, term in zip(rows, (top, tile - top)):
            out.append(jnp.where(here, term, 0.0))
    terms = jnp.concatenate([jnp.concatenate(r, axis=0).astype(jnp.bfloat16) for r in rows], axis=1)
    source, target = [lax.broadcasted_iota(jnp.int32, (2 * LANES, LANES), k) for k in range(2)]
    same = jnp.where(source % LANES // width == target // width, 1.0, 0.0).astype(jnp.bfloat16)
    out = jnp.dot(terms, same, preferred_element_type=F32)
    for k, (_, _, _, ref, at) in enumerate(jobs):
        ref[rows_of(at)] = out[k * ROWS : (k + 1) * ROWS]


def halo_line(i, n):
    return jnp.where(i < LO, i - LO, i - LO + n)


def line_change(cells, winds):
    return changes(line_fluxes(cells, winds))


def changes(fluxes):
    return [a - b for a, b in zip(fluxes, fluxes[1:])]


def long_line(cells, winds, low_edge, high_edge, n):
    begin, end = LO, n - HI
    low = line_fluxes(cells[: PAD_LO + begin + 1], winds[: LO + 1 + begin]) + [low_edge]
    high = [high_edge] + line_fluxes(cells[PAD_LO + end - HI :], winds[LO + 1 + end :])
    return dict(zip(range(-LO, begin), changes(low))) | dict(zip(range(end, n + HI), changes(high)))


def line_fluxes(cells, winds):
    first = [b - a for a, b in zip(cells, cells[1:])]
    twice = [d + d for d in first]
    second = [b - a for a, b in zip(first, first[1:])]
    third = [a - b for a, b in zip(second, second[1:])]
    curved = [(13.0 / 3.0) * (c * c) + 4.0 * EPS for c in second]
    fluxes = []
    for j in range(len(cells) - 4):
        left = twice[j + 1] + second[j]
        mid = first[j + 1] + first[j + 2]
        right = twice[j + 2] - second[j + 2]
        e0 = curved[j] + left * left
        e1 = curved[j + 1] + mid * mid
        e2 = curved[j + 2] + right * right
        e0 = e0 * e0
        e1 = e1 * e1
        e2 = e2 * e2
        e0 = 3.0 * e0
        e2_twice = e2 + e2
        top = e1 * (e2_twice * third[j] + e0 * third[j + 1])
        low = e1 * (e2 + e0) + e0 * e2_twice
        inverse = pl.reciprocal(low, approx=True)
        estimate = 6.0 * cells[j + 2] + (first[j + 1] + twice[j + 2]) + top * inverse
        fluxes.append((winds[j] + winds[j + 1]) * estimate)
    return fluxes


def from_below(value, width):
    return jnp.where(lane_ids() < width, 0.0, turn(value, width))


def from_above(value, width):
    return jnp.where(lane_ids() >= LANES - width, 0.0, turn(value, -width))


def level_change(cells, winds, width):
    long_cells = [from_below(v, width) for v in cells[ROWS - LO :]] + cells + [from_above(v, width) for v in cells[:HI]]
    long_winds = [from_below(winds[-1], width)] + winds + [from_above(winds[0], width)]
    return line_change(long_cells, long_winds)


def pack_kernel(mass_ref, send_ref, keep_ref):
    lower = is_even("gz")
    n = mass_ref.shape[0]
    zero = jnp.zeros((ROWS, LANES // 2), F32)
    for x in range(n // 2):
        for y in range(n):
            tiles = [
                jnp.concatenate([mass_ref[xx, y, z : z + ROWS], zero], axis=1) for xx in (x, x + n // 2) for z in (0, ROWS)
            ]
            low = by_quarter([turn(v, 32 * k) for k, v in enumerate(tiles)])
            high = by_quarter([turn(v, 32 * k - 32) for k, v in enumerate(tiles)])
            at = rows_of(x * n + y)
            keep_ref[at], send_ref[at] = order(low, high, lower)


def wind_kernel(wind_ref, keep_ref, out_ref):
    del keep_ref
    n = wind_ref.shape[1]
    for d in range(3):
        levels = wind_ref[d].reshape(n * n, 2 * ROWS).T * (1.0 / 12.0)
        out_ref[rows_of(d)] = jnp.concatenate([levels[:ROWS], levels[ROWS:]], axis=1)


def sides(axis, first_ref, second_ref):
    even, place = is_even(axis), lax.axis_index(axis)
    inner_low, inner_high = place > 0, place < lax.axis_size(axis) - 1

    def below(at):
        return jnp.where(inner_low, jnp.where(even, second_ref[at], first_ref[at]), 0.0)

    def above(at):
        return jnp.where(inner_high, jnp.where(even, first_ref[at], second_ref[at]), 0.0)

    return below, above


def by_parity(axis, body):
    even = is_even(axis)
    pl.when(even)(lambda: body(0, 1))
    pl.when(jnp.logical_not(even))(lambda: body(1, 0))


def merge_kernel(keep_ref, got_ref, own_wind_ref, got_wind_ref, lost_ref, block_ref, y_first, y_second, x_first, x_second):
    del lost_ref
    n = 8
    lower = is_even("gz")
    low = lane_ids() < 64
    for x in range(n // 2):
        for y in range(n):
            at = rows_of(x * n + y)
            a, b = order(keep_ref[at], got_ref[at], lower)
            block_ref[at] = jnp.where(low, a, turn(b, 64))
            block_ref[rows_of((x + n // 2) * n + y)] = jnp.where(low, turn(a, 64), b)
    for d in range(3):
        a, b = order(own_wind_ref[rows_of(d)], got_wind_ref[rows_of(d)], lower)
        block_ref[rows_of(n * n + 2 * d)] = by_quarter([a, turn(a, -32), turn(b, 64), turn(b, 32)])
        block_ref[rows_of(n * n + 2 * d + 1)] = by_quarter([turn(a, -32), turn(a, -64), turn(b, 32), b])

    def along_y(up, down):
        for ref, start, wide in (((y_first, y_second)[up], n - PAD_LO, PAD_LO), ((y_first, y_second)[down], 0, PAD_HI)):
            for x in range(n):
                ref[rows_of(x * wide, wide)] = block_ref[rows_of(x * n + start, wide)]
            ref[rows_of(n * wide, 6)] = block_ref[rows_of(n * n, 6)]

    def along_x(up, down):
        for ref, start, wide, part in (((x_first, x_second)[up], n - PAD_LO, PAD_LO, 1), ((x_first, x_second)[down], 0, PAD_HI, 0)):
            ref[rows_of(0, wide * n)] = block_ref[rows_of(start * n, wide * n)]
            for d in range(3):
                ref[rows_of(wide * n + d)] = block_ref[rows_of(n * n + 2 * d + part)]

    by_parity("gy", along_y)
    by_parity("gx", along_x)


def corner_kernel(n, parts, first_ref, second_ref, own_change, *messages):
    del own_change
    tiles = groups(parts)[2]
    half = tiles // 2
    below, above = sides("gy", first_ref, second_ref)

    def body(up, down):
        for ref, start, narrow, part in ((messages[up], n - LO, LO, half), (messages[down], 0, HI, 0)):
            at = 0
            for x in range(start, start + narrow):
                ref[rows_of(at, LO)] = below(rows_of(x * PAD_LO + PAD_LO - LO, LO))
                ref[rows_of(at + LO, HI)] = above(rows_of(x * PAD_HI, HI))
                at += LINES
            for side, base in ((below, n * PAD_LO), (above, n * PAD_HI)):
                ref[rows_of(at)] = side(rows_of(base + (tiles - 1 if part else 0)))
                ref[rows_of(at + 1, half)] = side(rows_of(base + tiles + part, half))
                at += 1 + half

    by_parity("gx", body)


def own_kernel(n, parts, block_ref, wind_x, wind_y, wind_z, change, edge_x, edge_y):
    width, deep, tiles = groups(parts)
    for d, out in enumerate((wind_x, wind_y, wind_z)):
        jobs = []
        for x in range(n):
            tile = block_ref[rows_of(n * n + d * tiles + x // deep)]
            jobs += [(tile, x, y, out, x * n + y) for y in range(n)]
        spread(jobs, parts)

    @pl.loop(0, n)
    def _(x):
        cells = [block_ref[eight(x * n, k)] for k in range(ROWS)]
        winds = [wind_z[eight(x * n, k)] for k in range(ROWS)]
        for k, value in enumerate(level_change(cells, winds, width)):
            change[eight(x * n, k)] = value

    begin, end = LO, n - HI
    for wind, edge, place in ((wind_x, edge_x, lambda i, k: k * n + i), (wind_y, edge_y, lambda i, k: i * n + k)):

        @pl.loop(0, n)
        def _(i):
            cells = [block_ref[rows_of(place(i, k))] for k in range(n)]
            fluxes = line_fluxes(cells, [wind[rows_of(place(i, k))] for k in range(begin - 1, end + 1)])
            edge[rows_of(i)] = fluxes[0]
            edge[rows_of(n + i)] = fluxes[-1]
            for k, value in zip(range(begin, end), changes(fluxes)):
                at = rows_of(place(i, k))
                change[at] = change[at] + value


def y_kernel(n, parts, block_ref, first_ref, second_ref, wind_y, own_change, edge_y, *refs):
    width, deep, tiles = groups(parts)
    cell, change, wind_x, far_y, wind_z, halo_change = refs
    below, above = sides("gy", first_ref, second_ref)
    span, reach = n + PAD_LO + PAD_HI, n + LINES

    for x in range(n):
        cell[rows_of(x * span, PAD_LO)] = below(rows_of(x * PAD_LO, PAD_LO))
        cell[rows_of(x * span + PAD_LO, n)] = block_ref[rows_of(x * n, n)]
        cell[rows_of(x * span + PAD_LO + n, PAD_HI)] = above(rows_of(x * PAD_HI, PAD_HI))
    jobs = []
    for d in range(3):
        for t in range(tiles):
            low, high = below(rows_of(n * PAD_LO + d * tiles + t)), above(rows_of(n * PAD_HI + d * tiles + t))
            for x in range(t * deep, (t + 1) * deep):
                if d == 1:
                    jobs += [(low, x, n - LO - 1 + y, far_y, x * (LINES + 2) + y) for y in range(LO + 1)]
                    jobs += [(high, x, y, far_y, x * (LINES + 2) + LO + 1 + y) for y in range(HI + 1)]
                else:
                    out = wind_z if d else wind_x
                    jobs += [(low, x, n - LO + y, out, y * n + x) for y in range(LO)]
                    jobs += [(high, x, y, out, (LO + y) * n + x) for y in range(HI)]
    spread(jobs, parts)

    @pl.loop(0, LINES)
    def _(i):
        first = halo_line(i, n) + PAD_LO
        cells = [cell[eight(first, k, span)] for k in range(ROWS)]
        winds = [wind_z[eight(i * n, k)] for k in range(ROWS)]
        for k, value in enumerate(level_change(cells, winds, width)):
            halo_change[eight(i * n, k)] = value

    @pl.loop(0, n)
    def _(x):
        cells = [cell[rows_of(x * span + y)] for y in range(span)]
        far = [far_y[rows_of(x * (LINES + 2) + y)] for y in range(LINES + 2)]
        winds = far[: LO + 1] + [wind_y[rows_of(x * n + y)] for y in range(n)] + far[LO + 1 :]
        for y, value in long_line(cells, winds, edge_y[rows_of(x)], edge_y[rows_of(n + x)], n).items():
            if 0 <= y < n:
                value = value + own_change[rows_of(x * n + y)]
            else:
                value = value + halo_change[rows_of((y + LO if y < 0 else y + LO - n) * n + x)]
            change[rows_of(x * reach + y + LO)] = value
        for y in range(LO, n - HI):
            change[rows_of(x * reach + y + LO)] = own_change[rows_of(x * n + y)]


def inside(axis):
    place = lax.axis_index(axis)
    return [jnp.where(ok, 1.0, 0.0) for ok in (place > 0, place < lax.axis_size(axis) - 1)]


def inner_kernel(n, parts, cell, change, halo_wind_x, wind_y, far_wind_y, wind_z, edge_x, one, edge, second):
    width = groups(parts)[0]
    span, reach = n + PAD_LO + PAD_HI, n + LINES
    begin, end = LO, n - HI
    south_in, north_in = inside("gy")

    for k in range(2):
        edge[rows_of(k * reach + LO, n)] = edge_x[rows_of(k * n, n)]
    for i in range(end - begin):
        x = begin + i
        one[rows_of(i * reach + LO, n)] = cell[rows_of(x * span + PAD_LO, n)] + change[rows_of(x * reach + LO, n)]

    @pl.loop(0, LINES)
    def _(i):
        at = halo_line(i, n) + LO
        cells = [cell[rows_of(x * span + LO + at)] for x in range(n)]
        fluxes = line_fluxes(cells, [halo_wind_x[rows_of(i * n + x)] for x in range(begin - 1, end + 1)])
        edge[rows_of(at)] = fluxes[0]
        edge[rows_of(reach + at)] = fluxes[-1]
        keep = jnp.where(i < LO, south_in, north_in)
        for k, value in enumerate(changes(fluxes)):
            x = begin + k
            one[rows_of(k * reach + at)] = (cells[x] + (value + change[rows_of(x * reach + at)])) * keep

    @pl.loop(0, end - begin)
    def _(i):
        second_y_z(n, width, begin + i, one, i, wind_y, far_wind_y, wind_z, second, i)


def second_y_z(n, width, x, one, one_x, wind_y, far_wind_y, wind_z, second, second_x):
    reach = n + LINES
    cells = [one[rows_of(one_x * reach + y)] for y in range(reach)]
    winds = [far_wind_y[rows_of(x * (LINES + 2) + LO)]] + [wind_y[rows_of(x * n + y)] for y in range(n)]
    winds += [far_wind_y[rows_of(x * (LINES + 2) + LO + 1)]]
    for y, value in enumerate(line_change(cells, winds)):
        second[rows_of(second_x * n + y)] = value
    cells = [one[eight(one_x * reach + LO, k)] for k in range(ROWS)]
    winds = [wind_z[eight(x * n, k)] for k in range(ROWS)]
    for k, value in enumerate(level_change(cells, winds, width)):
        at = eight(second_x * n, k)
        second[at] = second[at] + value


def x_kernel(n, parts, cell, change, wind_x, edge, second_ref, first_ref, mid, far_wind_x, side, side_wind_y, *scratch):
    far, side_wind_z, side_change = scratch
    width, deep, tiles = groups(parts)
    half = tiles // 2
    west, east = sides("gx", first_ref, second_ref)
    span, reach = n + PAD_LO + PAD_HI, n + LINES

    jobs = []
    for take, wide, near_from, far_from, line in ((west, PAD_LO, LO, 0, 0), (east, PAD_HI, 0, HI, LO)):
        narrow = wide // 2
        side[rows_of(line * n, narrow * n)] = take(rows_of(near_from * n, narrow * n))
        far[rows_of(line * n, narrow * n)] = take(rows_of(far_from * n, narrow * n))
        layers, shift = (range(n - narrow, n), half) if line == 0 else (range(narrow), 0)
        wider = range(n - narrow - 1, n) if line == 0 else range(narrow + 1)

        def winds_of(d, x):
            return take(rows_of(wide * n + d * half + x // deep - shift))

        for i, x in enumerate(wider):
            jobs += [(winds_of(0, x), x, y, far_wind_x, (line + bool(line) + i) * n + y) for y in range(n)]
        for d, out in ((1, side_wind_y), (2, side_wind_z)):
            for i, x in enumerate(layers):
                jobs += [(winds_of(d, x), x, y, out, (line + i) * n + y) for y in range(n)]
    spread(jobs, parts)

    @pl.loop(0, LINES)
    def _(i):
        cells = [side[eight(i * n, k)] for k in range(ROWS)]
        winds = [side_wind_z[eight(i * n, k)] for k in range(ROWS)]
        for k, value in enumerate(level_change(cells, winds, width)):
            side_change[eight(i * n, k)] = value

    @pl.loop(0, n)
    def _(y):
        outer = [far[rows_of(i * n + y)] for i in range(LINES)]
        near = [side[rows_of(i * n + y)] for i in range(LINES)]
        cells = outer[:LO] + near[:LO] + [cell[rows_of(x * span + PAD_LO + y)] for x in range(n)] + near[LO:] + outer[LO:]
        winds = [far_wind_x[rows_of(i * n + y)] for i in range(LINES + 2)]
        winds = winds[: LO + 1] + [wind_x[rows_of(x * n + y)] for x in range(n)] + winds[LO + 1 :]
        for x, value in long_line(cells, winds, edge[rows_of(LO + y)], edge[rows_of(reach + LO + y)], n).items():
            if 0 <= x < n:
                value = value + change[rows_of(x * reach + LO + y)]
            else:
                value = value + side_change[rows_of((x + LO if x < 0 else x + LO - n) * n + y)]
            mid[rows_of((x + LO) * n + y)] = cells[PAD_LO + x] + value


def main_kernel(n, parts, *refs):
    cell, change, wind_x, wind_y, wind_z, halo_wind_x, far_wind_y, inner, edge, inner_second = refs[:10]
    mid, far_wind_x, side, side_wind_y, second_ref, first_ref, rate_ref, steps_ref = refs[10:18]
    one, *out_refs = refs[18:21]
    corner, corner_wind_x, edge_wind_y, second, fallen = refs[21:]
    deep, tiles = groups(parts)[1:]
    half = tiles // 2
    west, east = sides("gx", first_ref, second_ref)
    span, reach = n + PAD_LO + PAD_HI, n + LINES

    jobs = []
    for take, narrow, line in ((west, LO, 0), (east, HI, LO)):
        at = narrow * LINES
        corner[rows_of(line * LINES, at)] = take(rows_of(0, at))
        below, above = at, at + 1 + half
        layers, shift = (range(n - narrow, n), half) if line == 0 else (range(narrow), 0)
        for y in range(LINES):
            tile = take(rows_of(below if y < LO else above))
            x = layers[-1] if line == 0 else layers[0]
            jobs.append((tile, x, n - LO + y if y < LO else y - LO, corner_wind_x, bool(line) * LINES + y))
        for i, x in enumerate(layers):
            tile = x // deep - shift
            jobs.append((take(rows_of(below + 1 + tile)), x, n - 1, edge_wind_y, 2 * (line + i)))
            jobs.append((take(rows_of(above + 1 + tile)), x, 0, edge_wind_y, 2 * (line + i) + 1))
    spread(jobs, parts)

    west_in, east_in = inside("gx")
    south_in, north_in = inside("gy")
    begin, end = LO, n - HI
    one[rows_of((begin + LO) * reach, (end - begin) * reach)] = inner[...]
    for x in [x for x in range(n) if not begin <= x < end]:
        one[rows_of((x + LO) * reach + LO, n)] = mid[rows_of((x + LO) * n, n)]

    @pl.loop(0, LINES)
    def _(i):
        corners = [corner[rows_of(i * LINES + y)] for y in range(LINES)]
        cells = corners[:LO] + [side[rows_of(i * n + y)] for y in range(n)] + corners[LO:]
        winds = [side_wind_y[rows_of(i * n + y)] for y in range(n)]
        winds = [edge_wind_y[rows_of(2 * i)]] + winds + [edge_wind_y[rows_of(2 * i + 1)]]
        keep = jnp.where(i < LO, west_in, east_in)
        line = halo_line(i, n) + LO
        for y, value in enumerate(line_change(cells, winds)):
            one[rows_of(line * reach + LO + y)] = (mid[rows_of(line * n + y)] + value) * keep

    @pl.loop(0, LINES)
    def _(i):
        line = halo_line(i, n) + LO
        near = [corner[rows_of(k * LINES + i)] for k in range(LINES)]
        cells = near[:LO] + [cell[rows_of(x * span + LO + line)] for x in range(n)] + near[LO:]
        winds = [halo_wind_x[rows_of(i * n + x)] for x in range(n)]
        winds = [corner_wind_x[rows_of(i)]] + winds + [corner_wind_x[rows_of(LINES + i)]]
        keep = jnp.where(i < LO, south_in, north_in)
        low = line_fluxes(cells[: LO + begin + 1], winds[: begin + 1]) + [edge[rows_of(line)]]
        high = [edge[rows_of(reach + line)]] + line_fluxes(cells[LO + end - HI :], winds[end + 1 :])
        values = dict(zip(range(begin), changes(low))) | dict(zip(range(end, n), changes(high)))
        for x, value in values.items():
            one[rows_of((x + LO) * reach + line)] = (cells[x + LO] + (value + change[rows_of(x * reach + line)])) * keep

    fall_layers(
        n, parts, 0, EARLY, one, cell, wind_x, far_wind_x, wind_y, far_wind_y, wind_z, inner_second, rate_ref, steps_ref,
        out_refs, second, fallen,
    )


def late_kernel(
    n, parts, one, cell, wind_x, far_wind_x, wind_y, far_wind_y, wind_z, inner_second, rate_ref, steps_ref, *refs
):
    fall_layers(
        n, parts, EARLY, n, one, cell, wind_x, far_wind_x, wind_y, far_wind_y, wind_z, inner_second, rate_ref, steps_ref,
        refs[:2], *refs[2:],
    )


def fall_layers(
    n, parts, begin, end, one, cell, wind_x, far_wind_x, wind_y, far_wind_y, wind_z, inner_second, rate_ref, steps_ref,
    out_refs, second, fallen,
):
    width = groups(parts)[0]
    span, reach, count = n + PAD_LO + PAD_HI, n + LINES, end - begin
    ready = [x for x in range(LO, n - HI) if begin <= x < end]
    left = [x for x in range(begin, end) if x not in ready]
    if ready:
        second[rows_of((ready[0] - begin) * n, len(ready) * n)] = inner_second[rows_of((ready[0] - LO) * n, len(ready) * n)]

    @pl.loop(left[0], left[-1] + 1)
    def _(x):
        second_y_z(n, width, x, one, x + LO, wind_y, far_wind_y, wind_z, second, x - begin)

    @pl.loop(0, n)
    def _(y):
        cells = [one[rows_of(x * reach + LO + y)] for x in range(begin, end + LINES)]
        winds = [wind_x[rows_of(x * n + y)] for x in range(max(begin - 1, 0), min(end + 1, n))]
        if begin == 0:
            winds = [far_wind_x[rows_of(LO * n + y)]] + winds
        if end == n:
            winds = winds + [far_wind_x[rows_of((LO + 1) * n + y)]]
        for i, value in enumerate(line_change(cells, winds)):
            value = cells[i + LO] + (value + second[rows_of(i * n + y)])
            fallen[rows_of(i * n + y)] = 0.5 * cell[rows_of((begin + i) * span + PAD_LO + y)] + 0.5 * value

    bins = LANES // 2 // parts
    ids = lax.axis_index("gz") * bins + lane_ids() % bins
    rates, steps = [
        pick(jnp.broadcast_to(jnp.concatenate([ref[...]] * 2, axis=1), (ROWS, LANES)), ids) for ref in (rate_ref, steps_ref)
    ]

    rain = []
    for some in [range(i, min(i + 3, count)) for i in range(0, count, 3)]:
        columns = [[fallen[eight(i * n, k)] for k in range(ROWS)] for i in some]
        drops = [jnp.zeros((ROWS, LANES), F32) for _ in some]
        for block in range(SUBS // AHEAD):
            columns = [column + [from_above(v, width) for v in column[:AHEAD]] for column in columns]
            for s in range(AHEAD):
                rate = jnp.where(block * AHEAD + s < steps, rates, 0.0)
                for i, column in enumerate(columns):
                    drops[i] = drops[i] + rate * column[0]
                    columns[i] = [v + rate * (u - v) for v, u in zip(column, column[1:])]
        for i, column in zip(some, columns):
            for k in range(ROWS):
                fallen[eight(i * n, k)] = column[k]
        rain += drops

    if parts == 2:
        send_ref, keep_ref = out_refs
        lower = is_even("gz")
        low = lane_ids() < 64
        half = count * n // 2
        for c in range(half):
            a, b = fallen[rows_of(c)], fallen[rows_of(half + c)]
            at = rows_of(c)
            keep_ref[at], send_ref[at] = order(jnp.where(low, a, turn(b, 64)), jnp.where(low, turn(a, 64), b), lower)
        for j in range(0, count, 4):
            four = (rain[j : j + 4] + rain[j:] * 3)[:4]
            value = by_quarter([turn(v, 32 * i) for i, v in enumerate(four)])
            keep_ref[rows_of(half + j // 4)] = value
            send_ref[rows_of(half + j // 4)] = value
    else:
        settled_ref, rain_ref = out_refs
        settled_ref[...] = fallen[...]
        for i in range(count):
            rain_ref[rows_of(i)] = rain[i]


def matrix_kernel(bins, gain_ref, loss_ref, pairs_ref, lost_ref, wide, tall):
    zero = jnp.zeros((bins, LANES - bins), F32)
    shifts = bins // 2

    @pl.loop(0, bins)
    def _(i):
        rows = gain_ref[pl.ds(i * bins, bins)].astype(F32)
        rows = jnp.concatenate([rows, zero], axis=1)
        wide[pl.ds(i * 2 * bins, bins)] = rows
        wide[pl.ds(i * 2 * bins + bins, bins)] = rows
        tall[pl.ds(i * bins, bins)] = rows

        @pl.when(i < shifts)
        def _():
            tall[pl.ds((i + bins) * bins, bins)] = rows

    for d in range(shifts + 1):
        rows = wide[pl.ds(d, bins, stride=2 * bins + 1)]
        if 0 < d < shifts:
            rows = rows + tall[pl.ds(d * bins, bins, stride=bins + 1)]
        pairs_ref[pl.ds(d * LANES, bins)] = rows.astype(jnp.bfloat16)
        pairs_ref[pl.ds(d * LANES + bins, bins)] = pltpu.roll(rows, bins, 1).astype(jnp.bfloat16)
    rows = jnp.concatenate([loss_ref[...].astype(F32), zero], axis=1)
    lost_ref[pl.ds(0, bins)] = rows.astype(jnp.bfloat16)
    lost_ref[pl.ds(bins, bins)] = pltpu.roll(rows, bins, 1).astype(jnp.bfloat16)


def breakup_rows(mass, pairs_ref, lost_ref, products):
    bins = LANES // 2
    count = mass.shape[0]
    lanes = lane_ids()
    rounded = mass.astype(jnp.bfloat16)
    wide = rounded.astype(F32)
    gained = None
    shifts = bins // 2 + 1
    for begin in range(0, shifts, 4):
        end = min(begin + 4, shifts)
        for d in range(begin, end):
            ids = lanes // bins * bins + (lanes + d) % bins
            for r in range(0, count, 2 * ROWS):
                halves = [wide[r + ROWS * k : r + ROWS * (k + 1)] for k in range(2)]
                halves = [v * pick(v, ids) if d else v * v for v in halves]
                both = jnp.concatenate(halves, axis=0).astype(jnp.bfloat16)
                products[pl.ds(r, 2 * ROWS), d * LANES : (d + 1) * LANES] = both
        part = jnp.dot(
            products[pl.ds(0, count), begin * LANES : end * LANES],
            pairs_ref[pl.ds(begin * LANES, (end - begin) * LANES)],
            preferred_element_type=F32,
        )
        gained = part if gained is None else gained + part
    loss = jnp.dot(rounded, lost_ref[...], preferred_element_type=F32)
    return mass + gained - mass * loss


def breakup_layers(n, count, keep_ref, got_ref, pairs_ref, lost_ref, columns, products):
    first = is_even("gz")
    half = count * n // 2
    for c in range(half):
        a, b = order(keep_ref[rows_of(c)], got_ref[rows_of(c)], first)
        columns[rows_of(c)] = by_quarter([a, turn(b, 32), turn(a, 32), turn(b, 64)])
        columns[rows_of(half + c)] = by_quarter([turn(a, -64), turn(b, -32), turn(a, -32), b])
    rain = []
    for i in range(count):
        a, b = order(keep_ref[rows_of(half + i // 4)], got_ref[rows_of(half + i // 4)], first)
        a, b = [jnp.where(first, v[: n // 2], v[n // 2 :])[:, 32 * (i % 4) : 32 * (i % 4) + 32] for v in (a, b)]
        rain.append(jnp.concatenate([a, b], axis=1))
    columns[...] = breakup_rows(columns[...], pairs_ref, lost_ref, products)
    return rain


def lay_out(columns, mass, n, count):
    for x in range(count):
        for y in range(n):
            value = columns[rows_of(x * n + y)]
            mass[x, y, 0:ROWS] = value[:, :64]
            mass[x, y, ROWS : 2 * ROWS] = value[:, 64:]


def breakup_first_kernel(n, keep_ref, got_ref, pairs_ref, lost_ref, mass_ref, rain_ref, columns, products):
    for i, value in enumerate(breakup_layers(n, EARLY, keep_ref, got_ref, pairs_ref, lost_ref, columns, products)):
        rain_ref[i] = value
    lay_out(columns, mass_ref, n, EARLY)


def breakup_last_kernel(
    n, keep_ref, got_ref, pairs_ref, lost_ref, early, early_rain, mass_out, rain_out, columns, products, mass, rain, sems
):
    early_copy = pltpu.make_async_copy(early, mass_out.at[pl.ds(0, EARLY)], sems.at[0])
    early_copy.start()
    late_rain = breakup_layers(n, n - EARLY, keep_ref, got_ref, pairs_ref, lost_ref, columns, products)
    for i in range(EARLY):
        rain[i] = early_rain[i]
    for i, value in enumerate(late_rain):
        rain[EARLY + i] = value
    rain_copy = pltpu.make_async_copy(rain, rain_out, sems.at[2])
    rain_copy.start()
    lay_out(columns, mass, n, n - EARLY)
    late_copy = pltpu.make_async_copy(mass, mass_out.at[pl.ds(EARLY, n - EARLY)], sems.at[1])
    late_copy.start()
    for copy in (early_copy, rain_copy, late_copy):
        copy.wait()


def breakup_plain_kernel(mass_ref, pairs_ref, lost_ref, out_ref, products):
    count = products.shape[0]

    @pl.loop(0, mass_ref.shape[0] // count)
    def _(i):
        start = pl.multiple_of(i * count, count)
        out_ref[pl.ds(start, count)] = breakup_rows(mass_ref[pl.ds(start, count)], pairs_ref, lost_ref, products)


def shape(*dims, dtype=F32):
    return jax.ShapeDtypeStruct(dims, dtype)


def tiles_of(count):
    return shape(count * ROWS, LANES)


def call(kernel, outs, args, scratch=(), micros=1.0, out_place=pltpu.VMEM, copies=0):
    scratch = [pltpu.VMEM(s.shape, s.dtype) for s in scratch]
    if copies:
        scratch.append(pltpu.SemaphoreType.DMA((copies,)))
    return pl.pallas_call(
        kernel,
        out_shape=outs,
        in_specs=[VMEM] * len(args),
        out_specs=jax.tree.map(lambda _: pl.BlockSpec(memory_space=out_place), outs),
        scratch_shapes=scratch,
        compiler_params=pltpu.CompilerParams(vmem_limit_bytes=40 << 20),
        cost_estimate=pl.CostEstimate(
            flops=int(micros * 1.1e9), bytes_accessed=int(micros * 3.6e6), transcendentals=0
        ),
    )(*args)


def swap_neighbours(axis, begin, message):
    axes = ("gx", "gy", "gz")
    sizes = [lax.axis_size(a) for a in axes]
    along, other = (0, 2) if axis == "gx" else (1, 0)

    def partner(place, start, count):
        to = start + ((place - start) ^ 1)
        return to if start <= place and to < count else place

    index = {place: i for i, place in enumerate(itertools.product(*map(range, sizes)))}
    pairs = []
    for place, i in index.items():
        to = list(place)
        to[along] = partner(place[along], begin, sizes[along])
        if to[along] == place[along]:
            to[other] = partner(place[other], 0, sizes[other])
        pairs.append((i, index[tuple(to)]))
    return lax.ppermute(message, axes, pairs)


def per_device(bin_mass, courant, sub_courant, fall_steps, frag_gain, collide):
    nx, ny, nz, bins = bin_mass.shape
    n = nx
    parts = lax.axis_size("gz")
    gz, gy = lax.axis_index("gz"), lax.axis_index("gy")
    width = bins // parts
    tiles = groups(parts)[2]
    winds = 3 * tiles

    pair_rows = (bins // 2 + 1) * LANES
    pairs, lost = call(
        functools.partial(matrix_kernel, bins),
        (shape(pair_rows, LANES, dtype=jnp.bfloat16), shape(LANES, LANES, dtype=jnp.bfloat16)),
        (frag_gain, collide),
        [shape(2 * bins * bins, LANES), shape(3 * bins * bins // 2, LANES)],
        micros=0.02,
    )

    y_message = tiles_of(n * PAD_LO + winds)
    x_message = tiles_of(n * PAD_LO + winds // 2)
    if parts == 2:
        half = tiles_of(n * n // 2)
        send, keep = call(pack_kernel, (half, half), (bin_mass,), micros=0.3)
        got = lax.ppermute(send, "gz", [(0, 1), (1, 0)])
        own_wind = call(wind_kernel, tiles_of(3), (courant, keep), micros=0.1)
        got_wind = lax.ppermute(own_wind, "gz", [(0, 1), (1, 0)])
        block, *messages = call(
            merge_kernel,
            [tiles_of(n * n + winds), y_message, y_message, x_message, x_message],
            (keep, got, own_wind, got_wind, lost),
            micros=0.2,
        )
    else:
        split = bin_mass.reshape(nx, ny, nz // ROWS, ROWS, parts, width).transpose(4, 0, 1, 3, 2, 5)
        split = lax.all_to_all(split, "gz", split_axis=0, concat_axis=0, tiled=True)
        cube = split.transpose(1, 2, 3, 0, 4, 5).reshape(n, n, ROWS, LANES)
        air = courant.reshape(3, nx, ny, nz // ROWS, ROWS).transpose(0, 4, 3, 1, 2) * (1.0 / 12.0)
        air = lax.all_gather(air, "gz").reshape(parts, 3, ROWS, nz // ROWS, tiles, nx // tiles, ny)
        air = air.transpose(1, 4, 2, 0, 3, 5, 6).reshape(3, tiles, ROWS, LANES)
        block = jnp.concatenate([cube.reshape(-1, LANES), air.reshape(-1, LANES)])
        messages = []
        for layers, low_air, high_air, message, even in (
            (cube.transpose(1, 0, 2, 3), air, air, y_message, gy % 2 == 0),
            (cube, air[:, : tiles // 2], air[:, tiles // 2 :], x_message, lax.axis_index("gx") % 2 == 0),
        ):
            up, down = layers[n - PAD_LO :], layers[:PAD_HI]
            if message is y_message:
                up, down = up.transpose(1, 0, 2, 3), down.transpose(1, 0, 2, 3)
            up = jnp.concatenate([up.reshape(-1, LANES), high_air.reshape(-1, LANES)])
            down = jnp.concatenate([down.reshape(-1, LANES), low_air.reshape(-1, LANES)])
            messages += order(up, jnp.pad(down, ((0, up.shape[0] - down.shape[0]), (0, 0))), even)

    from_y = swap_neighbours("gy", 0, messages[0]), swap_neighbours("gy", 1, messages[1])
    from_x = swap_neighbours("gx", 1, messages[3]), swap_neighbours("gx", 0, messages[2])
    wind_x, wind_y, wind_z, own_change, edge_x, edge_y = call(
        functools.partial(own_kernel, n, parts), [tiles_of(n * n)] * 4 + [tiles_of(2 * n)] * 2, (block,), micros=1.6
    )
    message = tiles_of(LO * LINES + 2 + tiles)
    corners = call(functools.partial(corner_kernel, n, parts), (message, message), (*from_y, own_change), micros=0.1)
    corners = swap_neighbours("gx", 1, corners[1]), swap_neighbours("gx", 0, corners[0])
    cell, change, halo_wind_x, far_wind_y = call(
        functools.partial(y_kernel, n, parts),
        [tiles_of(n * (n + PAD_LO + PAD_HI)), tiles_of(n * (n + LINES)), tiles_of(LINES * n), tiles_of(n * (LINES + 2))],
        (block, *from_y, wind_y, own_change, edge_y),
        [tiles_of(LINES * n)] * 2,
        micros=2.0,
    )
    reach, inner = n + LINES, n - LINES
    near = call(
        functools.partial(inner_kernel, n, parts),
        [tiles_of(inner * reach), tiles_of(2 * reach), tiles_of(inner * n)],
        (cell, change, halo_wind_x, wind_y, far_wind_y, wind_z, edge_x),
        micros=0.9,
    )
    mid, far_wind_x, side, side_wind_y = call(
        functools.partial(x_kernel, n, parts),
        [tiles_of(count) for count in (reach * n, (LINES + 2) * n, LINES * n, LINES * n)],
        (cell, change, wind_x, near[1], *from_x),
        [tiles_of(LINES * n)] * 3,
        micros=1.7,
    )
    fall = sub_courant.reshape(1, bins), fall_steps.reshape(1, bins)

    def fallen(count):
        if parts == 2:
            return [tiles_of(n * count // 2 + (count + 3) // 4)] * 2
        return [tiles_of(n * count), tiles_of(count)]

    one, *early = call(
        functools.partial(main_kernel, n, parts),
        [tiles_of(reach * reach)] + fallen(EARLY),
        (
            *(cell, change, wind_x, wind_y, wind_z, halo_wind_x, far_wind_y, *near),
            *(mid, far_wind_x, side, side_wind_y, *corners, *fall),
        ),
        [tiles_of(count) for count in (LINES * LINES, 2 * LINES, 2 * LINES, n * EARLY, n * EARLY)],
        micros=2.6,
    )
    if parts == 2:
        early_got = lax.ppermute(early[0], "gz", [(0, 1), (1, 0)])
    late = call(
        functools.partial(late_kernel, n, parts),
        fallen(n - EARLY),
        (one, cell, wind_x, far_wind_x, wind_y, far_wind_y, wind_z, near[2], *fall),
        [tiles_of(n * (n - EARLY))] * 2,
        micros=0.7,
    )

    def products(count):
        return shape(n * count * ROWS, pair_rows, dtype=jnp.bfloat16)

    if parts == 2:
        late_got = lax.ppermute(late[0], "gz", [(0, 1), (1, 0)])
        early = call(
            functools.partial(breakup_first_kernel, n),
            [shape(EARLY, ny, nz, bins), shape(EARLY, ny // parts, bins)],
            (early[1], early_got, pairs, lost),
            [tiles_of(n * EARLY), products(EARLY)],
            micros=1.8,
        )
        outs = [shape(nx, ny, nz, bins), shape(nx, ny // parts, bins)]
        return tuple(
            call(
                functools.partial(breakup_last_kernel, n),
                outs,
                (late[1], late_got, pairs, lost, *early),
                [tiles_of(n * (n - EARLY)), products(n - EARLY), shape(n - EARLY, ny, nz, bins), outs[1]],
                micros=1.2,
                out_place=pl.ANY,
                copies=3,
            )
        )

    settled, rain = [jnp.concatenate(halves) for halves in zip(early, late)]
    rain = rain.reshape(nx, ny, LANES)[:, :, :width]
    rain = lax.all_to_all(rain, "gz", split_axis=1, concat_axis=2, tiled=True)
    settled = settled.reshape(nx, ny, ROWS, parts, nz // ROWS, width).transpose(3, 0, 1, 4, 2, 5)
    settled = lax.all_to_all(settled, "gz", split_axis=0, concat_axis=0, tiled=True)
    settled = settled.transpose(1, 2, 3, 4, 0, 5).reshape(nx * ny, nz // ROWS, ROWS, bins)
    paired = settled.transpose(0, 2, 1, 3).reshape(-1, LANES)
    updated = call(breakup_plain_kernel, tiles_of(n * n), (paired, pairs, lost), [products(n // 2)], micros=3.0)
    updated = updated.reshape(nx, ny, ROWS, nz // ROWS, bins).transpose(0, 1, 3, 2, 4).reshape(nx, ny, nz, bins)
    return updated, rain


def solution(mesh):
    in_specs = (P("gx", "gy", "gz", None), P(None, "gx", "gy", "gz"), P(), P(), P(), P())
    out_specs = (P("gx", "gy", "gz", None), P("gx", ("gy", "gz"), None))
    return jax.shard_map(per_device, mesh=mesh, in_specs=in_specs, out_specs=out_specs, check_vma=False)
```

profile of v0, /device:TPU:0, one launch (start us, length us, event | category | flops | bytes accessed | tf_op | source)
XLA Modules:
  0.0 32.1 jit_solution(16903097688604364211)
XLA Ops:
  0.6 0.0 copy-start.1
  0.6 1.0 %copy-done.1 = f32[8,8,16,64]{3,2,1,0:T(8,128)S(1)} copy-done((f32[8,8,16,64]{3,2,1,0:T(8,128)S(1)}, f32[8,8,16,64]{3,2,1,0:T(8,128)}, u32[]{:S(2)}) %copy-start.1) | copy-done | bytes 262168
  1.7 0.0 copy-start.2
  1.7 0.0 copy-start.5
  1.7 0.3 shard_map.77
  2.0 0.0 copy-start
  2.0 3.0 %collective-permute-start = (f32[256,128]{1,0:T(8,128)S(1)}, f32[256,128]{1,0:T(8,128)S(1)}, u32[]{:S(2)}, u32[]{:S(2)}) collective-permute-start(f32[256,128]{1,0:T(8,128)S(1)} %get-tuple-element.38), channel_id=1, source_target_pairs={{0,1},{1,0},{2,3},{3,2},{4,5},{5,4},{6,7},{7,6},{8,9},{9,8},{10,11... | collective-permute-start | bytes 393224 | tf_op jit(solution)/shard_map/ppermute | solution.py:729
  5.0 0.0 copy-done.2
  5.0 0.1 shard_map.78.own_wind_ref
  5.1 0.6 %collective-permute-start.1 = (f32[24,128]{1,0:T(8,128)S(1)}, f32[24,128]{1,0:T(8,128)S(1)}, u32[]{:S(2)}, u32[]{:S(2)}) collective-permute-start(f32[24,128]{1,0:T(8,128)S(1)} %shard_map.78.own_wind_ref), channel_id=1, source_target_pairs={{0,1},{1,0},{2,3},{3,2},{4,5},{5,4},{6,7},{7,6},{8,9},{9,8},{10,11... | collective-permute-start | bytes 36872 | tf_op jit(solution)/shard_map/ppermute | solution.py:731
  5.7 0.0 copy-done.5
  5.7 0.5 %copy.8.gain_ref = bf16[4096,64]{1,0:T(8,128)(2,1)S(1)} copy(bf16[4096,64]{0,1:T(8,128)(2,1)S(1)} %copy-done.5) | data formatting | bytes 1048576 | tf_op args[4]
  6.2 0.0 copy-done
  6.2 1.4 %shard_map.79 = (bf16[4224,128]{1,0:T(8,128)(2,1)S(1)}, bf16[128,128]{1,0:T(8,128)(2,1)S(1)}) custom-call(bf16[4096,64]{1,0:T(8,128)(2,1)S(1)} %copy.8.gain_ref, bf16[64,64]{1,0:T(8,128)(2,1)S(1)} %copy-done), custom_call_target="tpu_custom_call" | custom-call | flops 22000000 | bytes 72000 | tf_op jit(solution)/shard_map/pallas_call | solution.py:673
  7.5 1.3 %collective-permute-done.1.got_wind_ref = f32[24,128]{1,0:T(8,128)S(1)} collective-permute-done((f32[24,128]{1,0:T(8,128)S(1)}, f32[24,128]{1,0:T(8,128)S(1)}, u32[]{:S(2)}, u32[]{:S(2)}) %collective-permute-start.1) | collective-permute-done | bytes 12320 | tf_op jit(solution)/shard_map/ppermute | solution.py:731
  8.9 0.0 collective-permute-done.got_ref
  8.9 0.2 shard_map.80
  9.1 1.8 %collective-permute-start.2 = (f32[432,128]{1,0:T(8,128)S(1)}, f32[432,128]{1,0:T(8,128)S(1)}, u32[]{:S(2)}, u32[]{:S(2)}) collective-permute-start(f32[432,128]{1,0:T(8,128)S(1)} %get-tuple-element.41), channel_id=1, source_target_pairs={{0,2},{1,3},{2,0},{3,1},{4,6},{5,7},{6,4},{7,5},{8,10},{9,11},{10,... | collective-permute-start | bytes 663560 | tf_op jit(solution)/shard_map/ppermute | solution.py:703
  10.8 0.0 collective-permute-start.3
  10.9 1.5 %collective-permute-start.4 = (f32[408,128]{1,0:T(8,128)S(1)}, f32[408,128]{1,0:T(8,128)S(1)}, u32[]{:S(2)}, u32[]{:S(2)}) collective-permute-start(f32[408,128]{1,0:T(8,128)S(1)} %get-tuple-element.56), channel_id=1, source_target_pairs={{0,1},{1,0},{2,3},{3,2},{4,5},{5,4},{6,7},{7,6},{8,16},{9,17},{10,... | collective-permute-start | bytes 626696 | tf_op jit(solution)/shard_map/ppermute | solution.py:703
  12.4 0.1 collective-permute-start.5
  12.5 1.7 %shard_map.81 = (f32[512,128]{1,0:T(8,128)S(1)}, f32[512,128]{1,0:T(8,128)S(1)}, f32[512,128]{1,0:T(8,128)S(1)}, f32[512,128]{1,0:T(8,128)S(1)}, f32[128,128]{1,0:T(8,128)S(1)}, /*index=5*/f32[128,128]{1,0:T(8,128)S(1)}) custom-call(f32[560,128]{1,0:T(8,128)S(1)} %get-tuple-element.40.block_ref), custom_call_target="tpu_custom_call" | custom-call | flops 1760000000 | bytes 5760000 | tf_op jit(solution)/shard_map/pallas_call | solution.py:673
  14.2 1.5 %collective-permute-done.2.first_ref = f32[432,128]{1,0:T(8,128)S(1)} collective-permute-done((f32[432,128]{1,0:T(8,128)S(1)}, f32[432,128]{1,0:T(8,128)S(1)}, u32[]{:S(2)}, u32[]{:S(2)}) %collective-permute-start.2) | collective-permute-done | bytes 221216 | tf_op jit(solution)/shard_map/ppermute | solution.py:703
  15.7 0.0 collective-permute-done.3.second_ref
  15.7 1.5 %collective-permute-start.6 = (f32[152,128]{1,0:T(8,128)S(1)}, f32[152,128]{1,0:T(8,128)S(1)}, u32[]{:S(2)}, u32[]{:S(2)}) collective-permute-start(f32[152,128]{1,0:T(8,128)S(1)} %get-tuple-element.62), channel_id=1, source_target_pairs={{0,1},{1,0},{2,3},{3,2},{4,5},{5,4},{6,7},{7,6},{8,16},{9,17},{10,... | collective-permute-start | bytes 233480 | tf_op jit(solution)/shard_map/ppermute | solution.py:703
  17.2 0.1 collective-permute-start.7
  17.3 1.4 %shard_map.82 = (f32[1152,128]{1,0:T(8,128)S(1)}, f32[832,128]{1,0:T(8,128)S(1)}, f32[320,128]{1,0:T(8,128)S(1)}, f32[448,128]{1,0:T(8,128)S(1)}) custom-call(f32[560,128]{1,0:T(8,128)S(1)} %get-tuple-element.40.block_ref, f32[432,128]{1,0:T(8,128)S(1)} %collective-permute-done.2.first_ref, f32[432,128]{1,0:T(8,128)S(1)} %collective-permute-done.3.second_ref, ...), custom_call_target="tpu_custom_call" | custom-call | flops 2200000000 | bytes 7200000 | tf_op jit(solution)/shard_map/pallas_call | solution.py:673
  18.7 0.6 %shard_map.83 = (f32[312,128]{1,0:T(8,128)S(1)}, f32[208,128]{1,0:T(8,128)S(1)}, f32[192,128]{1,0:T(8,128)S(1)}) custom-call(f32[1152,128]{1,0:T(8,128)S(1)} %get-tuple-element.46.cell.refs_0_, f32[832,128]{1,0:T(8,128)S(1)} %get-tuple-element.47.change.refs_1_, f32[320,128]{1,0:T(8,128)S(1)} %get-tuple-element.50.halo_wind_x.refs_5_, ...), custom_call_target="tpu_custom_call" | custom-call | flops 990000000 | bytes 3240000 | tf_op jit(solution)/shard_map/pallas_call | solution.py:673
  19.2 0.0 collective-permute-done.4.second_ref
  19.2 0.0 collective-permute-done.5.first_ref
  19.2 0.0 copy-start.3
  19.3 0.0 copy-start.4
  19.3 1.4 %shard_map.84 = (f32[832,128]{1,0:T(8,128)S(1)}, f32[448,128]{1,0:T(8,128)S(1)}, f32[320,128]{1,0:T(8,128)S(1)}, f32[320,128]{1,0:T(8,128)S(1)}) custom-call(f32[1152,128]{1,0:T(8,128)S(1)} %get-tuple-element.46.cell.refs_0_, f32[832,128]{1,0:T(8,128)S(1)} %get-tuple-element.47.change.refs_1_, f32[512,128]{1,0:T(8,128)S(1)} %get-tuple-element.48.wind_x.refs_2_, ...), custom_call_target="tpu_custom_call" | custom-call | flops 1870000000 | bytes 6120000 | tf_op jit(solution)/shard_map/pallas_call | solution.py:673
  20.7 0.0 collective-permute-done.6.refs_14_
  20.7 0.0 collective-permute-done.7.refs_15_
  20.7 0.0 copy-done.3
  20.7 0.0 copy-done.4
  20.7 2.4 %shard_map.86 = (f32[1352,128]{1,0:T(8,128)S(1)}, f32[208,128]{1,0:T(8,128)S(1)}, f32[208,128]{1,0:T(8,128)S(1)}) custom-call(f32[1152,128]{1,0:T(8,128)S(1)} %get-tuple-element.46.cell.refs_0_, f32[832,128]{1,0:T(8,128)S(1)} %get-tuple-element.47.change.refs_1_, f32[512,128]{1,0:T(8,128)S(1)} %get-tuple-element.48.wind_x.refs_2_, ...), custom_call_target="tpu_custom_call" | custom-call | flops 2860000000 | bytes 9360000 | tf_op jit(solution)/shard_map/pallas_call | solution.py:673
  23.1 1.6 %collective-permute-start.9 = (f32[208,128]{1,0:T(8,128)S(1)}, f32[208,128]{1,0:T(8,128)S(1)}, u32[]{:S(2)}, u32[]{:S(2)}) collective-permute-start(f32[208,128]{1,0:T(8,128)S(1)} %get-tuple-element.69), channel_id=1, source_target_pairs={{0,1},{1,0},{2,3},{3,2},{4,5},{5,4},{6,7},{7,6},{8,9},{9,8},{10,11... | collective-permute-start | bytes 319496 | tf_op jit(solution)/shard_map/ppermute | solution.py:805
  24.7 1.0 %shard_map.87 = (f32[72,128]{1,0:T(8,128)S(1)}, f32[72,128]{1,0:T(8,128)S(1)}) custom-call(f32[1352,128]{1,0:T(8,128)S(1)} %get-tuple-element.64.one, f32[1152,128]{1,0:T(8,128)S(1)} %get-tuple-element.46.cell.refs_0_, f32[512,128]{1,0:T(8,128)S(1)} %get-tuple-element.48.wind_x.refs_2_, f32[448,128]{1,0:T(8,128)S(1)} %get-tuple-element.59.refs_11_.far_wind_x, ...), custom_call_target="tpu_custom_call" | custom-call | flops 770000000 | bytes 2520000 | tf_op jit(solution)/shard_map/pallas_call | solution.py:673
  25.7 0.6 %collective-permute-start.8 = (f32[72,128]{1,0:T(8,128)S(1)}, f32[72,128]{1,0:T(8,128)S(1)}, u32[]{:S(2)}, u32[]{:S(2)}) collective-permute-start(f32[72,128]{1,0:T(8,128)S(1)} %get-tuple-element.66), channel_id=1, source_target_pairs={{0,1},{1,0},{2,3},{3,2},{4,5},{5,4},{6,7},{7,6},{8,9},{9,8},{10,11... | collective-permute-start | bytes 110600 | tf_op jit(solution)/shard_map/ppermute | solution.py:818
  26.3 2.5 %collective-permute-done.9.got_ref = f32[208,128]{1,0:T(8,128)S(1)} collective-permute-done((f32[208,128]{1,0:T(8,128)S(1)}, f32[208,128]{1,0:T(8,128)S(1)}, u32[]{:S(2)}, u32[]{:S(2)}) %collective-permute-start.9) | collective-permute-done | bytes 106528 | tf_op jit(solution)/shard_map/ppermute | solution.py:805
  28.8 1.8 %shard_map.88 = (f32[6,8,16,64]{3,2,1,0:T(8,128)S(1)}, f32[6,4,64]{2,1,0:T(4,128)S(1)}) custom-call(f32[208,128]{1,0:T(8,128)S(1)} %get-tuple-element.68.keep_ref, f32[208,128]{1,0:T(8,128)S(1)} %collective-permute-done.9.got_ref, bf16[4224,128]{1,0:T(8,128)(2,1)S(1)} %get-tuple-element.67.pairs_ref, bf16[128,128]{1,0:T(8,128)(2,1)S(1)} %get-tuple-element.39.lost_ref), custom_call_target="tpu_custom_call" | custom-call | flops 1980000000 | bytes 6480000 | tf_op jit(solution)/shard_map/pallas_call | solution.py:673
  30.5 0.0 collective-permute-done.8.got_ref
  30.5 1.6 %shard_map.89 = (f32[8,8,16,64]{3,2,1,0:T(8,128)}, f32[8,4,64]{2,1,0:T(4,128)}) custom-call(f32[72,128]{1,0:T(8,128)S(1)} %get-tuple-element.65.keep_ref, f32[72,128]{1,0:T(8,128)S(1)} %collective-permute-done.8.got_ref, bf16[4224,128]{1,0:T(8,128)(2,1)S(1)} %get-tuple-element.67.pairs_ref, bf16[128,128]{1,0:T(8,128)(2,1)S(1)} %get-tuple-element.39.lost_ref, ...), custom_call_target="tpu_custom_call" | custom-call | flops 1320000000 | bytes 4320000 | tf_op jit(solution)/shard_map/pallas_call | solution.py:673
  (1 shorter events, 0.0 us)
Async XLA Ops:
  0.6 1.0 %copy-start.1 = (f32[8,8,16,64]{3,2,1,0:T(8,128)S(1)}, f32[8,8,16,64]{3,2,1,0:T(8,128)}, u32[]{:S(2)}) copy-start(f32[8,8,16,64]{3,2,1,0:T(8,128)} %mass_ref.1) | copy-start | bytes 786436
  1.7 3.3 %copy-start.2 = (f32[3,8,8,16]{3,2,1,0:T(8,128)S(1)}, f32[3,8,8,16]{3,2,1,0:T(8,128)}, u32[]{:S(2)}) copy-start(f32[3,8,8,16]{3,2,1,0:T(8,128)} %wind_ref.1) | copy-start | bytes 36868
  1.7 4.0 %copy-start.5 = (bf16[4096,64]{0,1:T(8,128)(2,1)S(1)}, bf16[4096,64]{0,1:T(8,128)(2,1)}, u32[]{:S(2)}) copy-start(bf16[4096,64]{0,1:T(8,128)(2,1)} %param.10) | copy-start | bytes 1572868
  2.0 4.2 %copy-start = (bf16[64,64]{1,0:T(8,128)(2,1)S(1)}, bf16[64,64]{1,0:T(8,128)(2,1)}, u32[]{:S(2)}) copy-start(bf16[64,64]{1,0:T(8,128)(2,1)} %loss_ref.1) | copy-start | bytes 24580
  2.0 6.9 %collective-permute-start = (f32[256,128]{1,0:T(8,128)S(1)}, f32[256,128]{1,0:T(8,128)S(1)}, u32[]{:S(2)}, u32[]{:S(2)}) collective-permute-start(f32[256,128]{1,0:T(8,128)S(1)} %get-tuple-element.38), channel_id=1, source_target_pairs={{0,1},{1,0},{2,3},{3,2},{4,5},{5,4},{6,7},{7,6},{8,9},{9,8},{10,11... | collective-permute-start | bytes 393224 | tf_op jit(solution)/shard_map/ppermute | solution.py:729
  5.1 3.7 %collective-permute-start.1 = (f32[24,128]{1,0:T(8,128)S(1)}, f32[24,128]{1,0:T(8,128)S(1)}, u32[]{:S(2)}, u32[]{:S(2)}) collective-permute-start(f32[24,128]{1,0:T(8,128)S(1)} %shard_map.78.own_wind_ref), channel_id=1, source_target_pairs={{0,1},{1,0},{2,3},{3,2},{4,5},{5,4},{6,7},{7,6},{8,9},{9,8},{10,11... | collective-permute-start | bytes 36872 | tf_op jit(solution)/shard_map/ppermute | solution.py:731
  9.1 6.6 %collective-permute-start.2 = (f32[432,128]{1,0:T(8,128)S(1)}, f32[432,128]{1,0:T(8,128)S(1)}, u32[]{:S(2)}, u32[]{:S(2)}) collective-permute-start(f32[432,128]{1,0:T(8,128)S(1)} %get-tuple-element.41), channel_id=1, source_target_pairs={{0,2},{1,3},{2,0},{3,1},{4,6},{5,7},{6,4},{7,5},{8,10},{9,11},{10,... | collective-permute-start | bytes 663560 | tf_op jit(solution)/shard_map/ppermute | solution.py:703
  10.8 4.8 %collective-permute-start.3 = (f32[432,128]{1,0:T(8,128)S(1)}, f32[432,128]{1,0:T(8,128)S(1)}, u32[]{:S(2)}, u32[]{:S(2)}) collective-permute-start(f32[432,128]{1,0:T(8,128)S(1)} %get-tuple-element.42), channel_id=1, source_target_pairs={{0,8},{1,9},{2,4},{3,5},{4,2},{5,3},{6,14},{7,15},{8,0},{9,1},{10,... | collective-permute-start | bytes 663560 | tf_op jit(solution)/shard_map/ppermute | solution.py:703
  10.9 8.4 %collective-permute-start.4 = (f32[408,128]{1,0:T(8,128)S(1)}, f32[408,128]{1,0:T(8,128)S(1)}, u32[]{:S(2)}, u32[]{:S(2)}) collective-permute-start(f32[408,128]{1,0:T(8,128)S(1)} %get-tuple-element.56), channel_id=1, source_target_pairs={{0,1},{1,0},{2,3},{3,2},{4,5},{5,4},{6,7},{7,6},{8,16},{9,17},{10,... | collective-permute-start | bytes 626696 | tf_op jit(solution)/shard_map/ppermute | solution.py:703
  12.4 6.9 %collective-permute-start.5 = (f32[408,128]{1,0:T(8,128)S(1)}, f32[408,128]{1,0:T(8,128)S(1)}, u32[]{:S(2)}, u32[]{:S(2)}) collective-permute-start(f32[408,128]{1,0:T(8,128)S(1)} %get-tuple-element.57), channel_id=1, source_target_pairs={{0,8},{1,9},{2,10},{3,11},{4,12},{5,13},{6,14},{7,15},{8,0},{9,1},... | collective-permute-start | bytes 626696 | tf_op jit(solution)/shard_map/ppermute | solution.py:703
  15.7 5.0 %collective-permute-start.6 = (f32[152,128]{1,0:T(8,128)S(1)}, f32[152,128]{1,0:T(8,128)S(1)}, u32[]{:S(2)}, u32[]{:S(2)}) collective-permute-start(f32[152,128]{1,0:T(8,128)S(1)} %get-tuple-element.62), channel_id=1, source_target_pairs={{0,1},{1,0},{2,3},{3,2},{4,5},{5,4},{6,7},{7,6},{8,16},{9,17},{10,... | collective-permute-start | bytes 233480 | tf_op jit(solution)/shard_map/ppermute | solution.py:703
  17.2 3.5 %collective-permute-start.7 = (f32[152,128]{1,0:T(8,128)S(1)}, f32[152,128]{1,0:T(8,128)S(1)}, u32[]{:S(2)}, u32[]{:S(2)}) collective-permute-start(f32[152,128]{1,0:T(8,128)S(1)} %get-tuple-element.63), channel_id=1, source_target_pairs={{0,8},{1,9},{2,10},{3,11},{4,12},{5,13},{6,14},{7,15},{8,0},{9,1},... | collective-permute-start | bytes 233480 | tf_op jit(solution)/shard_map/ppermute | solution.py:703
  19.2 1.4 %copy-start.3 = (f32[64]{0:T(128)S(1)}, f32[64]{0:T(128)}, u32[]{:S(2)}) copy-start(f32[64]{0:T(128)} %param.8) | copy-start | bytes 772
  19.3 1.4 %copy-start.4 = (s32[64]{0:T(128)S(1)}, s32[64]{0:T(128)}, u32[]{:S(2)}) copy-start(s32[64]{0:T(128)} %param.9) | copy-start | bytes 772
  23.1 5.7 %collective-permute-start.9 = (f32[208,128]{1,0:T(8,128)S(1)}, f32[208,128]{1,0:T(8,128)S(1)}, u32[]{:S(2)}, u32[]{:S(2)}) collective-permute-start(f32[208,128]{1,0:T(8,128)S(1)} %get-tuple-element.69), channel_id=1, source_target_pairs={{0,1},{1,0},{2,3},{3,2},{4,5},{5,4},{6,7},{7,6},{8,9},{9,8},{10,11... | collective-permute-start | bytes 319496 | tf_op jit(solution)/shard_map/ppermute | solution.py:805
  25.7 4.8 %collective-permute-start.8 = (f32[72,128]{1,0:T(8,128)S(1)}, f32[72,128]{1,0:T(8,128)S(1)}, u32[]{:S(2)}, u32[]{:S(2)}) collective-permute-start(f32[72,128]{1,0:T(8,128)S(1)} %get-tuple-element.66), channel_id=1, source_target_pairs={{0,1},{1,0},{2,3},{3,2},{4,5},{5,4},{6,7},{7,6},{8,9},{9,8},{10,11... | collective-permute-start | bytes 110600 | tf_op jit(solution)/shard_map/ppermute | solution.py:818
where the time goes:
time: 32.3 us; the launch traced here: 32.1 us
  Pallas kernels  13.8 us (43%)
  starting transfers between devices  10.7 us (33%)
  waiting for transfers between devices  5.28 us (16%)
  local copies, waits for them, and re-layouts  1.54 us (5%)
  between operations  0.8 us (2%)
    pallas_call x13, Pallas kernels, call(): pl.pallas_call(kernel, out_shape=outs, in_specs=[VMEM] * len(args), out_s...  13.8 us
    ppermute x6, starting transfers between devices, swap_neighbours(): return lax.ppermute(message, axes, pairs)  4.95 us
    ppermute x1, starting transfers between devices, per_device(): got = lax.ppermute(send, 'gz', [(0, 1), (1, 0)])  3.03 us
    ppermute x1, waiting for transfers between devices, per_device(): early_got = lax.ppermute(early[0], 'gz', [(0, 1), (1, 0)])  2.47 us
    ppermute x1, starting transfers between devices, per_device(): early_got = lax.ppermute(early[0], 'gz', [(0, 1), (1, 0)])  1.58 us
    unnamed x13, local copies, waits for them, and re-layouts  1.54 us
    ppermute x6, waiting for transfers between devices, swap_neighbours(): return lax.ppermute(message, axes, pairs)  1.5 us
    ppermute x1, waiting for transfers between devices, per_device(): got_wind = lax.ppermute(own_wind, 'gz', [(0, 1), (1, 0)])  1.31 us
  transfers between devices with their start and end apart: 10, of which 3 were waited for; matrix products, arithmetic and copies ran while one was open for 1% of the time, Pallas kernels for 29%

commit v1 on v0

--- a/solution.py
+++ b/solution.py
@@ -15,7 +15,7 @@
 LINES = LO + HI
 ROWS, LANES = 8, 128
 AHEAD = 4
-EARLY = 6
+EARLY = 5
 F32 = jnp.float32
 VMEM = pl.BlockSpec(memory_space=pltpu.VMEM)
 
@@ -100,23 +100,21 @@
     twice = [d + d for d in first]
     second = [b - a for a, b in zip(first, first[1:])]
     third = [a - b for a, b in zip(second, second[1:])]
+    third_twice = [t + t for t in third]
     curved = [(13.0 / 3.0) * (c * c) + 4.0 * EPS for c in second]
     fluxes = []
     for j in range(len(cells) - 4):
         left = twice[j + 1] + second[j]
         mid = first[j + 1] + first[j + 2]
         right = twice[j + 2] - second[j + 2]
-        e0 = curved[j] + left * left
-        e1 = curved[j + 1] + mid * mid
-        e2 = curved[j + 2] + right * right
-        e0 = e0 * e0
-        e1 = e1 * e1
-        e2 = e2 * e2
-        e0 = 3.0 * e0
-        e2_twice = e2 + e2
-        top = e1 * (e2_twice * third[j] + e0 * third[j + 1])
-        low = e1 * (e2 + e0) + e0 * e2_twice
-        inverse = pl.reciprocal(low, approx=True)
+        w0 = pl.reciprocal(curved[j] + left * left, approx=True)
+        w1 = pl.reciprocal(curved[j + 1] + mid * mid, approx=True)
+        w2 = pl.reciprocal(curved[j + 2] + right * right, approx=True)
+        w0 = w0 * w0
+        w1 = 6.0 * (w1 * w1)
+        w2 = 3.0 * (w2 * w2)
+        top = w0 * third_twice[j] + w2 * third[j + 1]
+        inverse = pl.reciprocal(w0 + w1 + w2, approx=True)
         estimate = 6.0 * cells[j + 2] + (first[j + 1] + twice[j + 2]) + top * inverse
         fluxes.append((winds[j] + winds[j + 1]) * estimate)
     return fluxes

time: 32.3 us -> 32 us (level)
  waiting for transfers between devices: 5.28 us -> 4.8 us
    ppermute x1, waiting for transfers between devices: 2.47 us -> 1.7 us  [per_device(): early_got = lax.ppermute(early[0], 'gz', [(0, 1), (1, 0)])]
    ppermute x1, waiting for transfers between devices: 0.01 us -> 0.37 us  [per_device(): late_got = lax.ppermute(late[0], 'gz', [(0, 1), (1, 0)])]
  transfers between devices with their start and end apart: 10 -> 10, of which waited for: 3 -> 4; matrix products, arithmetic and copies ran while one was open for 1% -> 2% of each run, Pallas kernels for 29% -> 30%
where the time goes in v1:
time: 32 us; the launch traced here: 31.8 us
  Pallas kernels  14 us (44%)
  starting transfers between devices  10.7 us (33%)
  waiting for transfers between devices  4.8 us (15%)
  local copies, waits for them, and re-layouts  1.54 us (5%)
  between operations  0.81 us (3%)
    pallas_call x13, Pallas kernels, call(): pl.pallas_call(kernel, out_shape=outs, in_specs=[VMEM] * len(args), out_s...  14 us
    ppermute x6, starting transfers between devices, swap_neighbours(): return lax.ppermute(message, axes, pairs)  4.95 us
    ppermute x1, starting transfers between devices, per_device(): got = lax.ppermute(send, 'gz', [(0, 1), (1, 0)])  3.03 us
    ppermute x1, waiting for transfers between devices, per_device(): early_got = lax.ppermute(early[0], 'gz', [(0, 1), (1, 0)])  1.7 us
    ppermute x1, starting transfers between devices, per_device(): early_got = lax.ppermute(early[0], 'gz', [(0, 1), (1, 0)])  1.58 us
    unnamed x13, local copies, waits for them, and re-layouts  1.54 us
    ppermute x6, waiting for transfers between devices, swap_neighbours(): return lax.ppermute(message, axes, pairs)  1.42 us
    ppermute x1, waiting for transfers between devices, per_device(): got_wind = lax.ppermute(own_wind, 'gz', [(0, 1), (1, 0)])  1.31 us
  transfers between devices with their start and end apart: 10, of which 4 were waited for; matrix products, arithmetic and copies ran while one was open for 2% of the time, Pallas kernels for 30%

profile of v1, /device:TPU:0, one launch (start us, length us, event | category | flops | bytes accessed | tf_op | source)
XLA Modules:
  0.0 31.8 jit_solution(11533877703685655135)
XLA Ops:
  0.6 0.0 copy-start.1
  0.6 1.0 %copy-done.1 = f32[8,8,16,64]{3,2,1,0:T(8,128)S(1)} copy-done((f32[8,8,16,64]{3,2,1,0:T(8,128)S(1)}, f32[8,8,16,64]{3,2,1,0:T(8,128)}, u32[]{:S(2)}) %copy-start.1) | copy-done | bytes 262168
  1.7 0.0 copy-start.2
  1.7 0.0 copy-start.5
  1.7 0.3 shard_map.77
  2.0 0.0 copy-start
  2.0 3.0 %collective-permute-start = (f32[256,128]{1,0:T(8,128)S(1)}, f32[256,128]{1,0:T(8,128)S(1)}, u32[]{:S(2)}, u32[]{:S(2)}) collective-permute-start(f32[256,128]{1,0:T(8,128)S(1)} %get-tuple-element.38), channel_id=1, source_target_pairs={{0,1},{1,0},{2,3},{3,2},{4,5},{5,4},{6,7},{7,6},{8,9},{9,8},{10,11... | collective-permute-start | bytes 393224 | tf_op jit(solution)/shard_map/ppermute | solution.py:727
  5.0 0.0 copy-done.2
  5.0 0.1 shard_map.78.own_wind_ref
  5.1 0.6 %collective-permute-start.1 = (f32[24,128]{1,0:T(8,128)S(1)}, f32[24,128]{1,0:T(8,128)S(1)}, u32[]{:S(2)}, u32[]{:S(2)}) collective-permute-start(f32[24,128]{1,0:T(8,128)S(1)} %shard_map.78.own_wind_ref), channel_id=1, source_target_pairs={{0,1},{1,0},{2,3},{3,2},{4,5},{5,4},{6,7},{7,6},{8,9},{9,8},{10,11... | collective-permute-start | bytes 36872 | tf_op jit(solution)/shard_map/ppermute | solution.py:729
  5.7 0.0 copy-done.5
  5.7 0.5 %copy.8.gain_ref = bf16[4096,64]{1,0:T(8,128)(2,1)S(1)} copy(bf16[4096,64]{0,1:T(8,128)(2,1)S(1)} %copy-done.5) | data formatting | bytes 1048576 | tf_op args[4]
  6.2 0.0 copy-done
  6.2 1.4 %shard_map.79 = (bf16[4224,128]{1,0:T(8,128)(2,1)S(1)}, bf16[128,128]{1,0:T(8,128)(2,1)S(1)}) custom-call(bf16[4096,64]{1,0:T(8,128)(2,1)S(1)} %copy.8.gain_ref, bf16[64,64]{1,0:T(8,128)(2,1)S(1)} %copy-done), custom_call_target="tpu_custom_call" | custom-call | flops 22000000 | bytes 72000 | tf_op jit(solution)/shard_map/pallas_call | solution.py:671
  7.5 1.3 %collective-permute-done.1.got_wind_ref = f32[24,128]{1,0:T(8,128)S(1)} collective-permute-done((f32[24,128]{1,0:T(8,128)S(1)}, f32[24,128]{1,0:T(8,128)S(1)}, u32[]{:S(2)}, u32[]{:S(2)}) %collective-permute-start.1) | collective-permute-done | bytes 12320 | tf_op jit(solution)/shard_map/ppermute | solution.py:729
  8.9 0.0 collective-permute-done.got_ref
  8.9 0.2 shard_map.80
  9.1 1.8 %collective-permute-start.2 = (f32[432,128]{1,0:T(8,128)S(1)}, f32[432,128]{1,0:T(8,128)S(1)}, u32[]{:S(2)}, u32[]{:S(2)}) collective-permute-start(f32[432,128]{1,0:T(8,128)S(1)} %get-tuple-element.41), channel_id=1, source_target_pairs={{0,2},{1,3},{2,0},{3,1},{4,6},{5,7},{6,4},{7,5},{8,10},{9,11},{10,... | collective-permute-start | bytes 663560 | tf_op jit(solution)/shard_map/ppermute | solution.py:701
  10.8 0.0 collective-permute-start.3
  10.9 1.5 %collective-permute-start.4 = (f32[408,128]{1,0:T(8,128)S(1)}, f32[408,128]{1,0:T(8,128)S(1)}, u32[]{:S(2)}, u32[]{:S(2)}) collective-permute-start(f32[408,128]{1,0:T(8,128)S(1)} %get-tuple-element.56), channel_id=1, source_target_pairs={{0,1},{1,0},{2,3},{3,2},{4,5},{5,4},{6,7},{7,6},{8,16},{9,17},{10,... | collective-permute-start | bytes 626696 | tf_op jit(solution)/shard_map/ppermute | solution.py:701
  12.4 0.1 collective-permute-start.5
  12.5 1.8 %shard_map.81 = (f32[512,128]{1,0:T(8,128)S(1)}, f32[512,128]{1,0:T(8,128)S(1)}, f32[512,128]{1,0:T(8,128)S(1)}, f32[512,128]{1,0:T(8,128)S(1)}, f32[128,128]{1,0:T(8,128)S(1)}, /*index=5*/f32[128,128]{1,0:T(8,128)S(1)}) custom-call(f32[560,128]{1,0:T(8,128)S(1)} %get-tuple-element.40.block_ref), custom_call_target="tpu_custom_call" | custom-call | flops 1760000000 | bytes 5760000 | tf_op jit(solution)/shard_map/pallas_call | solution.py:671
  14.3 1.4 %collective-permute-done.2.first_ref = f32[432,128]{1,0:T(8,128)S(1)} collective-permute-done((f32[432,128]{1,0:T(8,128)S(1)}, f32[432,128]{1,0:T(8,128)S(1)}, u32[]{:S(2)}, u32[]{:S(2)}) %collective-permute-start.2) | collective-permute-done | bytes 221216 | tf_op jit(solution)/shard_map/ppermute | solution.py:701
  15.7 0.0 collective-permute-done.3.second_ref
  15.7 1.5 %collective-permute-start.6 = (f32[152,128]{1,0:T(8,128)S(1)}, f32[152,128]{1,0:T(8,128)S(1)}, u32[]{:S(2)}, u32[]{:S(2)}) collective-permute-start(f32[152,128]{1,0:T(8,128)S(1)} %get-tuple-element.62), channel_id=1, source_target_pairs={{0,1},{1,0},{2,3},{3,2},{4,5},{5,4},{6,7},{7,6},{8,16},{9,17},{10,... | collective-permute-start | bytes 233480 | tf_op jit(solution)/shard_map/ppermute | solution.py:701
  17.2 0.1 collective-permute-start.7
  17.3 1.4 %shard_map.82 = (f32[1152,128]{1,0:T(8,128)S(1)}, f32[832,128]{1,0:T(8,128)S(1)}, f32[320,128]{1,0:T(8,128)S(1)}, f32[448,128]{1,0:T(8,128)S(1)}) custom-call(f32[560,128]{1,0:T(8,128)S(1)} %get-tuple-element.40.block_ref, f32[432,128]{1,0:T(8,128)S(1)} %collective-permute-done.2.first_ref, f32[432,128]{1,0:T(8,128)S(1)} %collective-permute-done.3.second_ref, ...), custom_call_target="tpu_custom_call" | custom-call | flops 2200000000 | bytes 7200000 | tf_op jit(solution)/shard_map/pallas_call | solution.py:671
  18.7 0.6 %shard_map.83 = (f32[312,128]{1,0:T(8,128)S(1)}, f32[208,128]{1,0:T(8,128)S(1)}, f32[192,128]{1,0:T(8,128)S(1)}) custom-call(f32[1152,128]{1,0:T(8,128)S(1)} %get-tuple-element.46.cell.refs_0_, f32[832,128]{1,0:T(8,128)S(1)} %get-tuple-element.47.change.refs_1_, f32[320,128]{1,0:T(8,128)S(1)} %get-tuple-element.50.halo_wind_x.refs_5_, ...), custom_call_target="tpu_custom_call" | custom-call | flops 990000000 | bytes 3240000 | tf_op jit(solution)/shard_map/pallas_call | solution.py:671
  19.3 0.0 collective-permute-done.4.second_ref
  19.3 0.0 collective-permute-done.5.first_ref
  19.3 0.0 copy-start.3
  19.3 0.0 copy-start.4
  19.3 1.4 %shard_map.84 = (f32[832,128]{1,0:T(8,128)S(1)}, f32[448,128]{1,0:T(8,128)S(1)}, f32[320,128]{1,0:T(8,128)S(1)}, f32[320,128]{1,0:T(8,128)S(1)}) custom-call(f32[1152,128]{1,0:T(8,128)S(1)} %get-tuple-element.46.cell.refs_0_, f32[832,128]{1,0:T(8,128)S(1)} %get-tuple-element.47.change.refs_1_, f32[512,128]{1,0:T(8,128)S(1)} %get-tuple-element.48.wind_x.refs_2_, ...), custom_call_target="tpu_custom_call" | custom-call | flops 1870000000 | bytes 6120000 | tf_op jit(solution)/shard_map/pallas_call | solution.py:671
  20.8 0.0 collective-permute-done.6.refs_14_
  20.8 0.0 collective-permute-done.7.refs_15_
  20.8 0.0 copy-done.3
  20.8 0.0 copy-done.4
  20.8 2.3 %shard_map.86 = (f32[1352,128]{1,0:T(8,128)S(1)}, f32[176,128]{1,0:T(8,128)S(1)}, f32[176,128]{1,0:T(8,128)S(1)}) custom-call(f32[1152,128]{1,0:T(8,128)S(1)} %get-tuple-element.46.cell.refs_0_, f32[832,128]{1,0:T(8,128)S(1)} %get-tuple-element.47.change.refs_1_, f32[512,128]{1,0:T(8,128)S(1)} %get-tuple-element.48.wind_x.refs_2_, ...), custom_call_target="tpu_custom_call" | custom-call | flops 2860000000 | bytes 9360000 | tf_op jit(solution)/shard_map/pallas_call | solution.py:671
  23.1 1.6 %collective-permute-start.9 = (f32[176,128]{1,0:T(8,128)S(1)}, f32[176,128]{1,0:T(8,128)S(1)}, u32[]{:S(2)}, u32[]{:S(2)}) collective-permute-start(f32[176,128]{1,0:T(8,128)S(1)} %get-tuple-element.69), channel_id=1, source_target_pairs={{0,1},{1,0},{2,3},{3,2},{4,5},{5,4},{6,7},{7,6},{8,9},{9,8},{10,11... | collective-permute-start | bytes 270344 | tf_op jit(solution)/shard_map/ppermute | solution.py:803
  24.7 1.2 %shard_map.87 = (f32[104,128]{1,0:T(8,128)S(1)}, f32[104,128]{1,0:T(8,128)S(1)}) custom-call(f32[1352,128]{1,0:T(8,128)S(1)} %get-tuple-element.64.one, f32[1152,128]{1,0:T(8,128)S(1)} %get-tuple-element.46.cell.refs_0_, f32[512,128]{1,0:T(8,128)S(1)} %get-tuple-element.48.wind_x.refs_2_, f32[448,128]{1,0:T(8,128)S(1)} %get-tuple-element.59.refs_11_.far_wind_x, ...), custom_call_target="tpu_custom_call" | custom-call | flops 770000000 | bytes 2520000 | tf_op jit(solution)/shard_map/pallas_call | solution.py:671
  25.9 0.6 %collective-permute-start.8 = (f32[104,128]{1,0:T(8,128)S(1)}, f32[104,128]{1,0:T(8,128)S(1)}, u32[]{:S(2)}, u32[]{:S(2)}) collective-permute-start(f32[104,128]{1,0:T(8,128)S(1)} %get-tuple-element.66), channel_id=1, source_target_pairs={{0,1},{1,0},{2,3},{3,2},{4,5},{5,4},{6,7},{7,6},{8,9},{9,8},{10,11... | collective-permute-start | bytes 159752 | tf_op jit(solution)/shard_map/ppermute | solution.py:816
  26.4 1.7 %collective-permute-done.9.got_ref = f32[176,128]{1,0:T(8,128)S(1)} collective-permute-done((f32[176,128]{1,0:T(8,128)S(1)}, f32[176,128]{1,0:T(8,128)S(1)}, u32[]{:S(2)}, u32[]{:S(2)}) %collective-permute-start.9) | collective-permute-done | bytes 90144 | tf_op jit(solution)/shard_map/ppermute | solution.py:803
  28.1 1.6 %shard_map.88 = (f32[5,8,16,64]{3,2,1,0:T(8,128)S(1)}, f32[5,4,64]{2,1,0:T(4,128)S(1)}) custom-call(f32[176,128]{1,0:T(8,128)S(1)} %get-tuple-element.68.keep_ref, f32[176,128]{1,0:T(8,128)S(1)} %collective-permute-done.9.got_ref, bf16[4224,128]{1,0:T(8,128)(2,1)S(1)} %get-tuple-element.67.pairs_ref, bf16[128,128]{1,0:T(8,128)(2,1)S(1)} %get-tuple-element.39.lost_ref), custom_call_target="tpu_custom_call" | custom-call | flops 1980000000 | bytes 6480000 | tf_op jit(solution)/shard_map/pallas_call | solution.py:671
  29.7 0.4 %collective-permute-done.8.got_ref = f32[104,128]{1,0:T(8,128)S(1)} collective-permute-done((f32[104,128]{1,0:T(8,128)S(1)}, f32[104,128]{1,0:T(8,128)S(1)}, u32[]{:S(2)}, u32[]{:S(2)}) %collective-permute-start.8) | collective-permute-done | bytes 53280 | tf_op jit(solution)/shard_map/ppermute | solution.py:816
  30.1 1.8 %shard_map.89 = (f32[8,8,16,64]{3,2,1,0:T(8,128)}, f32[8,4,64]{2,1,0:T(4,128)}) custom-call(f32[104,128]{1,0:T(8,128)S(1)} %get-tuple-element.65.keep_ref, f32[104,128]{1,0:T(8,128)S(1)} %collective-permute-done.8.got_ref, bf16[4224,128]{1,0:T(8,128)(2,1)S(1)} %get-tuple-element.67.pairs_ref, bf16[128,128]{1,0:T(8,128)(2,1)S(1)} %get-tuple-element.39.lost_ref, ...), custom_call_target="tpu_custom_call" | custom-call | flops 1320000000 | bytes 4320000 | tf_op jit(solution)/shard_map/pallas_call | solution.py:671
  (1 shorter events, 0.0 us)
Async XLA Ops:
  0.6 1.0 %copy-start.1 = (f32[8,8,16,64]{3,2,1,0:T(8,128)S(1)}, f32[8,8,16,64]{3,2,1,0:T(8,128)}, u32[]{:S(2)}) copy-start(f32[8,8,16,64]{3,2,1,0:T(8,128)} %mass_ref.1) | copy-start | bytes 786436
  1.7 3.3 %copy-start.2 = (f32[3,8,8,16]{3,2,1,0:T(8,128)S(1)}, f32[3,8,8,16]{3,2,1,0:T(8,128)}, u32[]{:S(2)}) copy-start(f32[3,8,8,16]{3,2,1,0:T(8,128)} %wind_ref.1) | copy-start | bytes 36868
  1.7 4.0 %copy-start.5 = (bf16[4096,64]{0,1:T(8,128)(2,1)S(1)}, bf16[4096,64]{0,1:T(8,128)(2,1)}, u32[]{:S(2)}) copy-start(bf16[4096,64]{0,1:T(8,128)(2,1)} %param.10) | copy-start | bytes 1572868
  2.0 4.2 %copy-start = (bf16[64,64]{1,0:T(8,128)(2,1)S(1)}, bf16[64,64]{1,0:T(8,128)(2,1)}, u32[]{:S(2)}) copy-start(bf16[64,64]{1,0:T(8,128)(2,1)} %loss_ref.1) | copy-start | bytes 24580
  2.0 6.9 %collective-permute-start = (f32[256,128]{1,0:T(8,128)S(1)}, f32[256,128]{1,0:T(8,128)S(1)}, u32[]{:S(2)}, u32[]{:S(2)}) collective-permute-start(f32[256,128]{1,0:T(8,128)S(1)} %get-tuple-element.38), channel_id=1, source_target_pairs={{0,1},{1,0},{2,3},{3,2},{4,5},{5,4},{6,7},{7,6},{8,9},{9,8},{10,11... | collective-permute-start | bytes 393224 | tf_op jit(solution)/shard_map/ppermute | solution.py:727
  5.1 3.7 %collective-permute-start.1 = (f32[24,128]{1,0:T(8,128)S(1)}, f32[24,128]{1,0:T(8,128)S(1)}, u32[]{:S(2)}, u32[]{:S(2)}) collective-permute-start(f32[24,128]{1,0:T(8,128)S(1)} %shard_map.78.own_wind_ref), channel_id=1, source_target_pairs={{0,1},{1,0},{2,3},{3,2},{4,5},{5,4},{6,7},{7,6},{8,9},{9,8},{10,11... | collective-permute-start | bytes 36872 | tf_op jit(solution)/shard_map/ppermute | solution.py:729
  9.1 6.6 %collective-permute-start.2 = (f32[432,128]{1,0:T(8,128)S(1)}, f32[432,128]{1,0:T(8,128)S(1)}, u32[]{:S(2)}, u32[]{:S(2)}) collective-permute-start(f32[432,128]{1,0:T(8,128)S(1)} %get-tuple-element.41), channel_id=1, source_target_pairs={{0,2},{1,3},{2,0},{3,1},{4,6},{5,7},{6,4},{7,5},{8,10},{9,11},{10,... | collective-permute-start | bytes 663560 | tf_op jit(solution)/shard_map/ppermute | solution.py:701
  10.8 4.8 %collective-permute-start.3 = (f32[432,128]{1,0:T(8,128)S(1)}, f32[432,128]{1,0:T(8,128)S(1)}, u32[]{:S(2)}, u32[]{:S(2)}) collective-permute-start(f32[432,128]{1,0:T(8,128)S(1)} %get-tuple-element.42), channel_id=1, source_target_pairs={{0,8},{1,9},{2,4},{3,5},{4,2},{5,3},{6,14},{7,15},{8,0},{9,1},{10,... | collective-permute-start | bytes 663560 | tf_op jit(solution)/shard_map/ppermute | solution.py:701
  10.9 8.4 %collective-permute-start.4 = (f32[408,128]{1,0:T(8,128)S(1)}, f32[408,128]{1,0:T(8,128)S(1)}, u32[]{:S(2)}, u32[]{:S(2)}) collective-permute-start(f32[408,128]{1,0:T(8,128)S(1)} %get-tuple-element.56), channel_id=1, source_target_pairs={{0,1},{1,0},{2,3},{3,2},{4,5},{5,4},{6,7},{7,6},{8,16},{9,17},{10,... | collective-permute-start | bytes 626696 | tf_op jit(solution)/shard_map/ppermute | solution.py:701
  12.4 6.9 %collective-permute-start.5 = (f32[408,128]{1,0:T(8,128)S(1)}, f32[408,128]{1,0:T(8,128)S(1)}, u32[]{:S(2)}, u32[]{:S(2)}) collective-permute-start(f32[408,128]{1,0:T(8,128)S(1)} %get-tuple-element.57), channel_id=1, source_target_pairs={{0,8},{1,9},{2,10},{3,11},{4,12},{5,13},{6,14},{7,15},{8,0},{9,1},... | collective-permute-start | bytes 626696 | tf_op jit(solution)/shard_map/ppermute | solution.py:701
  15.7 5.1 %collective-permute-start.6 = (f32[152,128]{1,0:T(8,128)S(1)}, f32[152,128]{1,0:T(8,128)S(1)}, u32[]{:S(2)}, u32[]{:S(2)}) collective-permute-start(f32[152,128]{1,0:T(8,128)S(1)} %get-tuple-element.62), channel_id=1, source_target_pairs={{0,1},{1,0},{2,3},{3,2},{4,5},{5,4},{6,7},{7,6},{8,16},{9,17},{10,... | collective-permute-start | bytes 233480 | tf_op jit(solution)/shard_map/ppermute | solution.py:701
  17.2 3.6 %collective-permute-start.7 = (f32[152,128]{1,0:T(8,128)S(1)}, f32[152,128]{1,0:T(8,128)S(1)}, u32[]{:S(2)}, u32[]{:S(2)}) collective-permute-start(f32[152,128]{1,0:T(8,128)S(1)} %get-tuple-element.63), channel_id=1, source_target_pairs={{0,8},{1,9},{2,10},{3,11},{4,12},{5,13},{6,14},{7,15},{8,0},{9,1},... | collective-permute-start | bytes 233480 | tf_op jit(solution)/shard_map/ppermute | solution.py:701
  19.3 1.5 %copy-start.3 = (f32[64]{0:T(128)S(1)}, f32[64]{0:T(128)}, u32[]{:S(2)}) copy-start(f32[64]{0:T(128)} %param.8) | copy-start | bytes 772
  19.3 1.5 %copy-start.4 = (s32[64]{0:T(128)S(1)}, s32[64]{0:T(128)}, u32[]{:S(2)}) copy-start(s32[64]{0:T(128)} %param.9) | copy-start | bytes 772
  23.1 5.0 %collective-permute-start.9 = (f32[176,128]{1,0:T(8,128)S(1)}, f32[176,128]{1,0:T(8,128)S(1)}, u32[]{:S(2)}, u32[]{:S(2)}) collective-permute-start(f32[176,128]{1,0:T(8,128)S(1)} %get-tuple-element.69), channel_id=1, source_target_pairs={{0,1},{1,0},{2,3},{3,2},{4,5},{5,4},{6,7},{7,6},{8,9},{9,8},{10,11... | collective-permute-start | bytes 270344 | tf_op jit(solution)/shard_map/ppermute | solution.py:803
  25.9 4.2 %collective-permute-start.8 = (f32[104,128]{1,0:T(8,128)S(1)}, f32[104,128]{1,0:T(8,128)S(1)}, u32[]{:S(2)}, u32[]{:S(2)}) collective-permute-start(f32[104,128]{1,0:T(8,128)S(1)} %get-tuple-element.66), channel_id=1, source_target_pairs={{0,1},{1,0},{2,3},{3,2},{4,5},{5,4},{6,7},{7,6},{8,9},{9,8},{10,11... | collective-permute-start | bytes 159752 | tf_op jit(solution)/shard_map/ppermute | solution.py:816

commit v2 on v0

--- a/solution.py
+++ b/solution.py
@@ -15,7 +15,7 @@
 LINES = LO + HI
 ROWS, LANES = 8, 128
 AHEAD = 4
-EARLY = 6
+EARLY = 5
 F32 = jnp.float32
 VMEM = pl.BlockSpec(memory_space=pltpu.VMEM)
 
@@ -76,7 +76,25 @@
         ref[rows_of(at)] = out[k * ROWS : (k + 1) * ROWS]
 
 
+def each(count, together, body):
+    def some(places):
+        stores = [store for i in places for store in body(i)]
+        for ref, at, value in stores:
+            ref[at] = value
+
+    whole = count // together
+
+    @pl.loop(0, whole)
+    def _(i):
+        some([i * together + k for k in range(together)])
+
+    if count % together:
+        some(range(whole * together, count))
+
+
 def halo_line(i, n):
+    if isinstance(i, int):
+        return i - LO + (n if i >= LO else 0)
     return jnp.where(i < LO, i - LO, i - LO + n)
 
 
@@ -109,14 +127,12 @@
         e0 = curved[j] + left * left
         e1 = curved[j + 1] + mid * mid
         e2 = curved[j + 2] + right * right
-        e0 = e0 * e0
+        e0 = 3.0 * (e0 * e0)
         e1 = e1 * e1
         e2 = e2 * e2
-        e0 = 3.0 * e0
         e2_twice = e2 + e2
         top = e1 * (e2_twice * third[j] + e0 * third[j + 1])
-        low = e1 * (e2 + e0) + e0 * e2_twice
-        inverse = pl.reciprocal(low, approx=True)
+        inverse = pl.reciprocal(e1 * (e2 + e0) + e0 * e2_twice, approx=True)
         estimate = 6.0 * cells[j + 2] + (first[j + 1] + twice[j + 2]) + top * inverse
         fluxes.append((winds[j] + winds[j + 1]) * estimate)
     return fluxes
@@ -240,25 +256,23 @@
             jobs += [(tile, x, y, out, x * n + y) for y in range(n)]
         spread(jobs, parts)
 
-    @pl.loop(0, n)
-    def _(x):
+    def along_z(x):
         cells = [block_ref[eight(x * n, k)] for k in range(ROWS)]
         winds = [wind_z[eight(x * n, k)] for k in range(ROWS)]
-        for k, value in enumerate(level_change(cells, winds, width)):
-            change[eight(x * n, k)] = value
-
+        return [(change, eight(x * n, k), value) for k, value in enumerate(level_change(cells, winds, width))]
+
+    each(n, 2, along_z)
     begin, end = LO, n - HI
     for wind, edge, place in ((wind_x, edge_x, lambda i, k: k * n + i), (wind_y, edge_y, lambda i, k: i * n + k)):
 
-        @pl.loop(0, n)
-        def _(i):
+        def along(i):
             cells = [block_ref[rows_of(place(i, k))] for k in range(n)]
             fluxes = line_fluxes(cells, [wind[rows_of(place(i, k))] for k in range(begin - 1, end + 1)])
-            edge[rows_of(i)] = fluxes[0]
-            edge[rows_of(n + i)] = fluxes[-1]
-            for k, value in zip(range(begin, end), changes(fluxes)):
-                at = rows_of(place(i, k))
-                change[at] = change[at] + value
+            at = [rows_of(place(i, k)) for k in range(begin, end)]
+            stores = [(change, here, change[here] + value) for here, value in zip(at, changes(fluxes))]
+            return stores + [(edge, rows_of(i), fluxes[0]), (edge, rows_of(n + i), fluxes[-1])]
+
+        each(n, 4, along)
 
 
 def y_kernel(n, parts, block_ref, first_ref, second_ref, wind_y, own_change, edge_y, *refs):
@@ -285,27 +299,36 @@
                     jobs += [(high, x, y, out, (LO + y) * n + x) for y in range(HI)]
     spread(jobs, parts)
 
-    @pl.loop(0, LINES)
-    def _(i):
+    def along_z(i):
         first = halo_line(i, n) + PAD_LO
         cells = [cell[eight(first, k, span)] for k in range(ROWS)]
         winds = [wind_z[eight(i * n, k)] for k in range(ROWS)]
-        for k, value in enumerate(level_change(cells, winds, width)):
-            halo_change[eight(i * n, k)] = value
-
-    @pl.loop(0, n)
-    def _(x):
+        return [(halo_change, eight(i * n, k), value) for k, value in enumerate(level_change(cells, winds, width))]
+
+    each(LINES, 2, along_z)
+
+    def along_y(x):
         cells = [cell[rows_of(x * span + y)] for y in range(span)]
         far = [far_y[rows_of(x * (LINES + 2) + y)] for y in range(LINES + 2)]
         winds = far[: LO + 1] + [wind_y[rows_of(x * n + y)] for y in range(n)] + far[LO + 1 :]
+        stores = []
         for y, value in long_line(cells, winds, edge_y[rows_of(x)], edge_y[rows_of(n + x)], n).items():
             if 0 <= y < n:
                 value = value + own_change[rows_of(x * n + y)]
             else:
                 value = value + halo_change[rows_of((y + LO if y < 0 else y + LO - n) * n + x)]
-            change[rows_of(x * reach + y + LO)] = value
+            stores.append((change, rows_of(x * reach + y + LO), value))
         for y in range(LO, n - HI):
-            change[rows_of(x * reach + y + LO)] = own_change[rows_of(x * n + y)]
+            stores.append((change, rows_of(x * reach + y + LO), own_change[rows_of(x * n + y)]))
+        return stores
+
+    each(n, 2, along_y)
+
+
+def which(i, lower, upper):
+    if isinstance(i, int):
+        return lower if i < LO else upper
+    return jnp.where(i < LO, lower, upper)
 
 
 def inside(axis):
@@ -325,35 +348,41 @@
         x = begin + i
         one[rows_of(i * reach + LO, n)] = cell[rows_of(x * span + PAD_LO, n)] + change[rows_of(x * reach + LO, n)]
 
-    @pl.loop(0, LINES)
-    def _(i):
+    def along_x(i):
         at = halo_line(i, n) + LO
         cells = [cell[rows_of(x * span + LO + at)] for x in range(n)]
         fluxes = line_fluxes(cells, [halo_wind_x[rows_of(i * n + x)] for x in range(begin - 1, end + 1)])
-        edge[rows_of(at)] = fluxes[0]
-        edge[rows_of(reach + at)] = fluxes[-1]
-        keep = jnp.where(i < LO, south_in, north_in)
+        keep = which(i, south_in, north_in)
+        stores = [(edge, rows_of(at), fluxes[0]), (edge, rows_of(reach + at), fluxes[-1])]
         for k, value in enumerate(changes(fluxes)):
             x = begin + k
-            one[rows_of(k * reach + at)] = (cells[x] + (value + change[rows_of(x * reach + at)])) * keep
-
-    @pl.loop(0, end - begin)
-    def _(i):
-        second_y_z(n, width, begin + i, one, i, wind_y, far_wind_y, wind_z, second, i)
-
-
-def second_y_z(n, width, x, one, one_x, wind_y, far_wind_y, wind_z, second, second_x):
+            value = (cells[x] + (value + change[rows_of(x * reach + at)])) * keep
+            stores.append((one, rows_of(k * reach + at), value))
+        return stores
+
+    each(LINES, LINES, along_x)
+    second_y_z(n, width, range(begin, end), begin, one, begin, wind_y, far_wind_y, wind_z, second)
+
+
+def second_y_z(n, width, layers, first, one, one_first, wind_y, far_wind_y, wind_z, second):
     reach = n + LINES
-    cells = [one[rows_of(one_x * reach + y)] for y in range(reach)]
-    winds = [far_wind_y[rows_of(x * (LINES + 2) + LO)]] + [wind_y[rows_of(x * n + y)] for y in range(n)]
-    winds += [far_wind_y[rows_of(x * (LINES + 2) + LO + 1)]]
-    for y, value in enumerate(line_change(cells, winds)):
-        second[rows_of(second_x * n + y)] = value
-    cells = [one[eight(one_x * reach + LO, k)] for k in range(ROWS)]
-    winds = [wind_z[eight(x * n, k)] for k in range(ROWS)]
-    for k, value in enumerate(level_change(cells, winds, width)):
-        at = eight(second_x * n, k)
-        second[at] = second[at] + value
+
+    def along_y(i):
+        x = layers[0] + i
+        cells = [one[rows_of((x - one_first) * reach + y)] for y in range(reach)]
+        winds = [far_wind_y[rows_of(x * (LINES + 2) + LO)]] + [wind_y[rows_of(x * n + y)] for y in range(n)]
+        winds += [far_wind_y[rows_of(x * (LINES + 2) + LO + 1)]]
+        return [(second, rows_of((x - first) * n + y), value) for y, value in enumerate(line_change(cells, winds))]
+
+    def along_z(i):
+        x = layers[0] + i
+        cells = [one[eight((x - one_first) * reach + LO, k)] for k in range(ROWS)]
+        winds = [wind_z[eight(x * n, k)] for k in range(ROWS)]
+        at = [eight((x - first) * n, k) for k in range(ROWS)]
+        return [(second, here, second[here] + value) for here, value in zip(at, level_change(cells, winds, width))]
+
+    each(len(layers), len(layers), along_y)
+    each(len(layers), len(layers), along_z)
 
 
 def x_kernel(n, parts, cell, change, wind_x, edge, second_ref, first_ref, mid, far_wind_x, side, side_wind_y, *scratch):
@@ -381,26 +410,29 @@
                 jobs += [(winds_of(d, x), x, y, out, (line + i) * n + y) for y in range(n)]
     spread(jobs, parts)
 
-    @pl.loop(0, LINES)
-    def _(i):
+    def along_z(i):
         cells = [side[eight(i * n, k)] for k in range(ROWS)]
         winds = [side_wind_z[eight(i * n, k)] for k in range(ROWS)]
-        for k, value in enumerate(level_change(cells, winds, width)):
-            side_change[eight(i * n, k)] = value
-
-    @pl.loop(0, n)
-    def _(y):
+        return [(side_change, eight(i * n, k), value) for k, value in enumerate(level_change(cells, winds, width))]
+
+    each(LINES, 2, along_z)
+
+    def along_x(y):
         outer = [far[rows_of(i * n + y)] for i in range(LINES)]
         near = [side[rows_of(i * n + y)] for i in range(LINES)]
         cells = outer[:LO] + near[:LO] + [cell[rows_of(x * span + PAD_LO + y)] for x in range(n)] + near[LO:] + outer[LO:]
         winds = [far_wind_x[rows_of(i * n + y)] for i in range(LINES + 2)]
         winds = winds[: LO + 1] + [wind_x[rows_of(x * n + y)] for x in range(n)] + winds[LO + 1 :]
+        stores = []
         for x, value in long_line(cells, winds, edge[rows_of(LO + y)], edge[rows_of(reach + LO + y)], n).items():
             if 0 <= x < n:
                 value = value + change[rows_of(x * reach + LO + y)]
             else:
                 value = value + side_change[rows_of((x + LO if x < 0 else x + LO - n) * n + y)]
-            mid[rows_of((x + LO) * n + y)] = cells[PAD_LO + x] + value
+            stores.append((mid, rows_of((x + LO) * n + y), cells[PAD_LO + x] + value))
+        return stores
+
+    each(n, 2, along_x)
 
 
 def main_kernel(n, parts, *refs):
@@ -436,31 +468,34 @@
     for x in [x for x in range(n) if not begin <= x < end]:
         one[rows_of((x + LO) * reach + LO, n)] = mid[rows_of((x + LO) * n, n)]
 
-    @pl.loop(0, LINES)
-    def _(i):
+    def along_y(i):
         corners = [corner[rows_of(i * LINES + y)] for y in range(LINES)]
         cells = corners[:LO] + [side[rows_of(i * n + y)] for y in range(n)] + corners[LO:]
         winds = [side_wind_y[rows_of(i * n + y)] for y in range(n)]
         winds = [edge_wind_y[rows_of(2 * i)]] + winds + [edge_wind_y[rows_of(2 * i + 1)]]
-        keep = jnp.where(i < LO, west_in, east_in)
         line = halo_line(i, n) + LO
-        for y, value in enumerate(line_change(cells, winds)):
-            one[rows_of(line * reach + LO + y)] = (mid[rows_of(line * n + y)] + value) * keep
-
-    @pl.loop(0, LINES)
-    def _(i):
+        return [
+            (one, rows_of(line * reach + LO + y), (mid[rows_of(line * n + y)] + value) * which(i, west_in, east_in))
+            for y, value in enumerate(line_change(cells, winds))
+        ]
+
+    def along_x(i):
         line = halo_line(i, n) + LO
         near = [corner[rows_of(k * LINES + i)] for k in range(LINES)]
         cells = near[:LO] + [cell[rows_of(x * span + LO + line)] for x in range(n)] + near[LO:]
         winds = [halo_wind_x[rows_of(i * n + x)] for x in range(n)]
         winds = [corner_wind_x[rows_of(i)]] + winds + [corner_wind_x[rows_of(LINES + i)]]
-        keep = jnp.where(i < LO, south_in, north_in)
         low = line_fluxes(cells[: LO + begin + 1], winds[: begin + 1]) + [edge[rows_of(line)]]
         high = [edge[rows_of(reach + line)]] + line_fluxes(cells[LO + end - HI :], winds[end + 1 :])
         values = dict(zip(range(begin), changes(low))) | dict(zip(range(end, n), changes(high)))
+        stores = []
         for x, value in values.items():
-            one[rows_of((x + LO) * reach + line)] = (cells[x + LO] + (value + change[rows_of(x * reach + line)])) * keep
-
+            value = (cells[x + LO] + (value + change[rows_of(x * reach + line)])) * which(i, south_in, north_in)
+            stores.append((one, rows_of((x + LO) * reach + line), value))
+        return stores
+
+    each(LINES, 2, along_y)
+    each(LINES, LINES, along_x)
     fall_layers(
         n, parts, 0, EARLY, one, cell, wind_x, far_wind_x, wind_y, far_wind_y, wind_z, inner_second, rate_ref, steps_ref,
         out_refs, second, fallen,
@@ -487,21 +522,23 @@
     if ready:
         second[rows_of((ready[0] - begin) * n, len(ready) * n)] = inner_second[rows_of((ready[0] - LO) * n, len(ready) * n)]
 
-    @pl.loop(left[0], left[-1] + 1)
-    def _(x):
-        second_y_z(n, width, x, one, x + LO, wind_y, far_wind_y, wind_z, second, x - begin)
-
-    @pl.loop(0, n)
-    def _(y):
+    second_y_z(n, width, left, begin, one, -LO, wind_y, far_wind_y, wind_z, second)
+
+    def along_x(y):
         cells = [one[rows_of(x * reach + LO + y)] for x in range(begin, end + LINES)]
         winds = [wind_x[rows_of(x * n + y)] for x in range(max(begin - 1, 0), min(end + 1, n))]
         if begin == 0:
             winds = [far_wind_x[rows_of(LO * n + y)]] + winds
         if end == n:
             winds = winds + [far_wind_x[rows_of((LO + 1) * n + y)]]
+        stores = []
         for i, value in enumerate(line_change(cells, winds)):
             value = cells[i + LO] + (value + second[rows_of(i * n + y)])
-            fallen[rows_of(i * n + y)] = 0.5 * cell[rows_of((begin + i) * span + PAD_LO + y)] + 0.5 * value
+            value = 0.5 * cell[rows_of((begin + i) * span + PAD_LO + y)] + 0.5 * value
+            stores.append((fallen, rows_of(i * n + y), value))
+        return stores
+
+    each(n, 4, along_x)
 
     bins = LANES // 2 // parts
     ids = lax.axis_index("gz") * bins + lane_ids() % bins

time: 32.3 us -> 30.9 us (0.957)
  Pallas kernels: 13.8 us -> 12.4 us
    pallas_call x13, Pallas kernels: 13.8 us -> 12.4 us  [call(): pl.pallas_call(kernel, out_shape=outs, in_specs=[VMEM] * len(args), out_s...]
    ppermute x1, waiting for transfers between devices: 2.47 us -> 1.81 us  [per_device(): early_got = lax.ppermute(early[0], 'gz', [(0, 1), (1, 0)])]
    ppermute x6, waiting for transfers between devices: 1.5 us -> 1.98 us  [swap_neighbours(): return lax.ppermute(message, axes, pairs)]
  transfers between devices with their start and end apart: 10 -> 10, of which waited for: 3 -> 4; matrix products, arithmetic and copies ran while one was open for 1% -> 2% of each run, Pallas kernels for 29% -> 27%
where the time goes in v2:
time: 30.9 us; the launch traced here: 30.8 us
  Pallas kernels  12.4 us (40%)
  starting transfers between devices  10.7 us (35%)
  waiting for transfers between devices  5.35 us (17%)
  local copies, waits for them, and re-layouts  1.54 us (5%)
  between operations  0.77 us (2%)
    pallas_call x13, Pallas kernels, call(): pl.pallas_call(kernel, out_shape=outs, in_specs=[VMEM] * len(args), out_s...  12.4 us
    ppermute x6, starting transfers between devices, swap_neighbours(): return lax.ppermute(message, axes, pairs)  4.95 us
    ppermute x1, starting transfers between devices, per_device(): got = lax.ppermute(send, 'gz', [(0, 1), (1, 0)])  3.03 us
    ppermute x6, waiting for transfers between devices, swap_neighbours(): return lax.ppermute(message, axes, pairs)  1.98 us
    ppermute x1, waiting for transfers between devices, per_device(): early_got = lax.ppermute(early[0], 'gz', [(0, 1), (1, 0)])  1.81 us
    ppermute x1, starting transfers between devices, per_device(): early_got = lax.ppermute(early[0], 'gz', [(0, 1), (1, 0)])  1.58 us
    unnamed x13, local copies, waits for them, and re-layouts  1.54 us
    ppermute x1, waiting for transfers between devices, per_device(): got_wind = lax.ppermute(own_wind, 'gz', [(0, 1), (1, 0)])  1.31 us
  transfers between devices with their start and end apart: 10, of which 4 were waited for; matrix products, arithmetic and copies ran while one was open for 2% of the time, Pallas kernels for 27%

profile of v2, /device:TPU:0, one launch (start us, length us, event | category | flops | bytes accessed | tf_op | source)
XLA Modules:
  0.0 30.8 jit_solution(3319963056727133538)
XLA Ops:
  0.6 0.0 copy-start.1
  0.6 1.0 %copy-done.1 = f32[8,8,16,64]{3,2,1,0:T(8,128)S(1)} copy-done((f32[8,8,16,64]{3,2,1,0:T(8,128)S(1)}, f32[8,8,16,64]{3,2,1,0:T(8,128)}, u32[]{:S(2)}) %copy-start.1) | copy-done | bytes 262168
  1.7 0.0 copy-start.2
  1.7 0.0 copy-start.5
  1.7 0.3 shard_map.77
  2.0 0.0 copy-start
  2.0 3.0 %collective-permute-start = (f32[256,128]{1,0:T(8,128)S(1)}, f32[256,128]{1,0:T(8,128)S(1)}, u32[]{:S(2)}, u32[]{:S(2)}) collective-permute-start(f32[256,128]{1,0:T(8,128)S(1)} %get-tuple-element.38), channel_id=1, source_target_pairs={{0,1},{1,0},{2,3},{3,2},{4,5},{5,4},{6,7},{7,6},{8,9},{9,8},{10,11... | collective-permute-start | bytes 393224 | tf_op jit(solution)/shard_map/ppermute | solution.py:766
  5.0 0.0 copy-done.2
  5.0 0.1 shard_map.78.own_wind_ref
  5.1 0.6 %collective-permute-start.1 = (f32[24,128]{1,0:T(8,128)S(1)}, f32[24,128]{1,0:T(8,128)S(1)}, u32[]{:S(2)}, u32[]{:S(2)}) collective-permute-start(f32[24,128]{1,0:T(8,128)S(1)} %shard_map.78.own_wind_ref), channel_id=1, source_target_pairs={{0,1},{1,0},{2,3},{3,2},{4,5},{5,4},{6,7},{7,6},{8,9},{9,8},{10,11... | collective-permute-start | bytes 36872 | tf_op jit(solution)/shard_map/ppermute | solution.py:768
  5.7 0.0 copy-done.5
  5.7 0.5 %copy.8.gain_ref = bf16[4096,64]{1,0:T(8,128)(2,1)S(1)} copy(bf16[4096,64]{0,1:T(8,128)(2,1)S(1)} %copy-done.5) | data formatting | bytes 1048576 | tf_op args[4]
  6.2 0.0 copy-done
  6.2 1.4 %shard_map.79 = (bf16[4224,128]{1,0:T(8,128)(2,1)S(1)}, bf16[128,128]{1,0:T(8,128)(2,1)S(1)}) custom-call(bf16[4096,64]{1,0:T(8,128)(2,1)S(1)} %copy.8.gain_ref, bf16[64,64]{1,0:T(8,128)(2,1)S(1)} %copy-done), custom_call_target="tpu_custom_call" | custom-call | flops 22000000 | bytes 72000 | tf_op jit(solution)/shard_map/pallas_call | solution.py:710
  7.5 1.3 %collective-permute-done.1.got_wind_ref = f32[24,128]{1,0:T(8,128)S(1)} collective-permute-done((f32[24,128]{1,0:T(8,128)S(1)}, f32[24,128]{1,0:T(8,128)S(1)}, u32[]{:S(2)}, u32[]{:S(2)}) %collective-permute-start.1) | collective-permute-done | bytes 12320 | tf_op jit(solution)/shard_map/ppermute | solution.py:768
  8.9 0.0 collective-permute-done.got_ref
  8.9 0.2 shard_map.80
  9.1 1.8 %collective-permute-start.2 = (f32[432,128]{1,0:T(8,128)S(1)}, f32[432,128]{1,0:T(8,128)S(1)}, u32[]{:S(2)}, u32[]{:S(2)}) collective-permute-start(f32[432,128]{1,0:T(8,128)S(1)} %get-tuple-element.41), channel_id=1, source_target_pairs={{0,2},{1,3},{2,0},{3,1},{4,6},{5,7},{6,4},{7,5},{8,10},{9,11},{10,... | collective-permute-start | bytes 663560 | tf_op jit(solution)/shard_map/ppermute | solution.py:740
  10.8 0.0 collective-permute-start.3
  10.9 1.5 %collective-permute-start.4 = (f32[408,128]{1,0:T(8,128)S(1)}, f32[408,128]{1,0:T(8,128)S(1)}, u32[]{:S(2)}, u32[]{:S(2)}) collective-permute-start(f32[408,128]{1,0:T(8,128)S(1)} %get-tuple-element.56), channel_id=1, source_target_pairs={{0,1},{1,0},{2,3},{3,2},{4,5},{5,4},{6,7},{7,6},{8,16},{9,17},{10,... | collective-permute-start | bytes 626696 | tf_op jit(solution)/shard_map/ppermute | solution.py:740
  12.4 0.1 collective-permute-start.5
  12.5 1.3 %shard_map.81 = (f32[512,128]{1,0:T(8,128)S(1)}, f32[512,128]{1,0:T(8,128)S(1)}, f32[512,128]{1,0:T(8,128)S(1)}, f32[512,128]{1,0:T(8,128)S(1)}, f32[128,128]{1,0:T(8,128)S(1)}, /*index=5*/f32[128,128]{1,0:T(8,128)S(1)}) custom-call(f32[560,128]{1,0:T(8,128)S(1)} %get-tuple-element.40.block_ref), custom_call_target="tpu_custom_call" | custom-call | flops 1760000000 | bytes 5760000 | tf_op jit(solution)/shard_map/pallas_call | solution.py:710
  13.7 1.9 %collective-permute-done.2.first_ref = f32[432,128]{1,0:T(8,128)S(1)} collective-permute-done((f32[432,128]{1,0:T(8,128)S(1)}, f32[432,128]{1,0:T(8,128)S(1)}, u32[]{:S(2)}, u32[]{:S(2)}) %collective-permute-start.2) | collective-permute-done | bytes 221216 | tf_op jit(solution)/shard_map/ppermute | solution.py:740
  15.7 0.0 collective-permute-done.3.second_ref
  15.7 1.5 %collective-permute-start.6 = (f32[152,128]{1,0:T(8,128)S(1)}, f32[152,128]{1,0:T(8,128)S(1)}, u32[]{:S(2)}, u32[]{:S(2)}) collective-permute-start(f32[152,128]{1,0:T(8,128)S(1)} %get-tuple-element.62), channel_id=1, source_target_pairs={{0,1},{1,0},{2,3},{3,2},{4,5},{5,4},{6,7},{7,6},{8,16},{9,17},{10,... | collective-permute-start | bytes 233480 | tf_op jit(solution)/shard_map/ppermute | solution.py:740
  17.2 0.1 collective-permute-start.7
  17.3 1.2 %shard_map.82 = (f32[1152,128]{1,0:T(8,128)S(1)}, f32[832,128]{1,0:T(8,128)S(1)}, f32[320,128]{1,0:T(8,128)S(1)}, f32[448,128]{1,0:T(8,128)S(1)}) custom-call(f32[560,128]{1,0:T(8,128)S(1)} %get-tuple-element.40.block_ref, f32[432,128]{1,0:T(8,128)S(1)} %collective-permute-done.2.first_ref, f32[432,128]{1,0:T(8,128)S(1)} %collective-permute-done.3.second_ref, ...), custom_call_target="tpu_custom_call" | custom-call | flops 2200000000 | bytes 7200000 | tf_op jit(solution)/shard_map/pallas_call | solution.py:710
  18.4 0.5 %shard_map.83 = (f32[312,128]{1,0:T(8,128)S(1)}, f32[208,128]{1,0:T(8,128)S(1)}, f32[192,128]{1,0:T(8,128)S(1)}) custom-call(f32[1152,128]{1,0:T(8,128)S(1)} %get-tuple-element.46.cell.refs_0_, f32[832,128]{1,0:T(8,128)S(1)} %get-tuple-element.47.change.refs_1_, f32[320,128]{1,0:T(8,128)S(1)} %get-tuple-element.50.halo_wind_x.refs_5_, ...), custom_call_target="tpu_custom_call" | custom-call | flops 990000000 | bytes 3240000 | tf_op jit(solution)/shard_map/pallas_call | solution.py:710
  18.9 0.0 collective-permute-done.4.second_ref
  18.9 0.0 collective-permute-done.5.first_ref
  18.9 0.0 copy-start.3
  18.9 0.0 copy-start.4
  18.9 1.2 %shard_map.84 = (f32[832,128]{1,0:T(8,128)S(1)}, f32[448,128]{1,0:T(8,128)S(1)}, f32[320,128]{1,0:T(8,128)S(1)}, f32[320,128]{1,0:T(8,128)S(1)}) custom-call(f32[1152,128]{1,0:T(8,128)S(1)} %get-tuple-element.46.cell.refs_0_, f32[832,128]{1,0:T(8,128)S(1)} %get-tuple-element.47.change.refs_1_, f32[512,128]{1,0:T(8,128)S(1)} %get-tuple-element.48.wind_x.refs_2_, ...), custom_call_target="tpu_custom_call" | custom-call | flops 1870000000 | bytes 6120000 | tf_op jit(solution)/shard_map/pallas_call | solution.py:710
  20.1 0.0 collective-permute-done.6.refs_14_
  20.2 0.0 collective-permute-done.7.refs_15_
  20.2 0.0 copy-done.3
  20.2 0.0 copy-done.4
  20.2 2.0 %shard_map.86 = (f32[1352,128]{1,0:T(8,128)S(1)}, f32[176,128]{1,0:T(8,128)S(1)}, f32[176,128]{1,0:T(8,128)S(1)}) custom-call(f32[1152,128]{1,0:T(8,128)S(1)} %get-tuple-element.46.cell.refs_0_, f32[832,128]{1,0:T(8,128)S(1)} %get-tuple-element.47.change.refs_1_, f32[512,128]{1,0:T(8,128)S(1)} %get-tuple-element.48.wind_x.refs_2_, ...), custom_call_target="tpu_custom_call" | custom-call | flops 2860000000 | bytes 9360000 | tf_op jit(solution)/shard_map/pallas_call | solution.py:710
  22.2 1.6 %collective-permute-start.9 = (f32[176,128]{1,0:T(8,128)S(1)}, f32[176,128]{1,0:T(8,128)S(1)}, u32[]{:S(2)}, u32[]{:S(2)}) collective-permute-start(f32[176,128]{1,0:T(8,128)S(1)} %get-tuple-element.69), channel_id=1, source_target_pairs={{0,1},{1,0},{2,3},{3,2},{4,5},{5,4},{6,7},{7,6},{8,9},{9,8},{10,11... | collective-permute-start | bytes 270344 | tf_op jit(solution)/shard_map/ppermute | solution.py:842
  23.8 1.0 %shard_map.87 = (f32[104,128]{1,0:T(8,128)S(1)}, f32[104,128]{1,0:T(8,128)S(1)}) custom-call(f32[1352,128]{1,0:T(8,128)S(1)} %get-tuple-element.64.one, f32[1152,128]{1,0:T(8,128)S(1)} %get-tuple-element.46.cell.refs_0_, f32[512,128]{1,0:T(8,128)S(1)} %get-tuple-element.48.wind_x.refs_2_, f32[448,128]{1,0:T(8,128)S(1)} %get-tuple-element.59.refs_11_.far_wind_x, ...), custom_call_target="tpu_custom_call" | custom-call | flops 770000000 | bytes 2520000 | tf_op jit(solution)/shard_map/pallas_call | solution.py:710
  24.8 0.6 %collective-permute-start.8 = (f32[104,128]{1,0:T(8,128)S(1)}, f32[104,128]{1,0:T(8,128)S(1)}, u32[]{:S(2)}, u32[]{:S(2)}) collective-permute-start(f32[104,128]{1,0:T(8,128)S(1)} %get-tuple-element.66), channel_id=1, source_target_pairs={{0,1},{1,0},{2,3},{3,2},{4,5},{5,4},{6,7},{7,6},{8,9},{9,8},{10,11... | collective-permute-start | bytes 159752 | tf_op jit(solution)/shard_map/ppermute | solution.py:855
  25.4 1.8 %collective-permute-done.9.got_ref = f32[176,128]{1,0:T(8,128)S(1)} collective-permute-done((f32[176,128]{1,0:T(8,128)S(1)}, f32[176,128]{1,0:T(8,128)S(1)}, u32[]{:S(2)}, u32[]{:S(2)}) %collective-permute-start.9) | collective-permute-done | bytes 90144 | tf_op jit(solution)/shard_map/ppermute | solution.py:842
  27.2 1.6 %shard_map.88 = (f32[5,8,16,64]{3,2,1,0:T(8,128)S(1)}, f32[5,4,64]{2,1,0:T(4,128)S(1)}) custom-call(f32[176,128]{1,0:T(8,128)S(1)} %get-tuple-element.68.keep_ref, f32[176,128]{1,0:T(8,128)S(1)} %collective-permute-done.9.got_ref, bf16[4224,128]{1,0:T(8,128)(2,1)S(1)} %get-tuple-element.67.pairs_ref, bf16[128,128]{1,0:T(8,128)(2,1)S(1)} %get-tuple-element.39.lost_ref), custom_call_target="tpu_custom_call" | custom-call | flops 1980000000 | bytes 6480000 | tf_op jit(solution)/shard_map/pallas_call | solution.py:710
  28.8 0.2 collective-permute-done.8.got_ref
  29.0 1.8 %shard_map.89 = (f32[8,8,16,64]{3,2,1,0:T(8,128)}, f32[8,4,64]{2,1,0:T(4,128)}) custom-call(f32[104,128]{1,0:T(8,128)S(1)} %get-tuple-element.65.keep_ref, f32[104,128]{1,0:T(8,128)S(1)} %collective-permute-done.8.got_ref, bf16[4224,128]{1,0:T(8,128)(2,1)S(1)} %get-tuple-element.67.pairs_ref, bf16[128,128]{1,0:T(8,128)(2,1)S(1)} %get-tuple-element.39.lost_ref, ...), custom_call_target="tpu_custom_call" | custom-call | flops 1320000000 | bytes 4320000 | tf_op jit(solution)/shard_map/pallas_call | solution.py:710
  (1 shorter events, 0.0 us)
Async XLA Ops:
  0.6 1.0 %copy-start.1 = (f32[8,8,16,64]{3,2,1,0:T(8,128)S(1)}, f32[8,8,16,64]{3,2,1,0:T(8,128)}, u32[]{:S(2)}) copy-start(f32[8,8,16,64]{3,2,1,0:T(8,128)} %mass_ref.1) | copy-start | bytes 786436
  1.7 3.3 %copy-start.2 = (f32[3,8,8,16]{3,2,1,0:T(8,128)S(1)}, f32[3,8,8,16]{3,2,1,0:T(8,128)}, u32[]{:S(2)}) copy-start(f32[3,8,8,16]{3,2,1,0:T(8,128)} %wind_ref.1) | copy-start | bytes 36868
  1.7 4.0 %copy-start.5 = (bf16[4096,64]{0,1:T(8,128)(2,1)S(1)}, bf16[4096,64]{0,1:T(8,128)(2,1)}, u32[]{:S(2)}) copy-start(bf16[4096,64]{0,1:T(8,128)(2,1)} %param.10) | copy-start | bytes 1572868
  2.0 4.2 %copy-start = (bf16[64,64]{1,0:T(8,128)(2,1)S(1)}, bf16[64,64]{1,0:T(8,128)(2,1)}, u32[]{:S(2)}) copy-start(bf16[64,64]{1,0:T(8,128)(2,1)} %loss_ref.1) | copy-start | bytes 24580
  2.0 6.9 %collective-permute-start = (f32[256,128]{1,0:T(8,128)S(1)}, f32[256,128]{1,0:T(8,128)S(1)}, u32[]{:S(2)}, u32[]{:S(2)}) collective-permute-start(f32[256,128]{1,0:T(8,128)S(1)} %get-tuple-element.38), channel_id=1, source_target_pairs={{0,1},{1,0},{2,3},{3,2},{4,5},{5,4},{6,7},{7,6},{8,9},{9,8},{10,11... | collective-permute-start | bytes 393224 | tf_op jit(solution)/shard_map/ppermute | solution.py:766
  5.1 3.7 %collective-permute-start.1 = (f32[24,128]{1,0:T(8,128)S(1)}, f32[24,128]{1,0:T(8,128)S(1)}, u32[]{:S(2)}, u32[]{:S(2)}) collective-permute-start(f32[24,128]{1,0:T(8,128)S(1)} %shard_map.78.own_wind_ref), channel_id=1, source_target_pairs={{0,1},{1,0},{2,3},{3,2},{4,5},{5,4},{6,7},{7,6},{8,9},{9,8},{10,11... | collective-permute-start | bytes 36872 | tf_op jit(solution)/shard_map/ppermute | solution.py:768
  9.1 6.6 %collective-permute-start.2 = (f32[432,128]{1,0:T(8,128)S(1)}, f32[432,128]{1,0:T(8,128)S(1)}, u32[]{:S(2)}, u32[]{:S(2)}) collective-permute-start(f32[432,128]{1,0:T(8,128)S(1)} %get-tuple-element.41), channel_id=1, source_target_pairs={{0,2},{1,3},{2,0},{3,1},{4,6},{5,7},{6,4},{7,5},{8,10},{9,11},{10,... | collective-permute-start | bytes 663560 | tf_op jit(solution)/shard_map/ppermute | solution.py:740
  10.8 4.8 %collective-permute-start.3 = (f32[432,128]{1,0:T(8,128)S(1)}, f32[432,128]{1,0:T(8,128)S(1)}, u32[]{:S(2)}, u32[]{:S(2)}) collective-permute-start(f32[432,128]{1,0:T(8,128)S(1)} %get-tuple-element.42), channel_id=1, source_target_pairs={{0,8},{1,9},{2,4},{3,5},{4,2},{5,3},{6,14},{7,15},{8,0},{9,1},{10,... | collective-permute-start | bytes 663560 | tf_op jit(solution)/shard_map/ppermute | solution.py:740
  10.9 8.1 %collective-permute-start.4 = (f32[408,128]{1,0:T(8,128)S(1)}, f32[408,128]{1,0:T(8,128)S(1)}, u32[]{:S(2)}, u32[]{:S(2)}) collective-permute-start(f32[408,128]{1,0:T(8,128)S(1)} %get-tuple-element.56), channel_id=1, source_target_pairs={{0,1},{1,0},{2,3},{3,2},{4,5},{5,4},{6,7},{7,6},{8,16},{9,17},{10,... | collective-permute-start | bytes 626696 | tf_op jit(solution)/shard_map/ppermute | solution.py:740
  12.4 6.5 %collective-permute-start.5 = (f32[408,128]{1,0:T(8,128)S(1)}, f32[408,128]{1,0:T(8,128)S(1)}, u32[]{:S(2)}, u32[]{:S(2)}) collective-permute-start(f32[408,128]{1,0:T(8,128)S(1)} %get-tuple-element.57), channel_id=1, source_target_pairs={{0,8},{1,9},{2,10},{3,11},{4,12},{5,13},{6,14},{7,15},{8,0},{9,1},... | collective-permute-start | bytes 626696 | tf_op jit(solution)/shard_map/ppermute | solution.py:740
  15.7 4.5 %collective-permute-start.6 = (f32[152,128]{1,0:T(8,128)S(1)}, f32[152,128]{1,0:T(8,128)S(1)}, u32[]{:S(2)}, u32[]{:S(2)}) collective-permute-start(f32[152,128]{1,0:T(8,128)S(1)} %get-tuple-element.62), channel_id=1, source_target_pairs={{0,1},{1,0},{2,3},{3,2},{4,5},{5,4},{6,7},{7,6},{8,16},{9,17},{10,... | collective-permute-start | bytes 233480 | tf_op jit(solution)/shard_map/ppermute | solution.py:740
  17.2 3.0 %collective-permute-start.7 = (f32[152,128]{1,0:T(8,128)S(1)}, f32[152,128]{1,0:T(8,128)S(1)}, u32[]{:S(2)}, u32[]{:S(2)}) collective-permute-start(f32[152,128]{1,0:T(8,128)S(1)} %get-tuple-element.63), channel_id=1, source_target_pairs={{0,8},{1,9},{2,10},{3,11},{4,12},{5,13},{6,14},{7,15},{8,0},{9,1},... | collective-permute-start | bytes 233480 | tf_op jit(solution)/shard_map/ppermute | solution.py:740
  18.9 1.2 %copy-start.3 = (f32[64]{0:T(128)S(1)}, f32[64]{0:T(128)}, u32[]{:S(2)}) copy-start(f32[64]{0:T(128)} %param.8) | copy-start | bytes 772
  18.9 1.2 %copy-start.4 = (s32[64]{0:T(128)S(1)}, s32[64]{0:T(128)}, u32[]{:S(2)}) copy-start(s32[64]{0:T(128)} %param.9) | copy-start | bytes 772
  22.2 5.0 %collective-permute-start.9 = (f32[176,128]{1,0:T(8,128)S(1)}, f32[176,128]{1,0:T(8,128)S(1)}, u32[]{:S(2)}, u32[]{:S(2)}) collective-permute-start(f32[176,128]{1,0:T(8,128)S(1)} %get-tuple-element.69), channel_id=1, source_target_pairs={{0,1},{1,0},{2,3},{3,2},{4,5},{5,4},{6,7},{7,6},{8,9},{9,8},{10,11... | collective-permute-start | bytes 270344 | tf_op jit(solution)/shard_map/ppermute | solution.py:842
  24.8 4.2 %collective-permute-start.8 = (f32[104,128]{1,0:T(8,128)S(1)}, f32[104,128]{1,0:T(8,128)S(1)}, u32[]{:S(2)}, u32[]{:S(2)}) collective-permute-start(f32[104,128]{1,0:T(8,128)S(1)} %get-tuple-element.66), channel_id=1, source_target_pairs={{0,1},{1,0},{2,3},{3,2},{4,5},{5,4},{6,7},{7,6},{8,9},{9,8},{10,11... | collective-permute-start | bytes 159752 | tf_op jit(solution)/shard_map/ppermute | solution.py:855

commit v3 on v2

--- a/solution.py
+++ b/solution.py
@@ -118,21 +118,21 @@
     twice = [d + d for d in first]
     second = [b - a for a, b in zip(first, first[1:])]
     third = [a - b for a, b in zip(second, second[1:])]
+    third_twice = [t + t for t in third]
     curved = [(13.0 / 3.0) * (c * c) + 4.0 * EPS for c in second]
     fluxes = []
     for j in range(len(cells) - 4):
         left = twice[j + 1] + second[j]
         mid = first[j + 1] + first[j + 2]
         right = twice[j + 2] - second[j + 2]
-        e0 = curved[j] + left * left
-        e1 = curved[j + 1] + mid * mid
-        e2 = curved[j + 2] + right * right
-        e0 = 3.0 * (e0 * e0)
-        e1 = e1 * e1
-        e2 = e2 * e2
-        e2_twice = e2 + e2
-        top = e1 * (e2_twice * third[j] + e0 * third[j + 1])
-        inverse = pl.reciprocal(e1 * (e2 + e0) + e0 * e2_twice, approx=True)
+        w0 = pl.reciprocal(curved[j] + left * left, approx=True)
+        w1 = pl.reciprocal(curved[j + 1] + mid * mid, approx=True)
+        w2 = pl.reciprocal(curved[j + 2] + right * right, approx=True)
+        w0 = w0 * w0
+        w1 = 6.0 * (w1 * w1)
+        w2 = 3.0 * (w2 * w2)
+        top = w0 * third_twice[j] + w2 * third[j + 1]
+        inverse = pl.reciprocal(w0 + w1 + w2, approx=True)
         estimate = 6.0 * cells[j + 2] + (first[j + 1] + twice[j + 2]) + top * inverse
         fluxes.append((winds[j] + winds[j + 1]) * estimate)
     return fluxes
@@ -613,20 +613,20 @@
 def breakup_rows(mass, pairs_ref, lost_ref, products):
     bins = LANES // 2
     count = mass.shape[0]
-    lanes = lane_ids()
     rounded = mass.astype(jnp.bfloat16)
-    wide = rounded.astype(F32)
+    tiles = [rounded[r : r + 2 * ROWS] for r in range(0, count, 2 * ROWS)]
+    place = lax.broadcasted_iota(jnp.int32, (2 * ROWS, LANES), 1) % bins
     gained = None
     shifts = bins // 2 + 1
     for begin in range(0, shifts, 4):
         end = min(begin + 4, shifts)
         for d in range(begin, end):
-            ids = lanes // bins * bins + (lanes + d) % bins
-            for r in range(0, count, 2 * ROWS):
-                halves = [wide[r + ROWS * k : r + ROWS * (k + 1)] for k in range(2)]
-                halves = [v * pick(v, ids) if d else v * v for v in halves]
-                both = jnp.concatenate(halves, axis=0).astype(jnp.bfloat16)
-                products[pl.ds(r, 2 * ROWS), d * LANES : (d + 1) * LANES] = both
+            near = jnp.where(place < bins - d, 1.0, 0.0).astype(jnp.bfloat16) > 0
+            for k, tile in enumerate(tiles):
+                other = tile
+                if d:
+                    other = jnp.where(near, pltpu.roll(tile, LANES - d, 1), pltpu.roll(tile, bins - d, 1))
+                products[pl.ds(2 * ROWS * k, 2 * ROWS), d * LANES : (d + 1) * LANES] = tile * other
         part = jnp.dot(
             products[pl.ds(0, count), begin * LANES : end * LANES],
             pairs_ref[pl.ds(begin * LANES, (end - begin) * LANES)],

time: 30.9 us -> 31.7 us (1.026)
  Pallas kernels: 12.4 us -> 13.4 us
    pallas_call x13, Pallas kernels: 12.4 us -> 13.4 us  [call(): pl.pallas_call(kernel, out_shape=outs, in_specs=[VMEM] * len(args), out_s...]
  transfers between devices with their start and end apart: 10 -> 10, of which waited for: 4 -> 3; matrix products, arithmetic and copies ran while one was open for 2% -> 2% of each run, Pallas kernels for 27% -> 28%
where the time goes in v3:
time: 31.7 us; the launch traced here: 31.5 us
  Pallas kernels  13.4 us (42%)
  starting transfers between devices  10.7 us (34%)
  waiting for transfers between devices  5.06 us (16%)
  local copies, waits for them, and re-layouts  1.54 us (5%)
  between operations  0.81 us (3%)
    pallas_call x13, Pallas kernels, call(): pl.pallas_call(kernel, out_shape=outs, in_specs=[VMEM] * len(args), out_s...  13.4 us
    ppermute x6, starting transfers between devices, swap_neighbours(): return lax.ppermute(message, axes, pairs)  4.95 us
    ppermute x1, starting transfers between devices, per_device(): got = lax.ppermute(send, 'gz', [(0, 1), (1, 0)])  3.03 us
    ppermute x6, waiting for transfers between devices, swap_neighbours(): return lax.ppermute(message, axes, pairs)  1.94 us
    ppermute x1, waiting for transfers between devices, per_device(): early_got = lax.ppermute(early[0], 'gz', [(0, 1), (1, 0)])  1.81 us
    ppermute x1, starting transfers between devices, per_device(): early_got = lax.ppermute(early[0], 'gz', [(0, 1), (1, 0)])  1.58 us
    unnamed x13, local copies, waits for them, and re-layouts  1.54 us
    ppermute x1, waiting for transfers between devices, per_device(): got_wind = lax.ppermute(own_wind, 'gz', [(0, 1), (1, 0)])  1.31 us
  transfers between devices with their start and end apart: 10, of which 3 were waited for; matrix products, arithmetic and copies ran while one was open for 2% of the time, Pallas kernels for 28%

profile of v3, /device:TPU:0, one launch (start us, length us, event | category | flops | bytes accessed | tf_op | source)
XLA Modules:
  0.0 31.5 jit_solution(8282474580796962658)
XLA Ops:
  0.6 0.0 copy-start.1
  0.6 1.0 %copy-done.1 = f32[8,8,16,64]{3,2,1,0:T(8,128)S(1)} copy-done((f32[8,8,16,64]{3,2,1,0:T(8,128)S(1)}, f32[8,8,16,64]{3,2,1,0:T(8,128)}, u32[]{:S(2)}) %copy-start.1) | copy-done | bytes 262168
  1.7 0.0 copy-start.2
  1.7 0.0 copy-start.5
  1.7 0.3 shard_map.77
  2.0 0.0 copy-start
  2.0 3.0 %collective-permute-start = (f32[256,128]{1,0:T(8,128)S(1)}, f32[256,128]{1,0:T(8,128)S(1)}, u32[]{:S(2)}, u32[]{:S(2)}) collective-permute-start(f32[256,128]{1,0:T(8,128)S(1)} %get-tuple-element.38), channel_id=1, source_target_pairs={{0,1},{1,0},{2,3},{3,2},{4,5},{5,4},{6,7},{7,6},{8,9},{9,8},{10,11... | collective-permute-start | bytes 393224 | tf_op jit(solution)/shard_map/ppermute | solution.py:766
  5.0 0.0 copy-done.2
  5.0 0.1 shard_map.78.own_wind_ref
  5.1 0.6 %collective-permute-start.1 = (f32[24,128]{1,0:T(8,128)S(1)}, f32[24,128]{1,0:T(8,128)S(1)}, u32[]{:S(2)}, u32[]{:S(2)}) collective-permute-start(f32[24,128]{1,0:T(8,128)S(1)} %shard_map.78.own_wind_ref), channel_id=1, source_target_pairs={{0,1},{1,0},{2,3},{3,2},{4,5},{5,4},{6,7},{7,6},{8,9},{9,8},{10,11... | collective-permute-start | bytes 36872 | tf_op jit(solution)/shard_map/ppermute | solution.py:768
  5.7 0.0 copy-done.5
  5.7 0.5 %copy.8.gain_ref = bf16[4096,64]{1,0:T(8,128)(2,1)S(1)} copy(bf16[4096,64]{0,1:T(8,128)(2,1)S(1)} %copy-done.5) | data formatting | bytes 1048576 | tf_op args[4]
  6.2 0.0 copy-done
  6.2 1.4 %shard_map.79 = (bf16[4224,128]{1,0:T(8,128)(2,1)S(1)}, bf16[128,128]{1,0:T(8,128)(2,1)S(1)}) custom-call(bf16[4096,64]{1,0:T(8,128)(2,1)S(1)} %copy.8.gain_ref, bf16[64,64]{1,0:T(8,128)(2,1)S(1)} %copy-done), custom_call_target="tpu_custom_call" | custom-call | flops 22000000 | bytes 72000 | tf_op jit(solution)/shard_map/pallas_call | solution.py:710
  7.5 1.3 %collective-permute-done.1.got_wind_ref = f32[24,128]{1,0:T(8,128)S(1)} collective-permute-done((f32[24,128]{1,0:T(8,128)S(1)}, f32[24,128]{1,0:T(8,128)S(1)}, u32[]{:S(2)}, u32[]{:S(2)}) %collective-permute-start.1) | collective-permute-done | bytes 12320 | tf_op jit(solution)/shard_map/ppermute | solution.py:768
  8.9 0.0 collective-permute-done.got_ref
  8.9 0.2 shard_map.80
  9.1 1.8 %collective-permute-start.2 = (f32[432,128]{1,0:T(8,128)S(1)}, f32[432,128]{1,0:T(8,128)S(1)}, u32[]{:S(2)}, u32[]{:S(2)}) collective-permute-start(f32[432,128]{1,0:T(8,128)S(1)} %get-tuple-element.41), channel_id=1, source_target_pairs={{0,2},{1,3},{2,0},{3,1},{4,6},{5,7},{6,4},{7,5},{8,10},{9,11},{10,... | collective-permute-start | bytes 663560 | tf_op jit(solution)/shard_map/ppermute | solution.py:740
  10.8 0.0 collective-permute-start.3
  10.9 1.5 %collective-permute-start.4 = (f32[408,128]{1,0:T(8,128)S(1)}, f32[408,128]{1,0:T(8,128)S(1)}, u32[]{:S(2)}, u32[]{:S(2)}) collective-permute-start(f32[408,128]{1,0:T(8,128)S(1)} %get-tuple-element.56), channel_id=1, source_target_pairs={{0,1},{1,0},{2,3},{3,2},{4,5},{5,4},{6,7},{7,6},{8,16},{9,17},{10,... | collective-permute-start | bytes 626696 | tf_op jit(solution)/shard_map/ppermute | solution.py:740
  12.4 0.1 collective-permute-start.5
  12.5 1.3 %shard_map.81 = (f32[512,128]{1,0:T(8,128)S(1)}, f32[512,128]{1,0:T(8,128)S(1)}, f32[512,128]{1,0:T(8,128)S(1)}, f32[512,128]{1,0:T(8,128)S(1)}, f32[128,128]{1,0:T(8,128)S(1)}, /*index=5*/f32[128,128]{1,0:T(8,128)S(1)}) custom-call(f32[560,128]{1,0:T(8,128)S(1)} %get-tuple-element.40.block_ref), custom_call_target="tpu_custom_call" | custom-call | flops 1760000000 | bytes 5760000 | tf_op jit(solution)/shard_map/pallas_call | solution.py:710
  13.7 1.9 %collective-permute-done.2.first_ref = f32[432,128]{1,0:T(8,128)S(1)} collective-permute-done((f32[432,128]{1,0:T(8,128)S(1)}, f32[432,128]{1,0:T(8,128)S(1)}, u32[]{:S(2)}, u32[]{:S(2)}) %collective-permute-start.2) | collective-permute-done | bytes 221216 | tf_op jit(solution)/shard_map/ppermute | solution.py:740
  15.7 0.0 collective-permute-done.3.second_ref
  15.7 1.5 %collective-permute-start.6 = (f32[152,128]{1,0:T(8,128)S(1)}, f32[152,128]{1,0:T(8,128)S(1)}, u32[]{:S(2)}, u32[]{:S(2)}) collective-permute-start(f32[152,128]{1,0:T(8,128)S(1)} %get-tuple-element.62), channel_id=1, source_target_pairs={{0,1},{1,0},{2,3},{3,2},{4,5},{5,4},{6,7},{7,6},{8,16},{9,17},{10,... | collective-permute-start | bytes 233480 | tf_op jit(solution)/shard_map/ppermute | solution.py:740
  17.2 0.1 collective-permute-start.7
  17.3 1.2 %shard_map.82 = (f32[1152,128]{1,0:T(8,128)S(1)}, f32[832,128]{1,0:T(8,128)S(1)}, f32[320,128]{1,0:T(8,128)S(1)}, f32[448,128]{1,0:T(8,128)S(1)}) custom-call(f32[560,128]{1,0:T(8,128)S(1)} %get-tuple-element.40.block_ref, f32[432,128]{1,0:T(8,128)S(1)} %collective-permute-done.2.first_ref, f32[432,128]{1,0:T(8,128)S(1)} %collective-permute-done.3.second_ref, ...), custom_call_target="tpu_custom_call" | custom-call | flops 2200000000 | bytes 7200000 | tf_op jit(solution)/shard_map/pallas_call | solution.py:710
  18.5 0.5 %shard_map.83 = (f32[312,128]{1,0:T(8,128)S(1)}, f32[208,128]{1,0:T(8,128)S(1)}, f32[192,128]{1,0:T(8,128)S(1)}) custom-call(f32[1152,128]{1,0:T(8,128)S(1)} %get-tuple-element.46.cell.refs_0_, f32[832,128]{1,0:T(8,128)S(1)} %get-tuple-element.47.change.refs_1_, f32[320,128]{1,0:T(8,128)S(1)} %get-tuple-element.50.halo_wind_x.refs_5_, ...), custom_call_target="tpu_custom_call" | custom-call | flops 990000000 | bytes 3240000 | tf_op jit(solution)/shard_map/pallas_call | solution.py:710
  18.9 0.0 collective-permute-done.4.second_ref
  18.9 0.0 collective-permute-done.5.first_ref
  19.0 0.0 copy-start.3
  19.0 0.0 copy-start.4
  19.0 1.2 %shard_map.84 = (f32[832,128]{1,0:T(8,128)S(1)}, f32[448,128]{1,0:T(8,128)S(1)}, f32[320,128]{1,0:T(8,128)S(1)}, f32[320,128]{1,0:T(8,128)S(1)}) custom-call(f32[1152,128]{1,0:T(8,128)S(1)} %get-tuple-element.46.cell.refs_0_, f32[832,128]{1,0:T(8,128)S(1)} %get-tuple-element.47.change.refs_1_, f32[512,128]{1,0:T(8,128)S(1)} %get-tuple-element.48.wind_x.refs_2_, ...), custom_call_target="tpu_custom_call" | custom-call | flops 1870000000 | bytes 6120000 | tf_op jit(solution)/shard_map/pallas_call | solution.py:710
  20.2 0.0 collective-permute-done.6.refs_14_
  20.2 0.0 collective-permute-done.7.refs_15_
  20.2 0.0 copy-done.3
  20.2 0.0 copy-done.4
  20.2 2.0 %shard_map.86 = (f32[1352,128]{1,0:T(8,128)S(1)}, f32[176,128]{1,0:T(8,128)S(1)}, f32[176,128]{1,0:T(8,128)S(1)}) custom-call(f32[1152,128]{1,0:T(8,128)S(1)} %get-tuple-element.46.cell.refs_0_, f32[832,128]{1,0:T(8,128)S(1)} %get-tuple-element.47.change.refs_1_, f32[512,128]{1,0:T(8,128)S(1)} %get-tuple-element.48.wind_x.refs_2_, ...), custom_call_target="tpu_custom_call" | custom-call | flops 2860000000 | bytes 9360000 | tf_op jit(solution)/shard_map/pallas_call | solution.py:710
  22.3 1.6 %collective-permute-start.9 = (f32[176,128]{1,0:T(8,128)S(1)}, f32[176,128]{1,0:T(8,128)S(1)}, u32[]{:S(2)}, u32[]{:S(2)}) collective-permute-start(f32[176,128]{1,0:T(8,128)S(1)} %get-tuple-element.69), channel_id=1, source_target_pairs={{0,1},{1,0},{2,3},{3,2},{4,5},{5,4},{6,7},{7,6},{8,9},{9,8},{10,11... | collective-permute-start | bytes 270344 | tf_op jit(solution)/shard_map/ppermute | solution.py:842
  23.8 1.1 %shard_map.87 = (f32[104,128]{1,0:T(8,128)S(1)}, f32[104,128]{1,0:T(8,128)S(1)}) custom-call(f32[1352,128]{1,0:T(8,128)S(1)} %get-tuple-element.64.one, f32[1152,128]{1,0:T(8,128)S(1)} %get-tuple-element.46.cell.refs_0_, f32[512,128]{1,0:T(8,128)S(1)} %get-tuple-element.48.wind_x.refs_2_, f32[448,128]{1,0:T(8,128)S(1)} %get-tuple-element.59.refs_11_.far_wind_x, ...), custom_call_target="tpu_custom_call" | custom-call | flops 770000000 | bytes 2520000 | tf_op jit(solution)/shard_map/pallas_call | solution.py:710
  24.9 0.6 %collective-permute-start.8 = (f32[104,128]{1,0:T(8,128)S(1)}, f32[104,128]{1,0:T(8,128)S(1)}, u32[]{:S(2)}, u32[]{:S(2)}) collective-permute-start(f32[104,128]{1,0:T(8,128)S(1)} %get-tuple-element.66), channel_id=1, source_target_pairs={{0,1},{1,0},{2,3},{3,2},{4,5},{5,4},{6,7},{7,6},{8,9},{9,8},{10,11... | collective-permute-start | bytes 159752 | tf_op jit(solution)/shard_map/ppermute | solution.py:855
  25.5 1.8 %collective-permute-done.9.got_ref = f32[176,128]{1,0:T(8,128)S(1)} collective-permute-done((f32[176,128]{1,0:T(8,128)S(1)}, f32[176,128]{1,0:T(8,128)S(1)}, u32[]{:S(2)}, u32[]{:S(2)}) %collective-permute-start.9) | collective-permute-done | bytes 90144 | tf_op jit(solution)/shard_map/ppermute | solution.py:842
  27.3 2.1 %shard_map.88 = (f32[5,8,16,64]{3,2,1,0:T(8,128)S(1)}, f32[5,4,64]{2,1,0:T(4,128)S(1)}) custom-call(f32[176,128]{1,0:T(8,128)S(1)} %get-tuple-element.68.keep_ref, f32[176,128]{1,0:T(8,128)S(1)} %collective-permute-done.9.got_ref, bf16[4224,128]{1,0:T(8,128)(2,1)S(1)} %get-tuple-element.67.pairs_ref, bf16[128,128]{1,0:T(8,128)(2,1)S(1)} %get-tuple-element.39.lost_ref), custom_call_target="tpu_custom_call" | custom-call | flops 1980000000 | bytes 6480000 | tf_op jit(solution)/shard_map/pallas_call | solution.py:710
  29.4 0.0 collective-permute-done.8.got_ref
  29.4 2.1 %shard_map.89 = (f32[8,8,16,64]{3,2,1,0:T(8,128)}, f32[8,4,64]{2,1,0:T(4,128)}) custom-call(f32[104,128]{1,0:T(8,128)S(1)} %get-tuple-element.65.keep_ref, f32[104,128]{1,0:T(8,128)S(1)} %collective-permute-done.8.got_ref, bf16[4224,128]{1,0:T(8,128)(2,1)S(1)} %get-tuple-element.67.pairs_ref, bf16[128,128]{1,0:T(8,128)(2,1)S(1)} %get-tuple-element.39.lost_ref, ...), custom_call_target="tpu_custom_call" | custom-call | flops 1320000000 | bytes 4320000 | tf_op jit(solution)/shard_map/pallas_call | solution.py:710
  (1 shorter events, 0.0 us)
Async XLA Ops:
  0.6 1.0 %copy-start.1 = (f32[8,8,16,64]{3,2,1,0:T(8,128)S(1)}, f32[8,8,16,64]{3,2,1,0:T(8,128)}, u32[]{:S(2)}) copy-start(f32[8,8,16,64]{3,2,1,0:T(8,128)} %mass_ref.1) | copy-start | bytes 786436
  1.7 3.3 %copy-start.2 = (f32[3,8,8,16]{3,2,1,0:T(8,128)S(1)}, f32[3,8,8,16]{3,2,1,0:T(8,128)}, u32[]{:S(2)}) copy-start(f32[3,8,8,16]{3,2,1,0:T(8,128)} %wind_ref.1) | copy-start | bytes 36868
  1.7 4.0 %copy-start.5 = (bf16[4096,64]{0,1:T(8,128)(2,1)S(1)}, bf16[4096,64]{0,1:T(8,128)(2,1)}, u32[]{:S(2)}) copy-start(bf16[4096,64]{0,1:T(8,128)(2,1)} %param.10) | copy-start | bytes 1572868
  2.0 4.2 %copy-start = (bf16[64,64]{1,0:T(8,128)(2,1)S(1)}, bf16[64,64]{1,0:T(8,128)(2,1)}, u32[]{:S(2)}) copy-start(bf16[64,64]{1,0:T(8,128)(2,1)} %loss_ref.1) | copy-start | bytes 24580
  2.0 6.9 %collective-permute-start = (f32[256,128]{1,0:T(8,128)S(1)}, f32[256,128]{1,0:T(8,128)S(1)}, u32[]{:S(2)}, u32[]{:S(2)}) collective-permute-start(f32[256,128]{1,0:T(8,128)S(1)} %get-tuple-element.38), channel_id=1, source_target_pairs={{0,1},{1,0},{2,3},{3,2},{4,5},{5,4},{6,7},{7,6},{8,9},{9,8},{10,11... | collective-permute-start | bytes 393224 | tf_op jit(solution)/shard_map/ppermute | solution.py:766
  5.1 3.7 %collective-permute-start.1 = (f32[24,128]{1,0:T(8,128)S(1)}, f32[24,128]{1,0:T(8,128)S(1)}, u32[]{:S(2)}, u32[]{:S(2)}) collective-permute-start(f32[24,128]{1,0:T(8,128)S(1)} %shard_map.78.own_wind_ref), channel_id=1, source_target_pairs={{0,1},{1,0},{2,3},{3,2},{4,5},{5,4},{6,7},{7,6},{8,9},{9,8},{10,11... | collective-permute-start | bytes 36872 | tf_op jit(solution)/shard_map/ppermute | solution.py:768
  9.1 6.6 %collective-permute-start.2 = (f32[432,128]{1,0:T(8,128)S(1)}, f32[432,128]{1,0:T(8,128)S(1)}, u32[]{:S(2)}, u32[]{:S(2)}) collective-permute-start(f32[432,128]{1,0:T(8,128)S(1)} %get-tuple-element.41), channel_id=1, source_target_pairs={{0,2},{1,3},{2,0},{3,1},{4,6},{5,7},{6,4},{7,5},{8,10},{9,11},{10,... | collective-permute-start | bytes 663560 | tf_op jit(solution)/shard_map/ppermute | solution.py:740
  10.8 4.8 %collective-permute-start.3 = (f32[432,128]{1,0:T(8,128)S(1)}, f32[432,128]{1,0:T(8,128)S(1)}, u32[]{:S(2)}, u32[]{:S(2)}) collective-permute-start(f32[432,128]{1,0:T(8,128)S(1)} %get-tuple-element.42), channel_id=1, source_target_pairs={{0,8},{1,9},{2,4},{3,5},{4,2},{5,3},{6,14},{7,15},{8,0},{9,1},{10,... | collective-permute-start | bytes 663560 | tf_op jit(solution)/shard_map/ppermute | solution.py:740
  10.9 8.1 %collective-permute-start.4 = (f32[408,128]{1,0:T(8,128)S(1)}, f32[408,128]{1,0:T(8,128)S(1)}, u32[]{:S(2)}, u32[]{:S(2)}) collective-permute-start(f32[408,128]{1,0:T(8,128)S(1)} %get-tuple-element.56), channel_id=1, source_target_pairs={{0,1},{1,0},{2,3},{3,2},{4,5},{5,4},{6,7},{7,6},{8,16},{9,17},{10,... | collective-permute-start | bytes 626696 | tf_op jit(solution)/shard_map/ppermute | solution.py:740
  12.4 6.6 %collective-permute-start.5 = (f32[408,128]{1,0:T(8,128)S(1)}, f32[408,128]{1,0:T(8,128)S(1)}, u32[]{:S(2)}, u32[]{:S(2)}) collective-permute-start(f32[408,128]{1,0:T(8,128)S(1)} %get-tuple-element.57), channel_id=1, source_target_pairs={{0,8},{1,9},{2,10},{3,11},{4,12},{5,13},{6,14},{7,15},{8,0},{9,1},... | collective-permute-start | bytes 626696 | tf_op jit(solution)/shard_map/ppermute | solution.py:740
  15.7 4.5 %collective-permute-start.6 = (f32[152,128]{1,0:T(8,128)S(1)}, f32[152,128]{1,0:T(8,128)S(1)}, u32[]{:S(2)}, u32[]{:S(2)}) collective-permute-start(f32[152,128]{1,0:T(8,128)S(1)} %get-tuple-element.62), channel_id=1, source_target_pairs={{0,1},{1,0},{2,3},{3,2},{4,5},{5,4},{6,7},{7,6},{8,16},{9,17},{10,... | collective-permute-start | bytes 233480 | tf_op jit(solution)/shard_map/ppermute | solution.py:740
  17.2 3.0 %collective-permute-start.7 = (f32[152,128]{1,0:T(8,128)S(1)}, f32[152,128]{1,0:T(8,128)S(1)}, u32[]{:S(2)}, u32[]{:S(2)}) collective-permute-start(f32[152,128]{1,0:T(8,128)S(1)} %get-tuple-element.63), channel_id=1, source_target_pairs={{0,8},{1,9},{2,10},{3,11},{4,12},{5,13},{6,14},{7,15},{8,0},{9,1},... | collective-permute-start | bytes 233480 | tf_op jit(solution)/shard_map/ppermute | solution.py:740
  19.0 1.2 %copy-start.3 = (f32[64]{0:T(128)S(1)}, f32[64]{0:T(128)}, u32[]{:S(2)}) copy-start(f32[64]{0:T(128)} %param.8) | copy-start | bytes 772
  19.0 1.2 %copy-start.4 = (s32[64]{0:T(128)S(1)}, s32[64]{0:T(128)}, u32[]{:S(2)}) copy-start(s32[64]{0:T(128)} %param.9) | copy-start | bytes 772
  22.3 5.0 %collective-permute-start.9 = (f32[176,128]{1,0:T(8,128)S(1)}, f32[176,128]{1,0:T(8,128)S(1)}, u32[]{:S(2)}, u32[]{:S(2)}) collective-permute-start(f32[176,128]{1,0:T(8,128)S(1)} %get-tuple-element.69), channel_id=1, source_target_pairs={{0,1},{1,0},{2,3},{3,2},{4,5},{5,4},{6,7},{7,6},{8,9},{9,8},{10,11... | collective-permute-start | bytes 270344 | tf_op jit(solution)/shard_map/ppermute | solution.py:842
  24.9 4.5 %collective-permute-start.8 = (f32[104,128]{1,0:T(8,128)S(1)}, f32[104,128]{1,0:T(8,128)S(1)}, u32[]{:S(2)}, u32[]{:S(2)}) collective-permute-start(f32[104,128]{1,0:T(8,128)S(1)} %get-tuple-element.66), channel_id=1, source_target_pairs={{0,1},{1,0},{2,3},{3,2},{4,5},{5,4},{6,7},{7,6},{8,9},{9,8},{10,11... | collective-permute-start | bytes 159752 | tf_op jit(solution)/shard_map/ppermute | solution.py:855

commit v4 on v2

--- a/solution.py
+++ b/solution.py
@@ -60,20 +60,36 @@
 
 
 def spread(jobs, parts):
-    width, deep, _ = groups(parts)
+    width = groups(parts)[0]
     place = lane_ids() % width
     rows = [[], []]
-    for tile, x, y, _, _ in jobs:
+    for tile, lane, _, _ in jobs:
         top = tile.astype(jnp.bfloat16).astype(F32)
-        here = place == x % deep * ROWS + y
+        here = place == lane
         for out, term in zip(rows, (top, tile - top)):
             out.append(jnp.where(here, term, 0.0))
     terms = jnp.concatenate([jnp.concatenate(r, axis=0).astype(jnp.bfloat16) for r in rows], axis=1)
     source, target = [lax.broadcasted_iota(jnp.int32, (2 * LANES, LANES), k) for k in range(2)]
     same = jnp.where(source % LANES // width == target // width, 1.0, 0.0).astype(jnp.bfloat16)
     out = jnp.dot(terms, same, preferred_element_type=F32)
-    for k, (_, _, _, ref, at) in enumerate(jobs):
+    for k, (_, _, ref, at) in enumerate(jobs):
         ref[rows_of(at)] = out[k * ROWS : (k + 1) * ROWS]
+
+
+def lane_of(x, y, parts):
+    return x % groups(parts)[1] * ROWS + y
+
+
+def half_lane_of(x, y, parts):
+    _, deep, tiles = groups(parts)
+    return x % deep * ROWS + x // deep // (tiles // 2) * (ROWS // 2) + y % (ROWS // 2)
+
+
+def half_tiles(low, high, upper):
+    near = lane_ids() % ROWS < ROWS // 2
+    if upper:
+        return jnp.where(near, turn(low, -(ROWS // 2)), high)
+    return jnp.where(near, low, turn(high, ROWS // 2))
 
 
 def each(count, together, body):
@@ -214,7 +230,9 @@
         for ref, start, wide in (((y_first, y_second)[up], n - PAD_LO, PAD_LO), ((y_first, y_second)[down], 0, PAD_HI)):
             for x in range(n):
                 ref[rows_of(x * wide, wide)] = block_ref[rows_of(x * n + start, wide)]
-            ref[rows_of(n * wide, 6)] = block_ref[rows_of(n * n, 6)]
+            for d in range(3):
+                low, high = [block_ref[rows_of(n * n + 2 * d + k)] for k in range(2)]
+                ref[rows_of(n * wide + d)] = half_tiles(low, high, wide == PAD_LO)
 
     def along_x(up, down):
         for ref, start, wide, part in (((x_first, x_second)[up], n - PAD_LO, PAD_LO, 1), ((x_first, x_second)[down], 0, PAD_HI, 0)):
@@ -240,8 +258,8 @@
                 ref[rows_of(at + LO, HI)] = above(rows_of(x * PAD_HI, HI))
                 at += LINES
             for side, base in ((below, n * PAD_LO), (above, n * PAD_HI)):
-                ref[rows_of(at)] = side(rows_of(base + (tiles - 1 if part else 0)))
-                ref[rows_of(at + 1, half)] = side(rows_of(base + tiles + part, half))
+                ref[rows_of(at)] = side(rows_of(base + (half - 1 if part else 0)))
+                ref[rows_of(at + 1, half)] = side(rows_of(base + half, half))
                 at += 1 + half
 
     by_parity("gx", body)
@@ -253,7 +271,7 @@
         jobs = []
         for x in range(n):
             tile = block_ref[rows_of(n * n + d * tiles + x // deep)]
-            jobs += [(tile, x, y, out, x * n + y) for y in range(n)]
+            jobs += [(tile, lane_of(x, y, parts), out, x * n + y) for y in range(n)]
         spread(jobs, parts)
 
     def along_z(x):
@@ -286,17 +304,19 @@
         cell[rows_of(x * span + PAD_LO, n)] = block_ref[rows_of(x * n, n)]
         cell[rows_of(x * span + PAD_LO + n, PAD_HI)] = above(rows_of(x * PAD_HI, PAD_HI))
     jobs = []
+    half = tiles // 2
     for d in range(3):
-        for t in range(tiles):
-            low, high = below(rows_of(n * PAD_LO + d * tiles + t)), above(rows_of(n * PAD_HI + d * tiles + t))
-            for x in range(t * deep, (t + 1) * deep):
+        for t in range(half):
+            low, high = below(rows_of(n * PAD_LO + d * half + t)), above(rows_of(n * PAD_HI + d * half + t))
+            for x in [x for x in range(n) if x // deep % half == t]:
+                lanes = [half_lane_of(x, y, parts) for y in range(n)]
                 if d == 1:
-                    jobs += [(low, x, n - LO - 1 + y, far_y, x * (LINES + 2) + y) for y in range(LO + 1)]
-                    jobs += [(high, x, y, far_y, x * (LINES + 2) + LO + 1 + y) for y in range(HI + 1)]
+                    jobs += [(low, lanes[n - LO - 1 + y], far_y, x * (LINES + 2) + y) for y in range(LO + 1)]
+                    jobs += [(high, lanes[y], far_y, x * (LINES + 2) + LO + 1 + y) for y in range(HI + 1)]
                 else:
                     out = wind_z if d else wind_x
-                    jobs += [(low, x, n - LO + y, out, y * n + x) for y in range(LO)]
-                    jobs += [(high, x, y, out, (LO + y) * n + x) for y in range(HI)]
+                    jobs += [(low, lanes[n - LO + y], out, y * n + x) for y in range(LO)]
+                    jobs += [(high, lanes[y], out, (LO + y) * n + x) for y in range(HI)]
     spread(jobs, parts)
 
     def along_z(i):
@@ -404,10 +424,10 @@
             return take(rows_of(wide * n + d * half + x // deep - shift))
 
         for i, x in enumerate(wider):
-            jobs += [(winds_of(0, x), x, y, far_wind_x, (line + bool(line) + i) * n + y) for y in range(n)]
+            jobs += [(winds_of(0, x), lane_of(x, y, parts), far_wind_x, (line + bool(line) + i) * n + y) for y in range(n)]
         for d, out in ((1, side_wind_y), (2, side_wind_z)):
             for i, x in enumerate(layers):
-                jobs += [(winds_of(d, x), x, y, out, (line + i) * n + y) for y in range(n)]
+                jobs += [(winds_of(d, x), lane_of(x, y, parts), out, (line + i) * n + y) for y in range(n)]
     spread(jobs, parts)
 
     def along_z(i):
@@ -450,15 +470,17 @@
         at = narrow * LINES
         corner[rows_of(line * LINES, at)] = take(rows_of(0, at))
         below, above = at, at + 1 + half
-        layers, shift = (range(n - narrow, n), half) if line == 0 else (range(narrow), 0)
+        layers = range(n - narrow, n) if line == 0 else range(narrow)
         for y in range(LINES):
             tile = take(rows_of(below if y < LO else above))
             x = layers[-1] if line == 0 else layers[0]
-            jobs.append((tile, x, n - LO + y if y < LO else y - LO, corner_wind_x, bool(line) * LINES + y))
+            lane = half_lane_of(x, n - LO + y if y < LO else y - LO, parts)
+            jobs.append((tile, lane, corner_wind_x, bool(line) * LINES + y))
         for i, x in enumerate(layers):
-            tile = x // deep - shift
-            jobs.append((take(rows_of(below + 1 + tile)), x, n - 1, edge_wind_y, 2 * (line + i)))
-            jobs.append((take(rows_of(above + 1 + tile)), x, 0, edge_wind_y, 2 * (line + i) + 1))
+            tile = x // deep % half
+            for k, (base, y) in enumerate(((below, n - 1), (above, 0))):
+                lane = half_lane_of(x, y, parts)
+                jobs.append((take(rows_of(base + 1 + tile)), lane, edge_wind_y, 2 * (line + i) + k))
     spread(jobs, parts)
 
     west_in, east_in = inside("gx")
@@ -547,7 +569,7 @@
     ]
 
     rain = []
-    for some in [range(i, min(i + 3, count)) for i in range(0, count, 3)]:
+    for some in [range(count)]:
         columns = [[fallen[eight(i * n, k)] for k in range(ROWS)] for i in some]
         drops = [jnp.zeros((ROWS, LANES), F32) for _ in some]
         for block in range(SUBS // AHEAD):
@@ -758,7 +780,7 @@
         micros=0.02,
     )
 
-    y_message = tiles_of(n * PAD_LO + winds)
+    y_message = tiles_of(n * PAD_LO + winds // 2)
     x_message = tiles_of(n * PAD_LO + winds // 2)
     if parts == 2:
         half = tiles_of(n * n // 2)
@@ -780,10 +802,14 @@
         air = lax.all_gather(air, "gz").reshape(parts, 3, ROWS, nz // ROWS, tiles, nx // tiles, ny)
         air = air.transpose(1, 4, 2, 0, 3, 5, 6).reshape(3, tiles, ROWS, LANES)
         block = jnp.concatenate([cube.reshape(-1, LANES), air.reshape(-1, LANES)])
+        halves = [air[:, : tiles // 2], air[:, tiles // 2 :]]
+        near = jnp.arange(LANES) % ROWS < ROWS // 2
+        low_y = jnp.where(near, halves[0], jnp.roll(halves[1], ROWS // 2, axis=-1))
+        high_y = jnp.where(near, jnp.roll(halves[0], -(ROWS // 2), axis=-1), halves[1])
         messages = []
         for layers, low_air, high_air, message, even in (
-            (cube.transpose(1, 0, 2, 3), air, air, y_message, gy % 2 == 0),
-            (cube, air[:, : tiles // 2], air[:, tiles // 2 :], x_message, lax.axis_index("gx") % 2 == 0),
+            (cube.transpose(1, 0, 2, 3), low_y, high_y, y_message, gy % 2 == 0),
+            (cube, *halves, x_message, lax.axis_index("gx") % 2 == 0),
         ):
             up, down = layers[n - PAD_LO :], layers[:PAD_HI]
             if message is y_message:

time: 30.9 us -> 30.7 us (level)
  no operation moved by 1% of the time
where the time goes in v4:
time: 30.7 us; the launch traced here: 30.6 us
  Pallas kernels  12.5 us (41%)
  starting transfers between devices  10.7 us (35%)
  waiting for transfers between devices  5.09 us (17%)
  local copies, waits for them, and re-layouts  1.54 us (5%)
  between operations  0.77 us (3%)
    pallas_call x13, Pallas kernels, call(): pl.pallas_call(kernel, out_shape=outs, in_specs=[VMEM] * len(args), out_s...  12.5 us
    ppermute x6, starting transfers between devices, swap_neighbours(): return lax.ppermute(message, axes, pairs)  4.94 us
    ppermute x1, starting transfers between devices, per_device(): got = lax.ppermute(send, 'gz', [(0, 1), (1, 0)])  3.03 us
    ppermute x1, waiting for transfers between devices, per_device(): early_got = lax.ppermute(early[0], 'gz', [(0, 1), (1, 0)])  1.81 us
    ppermute x6, waiting for transfers between devices, swap_neighbours(): return lax.ppermute(message, axes, pairs)  1.73 us
    ppermute x1, starting transfers between devices, per_device(): early_got = lax.ppermute(early[0], 'gz', [(0, 1), (1, 0)])  1.57 us
    unnamed x13, local copies, waits for them, and re-layouts  1.54 us
    ppermute x1, waiting for transfers between devices, per_device(): got_wind = lax.ppermute(own_wind, 'gz', [(0, 1), (1, 0)])  1.31 us
  transfers between devices with their start and end apart: 10, of which 4 were waited for; matrix products, arithmetic and copies ran while one was open for 2% of the time, Pallas kernels for 27%

profile of v4, /device:TPU:0, one launch (start us, length us, event | category | flops | bytes accessed | tf_op | source)
XLA Modules:
  0.0 30.6 jit_solution(8723313294118575096)
XLA Ops:
  0.6 0.0 copy-start.1
  0.6 1.0 %copy-done.1 = f32[8,8,16,64]{3,2,1,0:T(8,128)S(1)} copy-done((f32[8,8,16,64]{3,2,1,0:T(8,128)S(1)}, f32[8,8,16,64]{3,2,1,0:T(8,128)}, u32[]{:S(2)}) %copy-start.1) | copy-done | bytes 262168
  1.7 0.0 copy-start.2
  1.7 0.0 copy-start.5
  1.7 0.3 shard_map.77
  2.0 0.0 copy-start
  2.0 3.0 %collective-permute-start = (f32[256,128]{1,0:T(8,128)S(1)}, f32[256,128]{1,0:T(8,128)S(1)}, u32[]{:S(2)}, u32[]{:S(2)}) collective-permute-start(f32[256,128]{1,0:T(8,128)S(1)} %get-tuple-element.38), channel_id=1, source_target_pairs={{0,1},{1,0},{2,3},{3,2},{4,5},{5,4},{6,7},{7,6},{8,9},{9,8},{10,11... | collective-permute-start | bytes 393224 | tf_op jit(solution)/shard_map/ppermute | solution.py:788
  5.0 0.0 copy-done.2
  5.0 0.1 shard_map.78.own_wind_ref
  5.1 0.6 %collective-permute-start.1 = (f32[24,128]{1,0:T(8,128)S(1)}, f32[24,128]{1,0:T(8,128)S(1)}, u32[]{:S(2)}, u32[]{:S(2)}) collective-permute-start(f32[24,128]{1,0:T(8,128)S(1)} %shard_map.78.own_wind_ref), channel_id=1, source_target_pairs={{0,1},{1,0},{2,3},{3,2},{4,5},{5,4},{6,7},{7,6},{8,9},{9,8},{10,11... | collective-permute-start | bytes 36872 | tf_op jit(solution)/shard_map/ppermute | solution.py:790
  5.7 0.0 copy-done.5
  5.7 0.5 %copy.8.gain_ref = bf16[4096,64]{1,0:T(8,128)(2,1)S(1)} copy(bf16[4096,64]{0,1:T(8,128)(2,1)S(1)} %copy-done.5) | data formatting | bytes 1048576 | tf_op args[4]
  6.2 0.0 copy-done
  6.2 1.4 %shard_map.79 = (bf16[4224,128]{1,0:T(8,128)(2,1)S(1)}, bf16[128,128]{1,0:T(8,128)(2,1)S(1)}) custom-call(bf16[4096,64]{1,0:T(8,128)(2,1)S(1)} %copy.8.gain_ref, bf16[64,64]{1,0:T(8,128)(2,1)S(1)} %copy-done), custom_call_target="tpu_custom_call" | custom-call | flops 22000000 | bytes 72000 | tf_op jit(solution)/shard_map/pallas_call | solution.py:732
  7.5 1.3 %collective-permute-done.1.got_wind_ref = f32[24,128]{1,0:T(8,128)S(1)} collective-permute-done((f32[24,128]{1,0:T(8,128)S(1)}, f32[24,128]{1,0:T(8,128)S(1)}, u32[]{:S(2)}, u32[]{:S(2)}) %collective-permute-start.1) | collective-permute-done | bytes 12320 | tf_op jit(solution)/shard_map/ppermute | solution.py:790
  8.9 0.0 collective-permute-done.got_ref
  8.9 0.3 shard_map.80
  9.1 1.8 %collective-permute-start.2 = (f32[408,128]{1,0:T(8,128)S(1)}, f32[408,128]{1,0:T(8,128)S(1)}, u32[]{:S(2)}, u32[]{:S(2)}) collective-permute-start(f32[408,128]{1,0:T(8,128)S(1)} %get-tuple-element.41), channel_id=1, source_target_pairs={{0,2},{1,3},{2,0},{3,1},{4,6},{5,7},{6,4},{7,5},{8,10},{9,11},{10,... | collective-permute-start | bytes 626696 | tf_op jit(solution)/shard_map/ppermute | solution.py:762
  10.9 0.0 collective-permute-start.3
  10.9 1.5 %collective-permute-start.4 = (f32[408,128]{1,0:T(8,128)S(1)}, f32[408,128]{1,0:T(8,128)S(1)}, u32[]{:S(2)}, u32[]{:S(2)}) collective-permute-start(f32[408,128]{1,0:T(8,128)S(1)} %get-tuple-element.56), channel_id=1, source_target_pairs={{0,1},{1,0},{2,3},{3,2},{4,5},{5,4},{6,7},{7,6},{8,16},{9,17},{10,... | collective-permute-start | bytes 626696 | tf_op jit(solution)/shard_map/ppermute | solution.py:762
  12.4 0.1 collective-permute-start.5
  12.5 1.3 %shard_map.81 = (f32[512,128]{1,0:T(8,128)S(1)}, f32[512,128]{1,0:T(8,128)S(1)}, f32[512,128]{1,0:T(8,128)S(1)}, f32[512,128]{1,0:T(8,128)S(1)}, f32[128,128]{1,0:T(8,128)S(1)}, /*index=5*/f32[128,128]{1,0:T(8,128)S(1)}) custom-call(f32[560,128]{1,0:T(8,128)S(1)} %get-tuple-element.40.block_ref), custom_call_target="tpu_custom_call" | custom-call | flops 1760000000 | bytes 5760000 | tf_op jit(solution)/shard_map/pallas_call | solution.py:732
  13.8 1.7 %collective-permute-done.2.first_ref = f32[408,128]{1,0:T(8,128)S(1)} collective-permute-done((f32[408,128]{1,0:T(8,128)S(1)}, f32[408,128]{1,0:T(8,128)S(1)}, u32[]{:S(2)}, u32[]{:S(2)}) %collective-permute-start.2) | collective-permute-done | bytes 208928 | tf_op jit(solution)/shard_map/ppermute | solution.py:762
  15.4 0.0 collective-permute-done.3.second_ref
  15.5 1.5 %collective-permute-start.6 = (f32[152,128]{1,0:T(8,128)S(1)}, f32[152,128]{1,0:T(8,128)S(1)}, u32[]{:S(2)}, u32[]{:S(2)}) collective-permute-start(f32[152,128]{1,0:T(8,128)S(1)} %get-tuple-element.62), channel_id=1, source_target_pairs={{0,1},{1,0},{2,3},{3,2},{4,5},{5,4},{6,7},{7,6},{8,16},{9,17},{10,... | collective-permute-start | bytes 233480 | tf_op jit(solution)/shard_map/ppermute | solution.py:762
  17.0 0.1 collective-permute-start.7
  17.1 1.2 %shard_map.82 = (f32[1152,128]{1,0:T(8,128)S(1)}, f32[832,128]{1,0:T(8,128)S(1)}, f32[320,128]{1,0:T(8,128)S(1)}, f32[448,128]{1,0:T(8,128)S(1)}) custom-call(f32[560,128]{1,0:T(8,128)S(1)} %get-tuple-element.40.block_ref, f32[408,128]{1,0:T(8,128)S(1)} %collective-permute-done.2.first_ref, f32[408,128]{1,0:T(8,128)S(1)} %collective-permute-done.3.second_ref, ...), custom_call_target="tpu_custom_call" | custom-call | flops 2200000000 | bytes 7200000 | tf_op jit(solution)/shard_map/pallas_call | solution.py:732
  18.2 0.5 %shard_map.83 = (f32[312,128]{1,0:T(8,128)S(1)}, f32[208,128]{1,0:T(8,128)S(1)}, f32[192,128]{1,0:T(8,128)S(1)}) custom-call(f32[1152,128]{1,0:T(8,128)S(1)} %get-tuple-element.46.cell.refs_0_, f32[832,128]{1,0:T(8,128)S(1)} %get-tuple-element.47.change.refs_1_, f32[320,128]{1,0:T(8,128)S(1)} %get-tuple-element.50.halo_wind_x.refs_5_, ...), custom_call_target="tpu_custom_call" | custom-call | flops 990000000 | bytes 3240000 | tf_op jit(solution)/shard_map/pallas_call | solution.py:732
  18.7 0.0 collective-permute-done.4.second_ref
  18.7 0.0 collective-permute-done.5.first_ref
  18.7 0.0 copy-start.3
  18.7 0.0 copy-start.4
  18.7 1.2 %shard_map.84 = (f32[832,128]{1,0:T(8,128)S(1)}, f32[448,128]{1,0:T(8,128)S(1)}, f32[320,128]{1,0:T(8,128)S(1)}, f32[320,128]{1,0:T(8,128)S(1)}) custom-call(f32[1152,128]{1,0:T(8,128)S(1)} %get-tuple-element.46.cell.refs_0_, f32[832,128]{1,0:T(8,128)S(1)} %get-tuple-element.47.change.refs_1_, f32[512,128]{1,0:T(8,128)S(1)} %get-tuple-element.48.wind_x.refs_2_, ...), custom_call_target="tpu_custom_call" | custom-call | flops 1870000000 | bytes 6120000 | tf_op jit(solution)/shard_map/pallas_call | solution.py:732
  19.9 0.0 collective-permute-done.6.refs_14_
  19.9 0.0 collective-permute-done.7.refs_15_
  19.9 0.0 copy-done.3
  19.9 0.0 copy-done.4
  20.0 2.0 %shard_map.86 = (f32[1352,128]{1,0:T(8,128)S(1)}, f32[176,128]{1,0:T(8,128)S(1)}, f32[176,128]{1,0:T(8,128)S(1)}) custom-call(f32[1152,128]{1,0:T(8,128)S(1)} %get-tuple-element.46.cell.refs_0_, f32[832,128]{1,0:T(8,128)S(1)} %get-tuple-element.47.change.refs_1_, f32[512,128]{1,0:T(8,128)S(1)} %get-tuple-element.48.wind_x.refs_2_, ...), custom_call_target="tpu_custom_call" | custom-call | flops 2860000000 | bytes 9360000 | tf_op jit(solution)/shard_map/pallas_call | solution.py:732
  22.0 1.6 %collective-permute-start.9 = (f32[176,128]{1,0:T(8,128)S(1)}, f32[176,128]{1,0:T(8,128)S(1)}, u32[]{:S(2)}, u32[]{:S(2)}) collective-permute-start(f32[176,128]{1,0:T(8,128)S(1)} %get-tuple-element.69), channel_id=1, source_target_pairs={{0,1},{1,0},{2,3},{3,2},{4,5},{5,4},{6,7},{7,6},{8,9},{9,8},{10,11... | collective-permute-start | bytes 270344 | tf_op jit(solution)/shard_map/ppermute | solution.py:868
  23.5 1.0 %shard_map.87 = (f32[104,128]{1,0:T(8,128)S(1)}, f32[104,128]{1,0:T(8,128)S(1)}) custom-call(f32[1352,128]{1,0:T(8,128)S(1)} %get-tuple-element.64.one, f32[1152,128]{1,0:T(8,128)S(1)} %get-tuple-element.46.cell.refs_0_, f32[512,128]{1,0:T(8,128)S(1)} %get-tuple-element.48.wind_x.refs_2_, f32[448,128]{1,0:T(8,128)S(1)} %get-tuple-element.59.refs_11_.far_wind_x, ...), custom_call_target="tpu_custom_call" | custom-call | flops 770000000 | bytes 2520000 | tf_op jit(solution)/shard_map/pallas_call | solution.py:732
  24.6 0.6 %collective-permute-start.8 = (f32[104,128]{1,0:T(8,128)S(1)}, f32[104,128]{1,0:T(8,128)S(1)}, u32[]{:S(2)}, u32[]{:S(2)}) collective-permute-start(f32[104,128]{1,0:T(8,128)S(1)} %get-tuple-element.66), channel_id=1, source_target_pairs={{0,1},{1,0},{2,3},{3,2},{4,5},{5,4},{6,7},{7,6},{8,9},{9,8},{10,11... | collective-permute-start | bytes 159752 | tf_op jit(solution)/shard_map/ppermute | solution.py:881
  25.2 1.8 %collective-permute-done.9.got_ref = f32[176,128]{1,0:T(8,128)S(1)} collective-permute-done((f32[176,128]{1,0:T(8,128)S(1)}, f32[176,128]{1,0:T(8,128)S(1)}, u32[]{:S(2)}, u32[]{:S(2)}) %collective-permute-start.9) | collective-permute-done | bytes 90144 | tf_op jit(solution)/shard_map/ppermute | solution.py:868
  27.0 1.6 %shard_map.88 = (f32[5,8,16,64]{3,2,1,0:T(8,128)S(1)}, f32[5,4,64]{2,1,0:T(4,128)S(1)}) custom-call(f32[176,128]{1,0:T(8,128)S(1)} %get-tuple-element.68.keep_ref, f32[176,128]{1,0:T(8,128)S(1)} %collective-permute-done.9.got_ref, bf16[4224,128]{1,0:T(8,128)(2,1)S(1)} %get-tuple-element.67.pairs_ref, bf16[128,128]{1,0:T(8,128)(2,1)S(1)} %get-tuple-element.39.lost_ref), custom_call_target="tpu_custom_call" | custom-call | flops 1980000000 | bytes 6480000 | tf_op jit(solution)/shard_map/pallas_call | solution.py:732
  28.6 0.2 collective-permute-done.8.got_ref
  28.8 1.8 %shard_map.89 = (f32[8,8,16,64]{3,2,1,0:T(8,128)}, f32[8,4,64]{2,1,0:T(4,128)}) custom-call(f32[104,128]{1,0:T(8,128)S(1)} %get-tuple-element.65.keep_ref, f32[104,128]{1,0:T(8,128)S(1)} %collective-permute-done.8.got_ref, bf16[4224,128]{1,0:T(8,128)(2,1)S(1)} %get-tuple-element.67.pairs_ref, bf16[128,128]{1,0:T(8,128)(2,1)S(1)} %get-tuple-element.39.lost_ref, ...), custom_call_target="tpu_custom_call" | custom-call | flops 1320000000 | bytes 4320000 | tf_op jit(solution)/shard_map/pallas_call | solution.py:732
  (1 shorter events, 0.0 us)
Async XLA Ops:
  0.6 1.0 %copy-start.1 = (f32[8,8,16,64]{3,2,1,0:T(8,128)S(1)}, f32[8,8,16,64]{3,2,1,0:T(8,128)}, u32[]{:S(2)}) copy-start(f32[8,8,16,64]{3,2,1,0:T(8,128)} %mass_ref.1) | copy-start | bytes 786436
  1.7 3.3 %copy-start.2 = (f32[3,8,8,16]{3,2,1,0:T(8,128)S(1)}, f32[3,8,8,16]{3,2,1,0:T(8,128)}, u32[]{:S(2)}) copy-start(f32[3,8,8,16]{3,2,1,0:T(8,128)} %wind_ref.1) | copy-start | bytes 36868
  1.7 4.0 %copy-start.5 = (bf16[4096,64]{0,1:T(8,128)(2,1)S(1)}, bf16[4096,64]{0,1:T(8,128)(2,1)}, u32[]{:S(2)}) copy-start(bf16[4096,64]{0,1:T(8,128)(2,1)} %param.10) | copy-start | bytes 1572868
  2.0 4.2 %copy-start = (bf16[64,64]{1,0:T(8,128)(2,1)S(1)}, bf16[64,64]{1,0:T(8,128)(2,1)}, u32[]{:S(2)}) copy-start(bf16[64,64]{1,0:T(8,128)(2,1)} %loss_ref.1) | copy-start | bytes 24580
  2.0 6.9 %collective-permute-start = (f32[256,128]{1,0:T(8,128)S(1)}, f32[256,128]{1,0:T(8,128)S(1)}, u32[]{:S(2)}, u32[]{:S(2)}) collective-permute-start(f32[256,128]{1,0:T(8,128)S(1)} %get-tuple-element.38), channel_id=1, source_target_pairs={{0,1},{1,0},{2,3},{3,2},{4,5},{5,4},{6,7},{7,6},{8,9},{9,8},{10,11... | collective-permute-start | bytes 393224 | tf_op jit(solution)/shard_map/ppermute | solution.py:788
  5.1 3.7 %collective-permute-start.1 = (f32[24,128]{1,0:T(8,128)S(1)}, f32[24,128]{1,0:T(8,128)S(1)}, u32[]{:S(2)}, u32[]{:S(2)}) collective-permute-start(f32[24,128]{1,0:T(8,128)S(1)} %shard_map.78.own_wind_ref), channel_id=1, source_target_pairs={{0,1},{1,0},{2,3},{3,2},{4,5},{5,4},{6,7},{7,6},{8,9},{9,8},{10,11... | collective-permute-start | bytes 36872 | tf_op jit(solution)/shard_map/ppermute | solution.py:790
  9.1 6.3 %collective-permute-start.2 = (f32[408,128]{1,0:T(8,128)S(1)}, f32[408,128]{1,0:T(8,128)S(1)}, u32[]{:S(2)}, u32[]{:S(2)}) collective-permute-start(f32[408,128]{1,0:T(8,128)S(1)} %get-tuple-element.41), channel_id=1, source_target_pairs={{0,2},{1,3},{2,0},{3,1},{4,6},{5,7},{6,4},{7,5},{8,10},{9,11},{10,... | collective-permute-start | bytes 626696 | tf_op jit(solution)/shard_map/ppermute | solution.py:762
  10.9 4.6 %collective-permute-start.3 = (f32[408,128]{1,0:T(8,128)S(1)}, f32[408,128]{1,0:T(8,128)S(1)}, u32[]{:S(2)}, u32[]{:S(2)}) collective-permute-start(f32[408,128]{1,0:T(8,128)S(1)} %get-tuple-element.42), channel_id=1, source_target_pairs={{0,8},{1,9},{2,4},{3,5},{4,2},{5,3},{6,14},{7,15},{8,0},{9,1},{10,... | collective-permute-start | bytes 626696 | tf_op jit(solution)/shard_map/ppermute | solution.py:762
  10.9 7.8 %collective-permute-start.4 = (f32[408,128]{1,0:T(8,128)S(1)}, f32[408,128]{1,0:T(8,128)S(1)}, u32[]{:S(2)}, u32[]{:S(2)}) collective-permute-start(f32[408,128]{1,0:T(8,128)S(1)} %get-tuple-element.56), channel_id=1, source_target_pairs={{0,1},{1,0},{2,3},{3,2},{4,5},{5,4},{6,7},{7,6},{8,16},{9,17},{10,... | collective-permute-start | bytes 626696 | tf_op jit(solution)/shard_map/ppermute | solution.py:762
  12.4 6.3 %collective-permute-start.5 = (f32[408,128]{1,0:T(8,128)S(1)}, f32[408,128]{1,0:T(8,128)S(1)}, u32[]{:S(2)}, u32[]{:S(2)}) collective-permute-start(f32[408,128]{1,0:T(8,128)S(1)} %get-tuple-element.57), channel_id=1, source_target_pairs={{0,8},{1,9},{2,10},{3,11},{4,12},{5,13},{6,14},{7,15},{8,0},{9,1},... | collective-permute-start | bytes 626696 | tf_op jit(solution)/shard_map/ppermute | solution.py:762
  15.5 4.5 %collective-permute-start.6 = (f32[152,128]{1,0:T(8,128)S(1)}, f32[152,128]{1,0:T(8,128)S(1)}, u32[]{:S(2)}, u32[]{:S(2)}) collective-permute-start(f32[152,128]{1,0:T(8,128)S(1)} %get-tuple-element.62), channel_id=1, source_target_pairs={{0,1},{1,0},{2,3},{3,2},{4,5},{5,4},{6,7},{7,6},{8,16},{9,17},{10,... | collective-permute-start | bytes 233480 | tf_op jit(solution)/shard_map/ppermute | solution.py:762
  17.0 3.0 %collective-permute-start.7 = (f32[152,128]{1,0:T(8,128)S(1)}, f32[152,128]{1,0:T(8,128)S(1)}, u32[]{:S(2)}, u32[]{:S(2)}) collective-permute-start(f32[152,128]{1,0:T(8,128)S(1)} %get-tuple-element.63), channel_id=1, source_target_pairs={{0,8},{1,9},{2,10},{3,11},{4,12},{5,13},{6,14},{7,15},{8,0},{9,1},... | collective-permute-start | bytes 233480 | tf_op jit(solution)/shard_map/ppermute | solution.py:762
  18.7 1.2 %copy-start.3 = (f32[64]{0:T(128)S(1)}, f32[64]{0:T(128)}, u32[]{:S(2)}) copy-start(f32[64]{0:T(128)} %param.8) | copy-start | bytes 772
  18.7 1.2 %copy-start.4 = (s32[64]{0:T(128)S(1)}, s32[64]{0:T(128)}, u32[]{:S(2)}) copy-start(s32[64]{0:T(128)} %param.9) | copy-start | bytes 772
  22.0 5.0 %collective-permute-start.9 = (f32[176,128]{1,0:T(8,128)S(1)}, f32[176,128]{1,0:T(8,128)S(1)}, u32[]{:S(2)}, u32[]{:S(2)}) collective-permute-start(f32[176,128]{1,0:T(8,128)S(1)} %get-tuple-element.69), channel_id=1, source_target_pairs={{0,1},{1,0},{2,3},{3,2},{4,5},{5,4},{6,7},{7,6},{8,9},{9,8},{10,11... | collective-permute-start | bytes 270344 | tf_op jit(solution)/shard_map/ppermute | solution.py:868
  24.6 4.2 %collective-permute-start.8 = (f32[104,128]{1,0:T(8,128)S(1)}, f32[104,128]{1,0:T(8,128)S(1)}, u32[]{:S(2)}, u32[]{:S(2)}) collective-permute-start(f32[104,128]{1,0:T(8,128)S(1)} %get-tuple-element.66), channel_id=1, source_target_pairs={{0,1},{1,0},{2,3},{3,2},{4,5},{5,4},{6,7},{7,6},{8,9},{9,8},{10,11... | collective-permute-start | bytes 159752 | tf_op jit(solution)/shard_map/ppermute | solution.py:881

commit v5 on v4

--- a/solution.py
+++ b/solution.py
@@ -279,7 +279,7 @@
         winds = [wind_z[eight(x * n, k)] for k in range(ROWS)]
         return [(change, eight(x * n, k), value) for k, value in enumerate(level_change(cells, winds, width))]
 
-    each(n, 2, along_z)
+    each(n, 4, along_z)
     begin, end = LO, n - HI
     for wind, edge, place in ((wind_x, edge_x, lambda i, k: k * n + i), (wind_y, edge_y, lambda i, k: i * n + k)):
 
@@ -325,7 +325,7 @@
         winds = [wind_z[eight(i * n, k)] for k in range(ROWS)]
         return [(halo_change, eight(i * n, k), value) for k, value in enumerate(level_change(cells, winds, width))]
 
-    each(LINES, 2, along_z)
+    each(LINES, LINES, along_z)
 
     def along_y(x):
         cells = [cell[rows_of(x * span + y)] for y in range(span)]
@@ -342,7 +342,7 @@
             stores.append((change, rows_of(x * reach + y + LO), own_change[rows_of(x * n + y)]))
         return stores
 
-    each(n, 2, along_y)
+    each(n, 4, along_y)
 
 
 def which(i, lower, upper):
@@ -435,7 +435,7 @@
         winds = [side_wind_z[eight(i * n, k)] for k in range(ROWS)]
         return [(side_change, eight(i * n, k), value) for k, value in enumerate(level_change(cells, winds, width))]
 
-    each(LINES, 2, along_z)
+    each(LINES, LINES, along_z)
 
     def along_x(y):
         outer = [far[rows_of(i * n + y)] for i in range(LINES)]
@@ -452,7 +452,7 @@
             stores.append((mid, rows_of((x + LO) * n + y), cells[PAD_LO + x] + value))
         return stores
 
-    each(n, 2, along_x)
+    each(n, 4, along_x)
 
 
 def main_kernel(n, parts, *refs):
@@ -516,7 +516,7 @@
             stores.append((one, rows_of((x + LO) * reach + line), value))
         return stores
 
-    each(LINES, 2, along_y)
+    each(LINES, LINES, along_y)
     each(LINES, LINES, along_x)
     fall_layers(
         n, parts, 0, EARLY, one, cell, wind_x, far_wind_x, wind_y, far_wind_y, wind_z, inner_second, rate_ref, steps_ref,
@@ -605,7 +605,11 @@
             rain_ref[rows_of(i)] = rain[i]
 
 
-def matrix_kernel(bins, gain_ref, loss_ref, pairs_ref, lost_ref, wide, tall):
+def by_matrix(bins):
+    return [d for d in range(bins // 2) if d % 4 > 1]
+
+
+def matrix_kernel(bins, gain_ref, loss_ref, pairs_ref, lost_ref, shifts_ref, wide, tall):
     zero = jnp.zeros((bins, LANES - bins), F32)
     shifts = bins // 2
 
@@ -627,12 +631,16 @@
             rows = rows + tall[pl.ds(d * bins, bins, stride=bins + 1)]
         pairs_ref[pl.ds(d * LANES, bins)] = rows.astype(jnp.bfloat16)
         pairs_ref[pl.ds(d * LANES + bins, bins)] = pltpu.roll(rows, bins, 1).astype(jnp.bfloat16)
+    source, target = [lax.broadcasted_iota(jnp.int32, (LANES, LANES), k) for k in range(2)]
+    for k, d in enumerate(by_matrix(bins)):
+        here = source == target // bins * bins + (target + d) % bins
+        shifts_ref[:, k * LANES : (k + 1) * LANES] = jnp.where(here, 1.0, 0.0).astype(jnp.bfloat16)
     rows = jnp.concatenate([loss_ref[...].astype(F32), zero], axis=1)
     lost_ref[pl.ds(0, bins)] = rows.astype(jnp.bfloat16)
     lost_ref[pl.ds(bins, bins)] = pltpu.roll(rows, bins, 1).astype(jnp.bfloat16)
 
 
-def breakup_rows(mass, pairs_ref, lost_ref, products):
+def breakup_rows(mass, pairs_ref, lost_ref, shifts_ref, products):
     bins = LANES // 2
     count = mass.shape[0]
     lanes = lane_ids()
@@ -642,11 +650,20 @@
     shifts = bins // 2 + 1
     for begin in range(0, shifts, 4):
         end = min(begin + 4, shifts)
+        matrix = begin // 2 * LANES
+        if end == begin + 4:
+            shifted = jnp.dot(rounded, shifts_ref[:, matrix : matrix + 2 * LANES], preferred_element_type=F32)
         for d in range(begin, end):
             ids = lanes // bins * bins + (lanes + d) % bins
             for r in range(0, count, 2 * ROWS):
-                halves = [wide[r + ROWS * k : r + ROWS * (k + 1)] for k in range(2)]
-                halves = [v * pick(v, ids) if d else v * v for v in halves]
+                halves = []
+                for at in (r, r + ROWS):
+                    value = other = wide[at : at + ROWS]
+                    if d % 4 > 1:
+                        other = shifted[at : at + ROWS, (d % 4 - 2) * LANES : (d % 4 - 1) * LANES]
+                    elif d:
+                        other = pick(value, ids)
+                    halves.append(value * other)
                 both = jnp.concatenate(halves, axis=0).astype(jnp.bfloat16)
                 products[pl.ds(r, 2 * ROWS), d * LANES : (d + 1) * LANES] = both
         part = jnp.dot(
@@ -659,7 +676,7 @@
     return mass + gained - mass * loss
 
 
-def breakup_layers(n, count, keep_ref, got_ref, pairs_ref, lost_ref, columns, products):
+def breakup_layers(n, count, keep_ref, got_ref, pairs_ref, lost_ref, shifts_ref, columns, products):
     first = is_even("gz")
     half = count * n // 2
     for c in range(half):
@@ -671,7 +688,7 @@
         a, b = order(keep_ref[rows_of(half + i // 4)], got_ref[rows_of(half + i // 4)], first)
         a, b = [jnp.where(first, v[: n // 2], v[n // 2 :])[:, 32 * (i % 4) : 32 * (i % 4) + 32] for v in (a, b)]
         rain.append(jnp.concatenate([a, b], axis=1))
-    columns[...] = breakup_rows(columns[...], pairs_ref, lost_ref, products)
+    columns[...] = breakup_rows(columns[...], pairs_ref, lost_ref, shifts_ref, products)
     return rain
 
 
@@ -683,18 +700,18 @@
             mass[x, y, ROWS : 2 * ROWS] = value[:, 64:]
 
 
-def breakup_first_kernel(n, keep_ref, got_ref, pairs_ref, lost_ref, mass_ref, rain_ref, columns, products):
-    for i, value in enumerate(breakup_layers(n, EARLY, keep_ref, got_ref, pairs_ref, lost_ref, columns, products)):
+def breakup_first_kernel(n, keep_ref, got_ref, pairs_ref, lost_ref, shifts_ref, mass_ref, rain_ref, columns, products):
+    for i, value in enumerate(breakup_layers(n, EARLY, keep_ref, got_ref, pairs_ref, lost_ref, shifts_ref, columns, products)):
         rain_ref[i] = value
     lay_out(columns, mass_ref, n, EARLY)
 
 
 def breakup_last_kernel(
-    n, keep_ref, got_ref, pairs_ref, lost_ref, early, early_rain, mass_out, rain_out, columns, products, mass, rain, sems
+    n, keep_ref, got_ref, pairs_ref, lost_ref, shifts_ref, early, early_rain, mass_out, rain_out, columns, products, mass, rain, sems
 ):
     early_copy = pltpu.make_async_copy(early, mass_out.at[pl.ds(0, EARLY)], sems.at[0])
     early_copy.start()
-    late_rain = breakup_layers(n, n - EARLY, keep_ref, got_ref, pairs_ref, lost_ref, columns, products)
+    late_rain = breakup_layers(n, n - EARLY, keep_ref, got_ref, pairs_ref, lost_ref, shifts_ref, columns, products)
     for i in range(EARLY):
         rain[i] = early_rain[i]
     for i, value in enumerate(late_rain):
@@ -708,13 +725,13 @@
         copy.wait()
 
 
-def breakup_plain_kernel(mass_ref, pairs_ref, lost_ref, out_ref, products):
+def breakup_plain_kernel(mass_ref, pairs_ref, lost_ref, shifts_ref, out_ref, products):
     count = products.shape[0]
 
     @pl.loop(0, mass_ref.shape[0] // count)
     def _(i):
         start = pl.multiple_of(i * count, count)
-        out_ref[pl.ds(start, count)] = breakup_rows(mass_ref[pl.ds(start, count)], pairs_ref, lost_ref, products)
+        out_ref[pl.ds(start, count)] = breakup_rows(mass_ref[pl.ds(start, count)], pairs_ref, lost_ref, shifts_ref, products)
 
 
 def shape(*dims, dtype=F32):
@@ -772,9 +789,13 @@
     winds = 3 * tiles
 
     pair_rows = (bins // 2 + 1) * LANES
-    pairs, lost = call(
+    matrices = pairs, lost, _ = call(
         functools.partial(matrix_kernel, bins),
-        (shape(pair_rows, LANES, dtype=jnp.bfloat16), shape(LANES, LANES, dtype=jnp.bfloat16)),
+        [
+            shape(pair_rows, LANES, dtype=jnp.bfloat16),
+            shape(LANES, LANES, dtype=jnp.bfloat16),
+            shape(LANES, len(by_matrix(bins)) * LANES, dtype=jnp.bfloat16),
+        ],
         (frag_gain, collide),
         [shape(2 * bins * bins, LANES), shape(3 * bins * bins // 2, LANES)],
         micros=0.02,
@@ -882,7 +903,7 @@
         early = call(
             functools.partial(breakup_first_kernel, n),
             [shape(EARLY, ny, nz, bins), shape(EARLY, ny // parts, bins)],
-            (early[1], early_got, pairs, lost),
+            (early[1], early_got, *matrices),
             [tiles_of(n * EARLY), products(EARLY)],
             micros=1.8,
         )
@@ -891,7 +912,7 @@
             call(
                 functools.partial(breakup_last_kernel, n),
                 outs,
-                (late[1], late_got, pairs, lost, *early),
+                (late[1], late_got, *matrices, *early),
                 [tiles_of(n * (n - EARLY)), products(n - EARLY), shape(n - EARLY, ny, nz, bins), outs[1]],
                 micros=1.2,
                 out_place=pl.ANY,
@@ -906,7 +927,7 @@
     settled = lax.all_to_all(settled, "gz", split_axis=0, concat_axis=0, tiled=True)
     settled = settled.transpose(1, 2, 3, 4, 0, 5).reshape(nx * ny, nz // ROWS, ROWS, bins)
     paired = settled.transpose(0, 2, 1, 3).reshape(-1, LANES)
-    updated = call(breakup_plain_kernel, tiles_of(n * n), (paired, pairs, lost), [products(n // 2)], micros=3.0)
+    updated = call(breakup_plain_kernel, tiles_of(n * n), (paired, *matrices), [products(n // 2)], micros=3.0)
     updated = updated.reshape(nx, ny, ROWS, nz // ROWS, bins).transpose(0, 1, 3, 2, 4).reshape(nx, ny, nz, bins)
     return updated, rain
 

time: 30.7 us -> 31 us (level)
    ppermute x6, waiting for transfers between devices: 1.73 us -> 2.2 us  [swap_neighbours(): return lax.ppermute(message, axes, pairs)]
    ppermute x1, waiting for transfers between devices: 1.81 us -> 1.44 us  [per_device(): early_got = lax.ppermute(early[0], 'gz', [(0, 1), (1, 0)])]
  transfers between devices with their start and end apart: 10 -> 10, of which waited for: 4 -> 5; matrix products, arithmetic and copies ran while one was open for 2% -> 2% of each run, Pallas kernels for 27% -> 27%
where the time goes in v5:
time: 31 us; the launch traced here: 30.7 us
  Pallas kernels  12.7 us (41%)
  starting transfers between devices  10.7 us (35%)
  waiting for transfers between devices  5.04 us (16%)
  local copies, waits for them, and re-layouts  1.54 us (5%)
  between operations  0.77 us (2%)
    pallas_call x13, Pallas kernels, call(): pl.pallas_call(kernel, out_shape=outs, in_specs=[VMEM] * len(args), out_s...  12.7 us
    ppermute x6, starting transfers between devices, swap_neighbours(): return lax.ppermute(message, axes, pairs)  4.94 us
    ppermute x1, starting transfers between devices, per_device(): got = lax.ppermute(send, 'gz', [(0, 1), (1, 0)])  3.03 us
    ppermute x6, waiting for transfers between devices, swap_neighbours(): return lax.ppermute(message, axes, pairs)  2.2 us
    unnamed x13, local copies, waits for them, and re-layouts  1.54 us
    ppermute x1, starting transfers between devices, per_device(): early_got = lax.ppermute(early[0], 'gz', [(0, 1), (1, 0)])  1.49 us
    ppermute x1, waiting for transfers between devices, per_device(): early_got = lax.ppermute(early[0], 'gz', [(0, 1), (1, 0)])  1.44 us
    ppermute x1, waiting for transfers between devices, per_device(): got_wind = lax.ppermute(own_wind, 'gz', [(0, 1), (1, 0)])  1.2 us
  transfers between devices with their start and end apart: 10, of which 5 were waited for; matrix products, arithmetic and copies ran while one was open for 2% of the time, Pallas kernels for 27%

profile of v5, /device:TPU:0, one launch (start us, length us, event | category | flops | bytes accessed | tf_op | source)
XLA Modules:
  0.0 30.7 jit_solution(1145476900827845964)
XLA Ops:
  0.6 0.0 copy-start.1
  0.6 1.0 %copy-done.1 = f32[8,8,16,64]{3,2,1,0:T(8,128)S(1)} copy-done((f32[8,8,16,64]{3,2,1,0:T(8,128)S(1)}, f32[8,8,16,64]{3,2,1,0:T(8,128)}, u32[]{:S(2)}) %copy-start.1) | copy-done | bytes 262168
  1.7 0.0 copy-start.2
  1.7 0.0 copy-start.5
  1.7 0.3 shard_map.77
  2.0 0.0 copy-start
  2.0 3.0 %collective-permute-start = (f32[256,128]{1,0:T(8,128)S(1)}, f32[256,128]{1,0:T(8,128)S(1)}, u32[]{:S(2)}, u32[]{:S(2)}) collective-permute-start(f32[256,128]{1,0:T(8,128)S(1)} %get-tuple-element.39), channel_id=1, source_target_pairs={{0,1},{1,0},{2,3},{3,2},{4,5},{5,4},{6,7},{7,6},{8,9},{9,8},{10,11... | collective-permute-start | bytes 393224 | tf_op jit(solution)/shard_map/ppermute | solution.py:809
  5.0 0.0 copy-done.2
  5.0 0.1 shard_map.78.own_wind_ref
  5.1 0.6 %collective-permute-start.1 = (f32[24,128]{1,0:T(8,128)S(1)}, f32[24,128]{1,0:T(8,128)S(1)}, u32[]{:S(2)}, u32[]{:S(2)}) collective-permute-start(f32[24,128]{1,0:T(8,128)S(1)} %shard_map.78.own_wind_ref), channel_id=1, source_target_pairs={{0,1},{1,0},{2,3},{3,2},{4,5},{5,4},{6,7},{7,6},{8,9},{9,8},{10,11... | collective-permute-start | bytes 36872 | tf_op jit(solution)/shard_map/ppermute | solution.py:811
  5.7 0.0 copy-done.5
  5.7 0.5 %copy.8.gain_ref = bf16[4096,64]{1,0:T(8,128)(2,1)S(1)} copy(bf16[4096,64]{0,1:T(8,128)(2,1)S(1)} %copy-done.5) | data formatting | bytes 1048576 | tf_op args[4]
  6.2 0.0 copy-done
  6.2 1.5 %shard_map.79 = (bf16[4224,128]{1,0:T(8,128)(2,1)S(1)}, bf16[128,128]{1,0:T(8,128)(2,1)S(1)}, bf16[128,2048]{1,0:T(8,128)(2,1)S(1)}) custom-call(bf16[4096,64]{1,0:T(8,128)(2,1)S(1)} %copy.8.gain_ref, bf16[64,64]{1,0:T(8,128)(2,1)S(1)} %copy-done), custom_call_target="tpu_custom_call" | custom-call | flops 22000000 | bytes 72000 | tf_op jit(solution)/shard_map/pallas_call | solution.py:749
  7.6 1.2 %collective-permute-done.1.got_wind_ref = f32[24,128]{1,0:T(8,128)S(1)} collective-permute-done((f32[24,128]{1,0:T(8,128)S(1)}, f32[24,128]{1,0:T(8,128)S(1)}, u32[]{:S(2)}, u32[]{:S(2)}) %collective-permute-start.1) | collective-permute-done | bytes 12320 | tf_op jit(solution)/shard_map/ppermute | solution.py:811
  8.9 0.0 collective-permute-done.got_ref
  8.9 0.3 shard_map.80
  9.1 1.8 %collective-permute-start.2 = (f32[408,128]{1,0:T(8,128)S(1)}, f32[408,128]{1,0:T(8,128)S(1)}, u32[]{:S(2)}, u32[]{:S(2)}) collective-permute-start(f32[408,128]{1,0:T(8,128)S(1)} %get-tuple-element.42), channel_id=1, source_target_pairs={{0,2},{1,3},{2,0},{3,1},{4,6},{5,7},{6,4},{7,5},{8,10},{9,11},{10,... | collective-permute-start | bytes 626696 | tf_op jit(solution)/shard_map/ppermute | solution.py:779
  10.9 0.0 collective-permute-start.3
  10.9 1.5 %collective-permute-start.4 = (f32[408,128]{1,0:T(8,128)S(1)}, f32[408,128]{1,0:T(8,128)S(1)}, u32[]{:S(2)}, u32[]{:S(2)}) collective-permute-start(f32[408,128]{1,0:T(8,128)S(1)} %get-tuple-element.57), channel_id=1, source_target_pairs={{0,1},{1,0},{2,3},{3,2},{4,5},{5,4},{6,7},{7,6},{8,16},{9,17},{10,... | collective-permute-start | bytes 626696 | tf_op jit(solution)/shard_map/ppermute | solution.py:779
  12.4 0.1 collective-permute-start.5
  12.5 1.3 %shard_map.81 = (f32[512,128]{1,0:T(8,128)S(1)}, f32[512,128]{1,0:T(8,128)S(1)}, f32[512,128]{1,0:T(8,128)S(1)}, f32[512,128]{1,0:T(8,128)S(1)}, f32[128,128]{1,0:T(8,128)S(1)}, /*index=5*/f32[128,128]{1,0:T(8,128)S(1)}) custom-call(f32[560,128]{1,0:T(8,128)S(1)} %get-tuple-element.41.block_ref), custom_call_target="tpu_custom_call" | custom-call | flops 1760000000 | bytes 5760000 | tf_op jit(solution)/shard_map/pallas_call | solution.py:749
  13.8 1.7 %collective-permute-done.2.first_ref = f32[408,128]{1,0:T(8,128)S(1)} collective-permute-done((f32[408,128]{1,0:T(8,128)S(1)}, f32[408,128]{1,0:T(8,128)S(1)}, u32[]{:S(2)}, u32[]{:S(2)}) %collective-permute-start.2) | collective-permute-done | bytes 208928 | tf_op jit(solution)/shard_map/ppermute | solution.py:779
  15.4 0.0 collective-permute-done.3.second_ref
  15.5 1.5 %collective-permute-start.6 = (f32[152,128]{1,0:T(8,128)S(1)}, f32[152,128]{1,0:T(8,128)S(1)}, u32[]{:S(2)}, u32[]{:S(2)}) collective-permute-start(f32[152,128]{1,0:T(8,128)S(1)} %get-tuple-element.63), channel_id=1, source_target_pairs={{0,1},{1,0},{2,3},{3,2},{4,5},{5,4},{6,7},{7,6},{8,16},{9,17},{10,... | collective-permute-start | bytes 233480 | tf_op jit(solution)/shard_map/ppermute | solution.py:779
  17.0 0.1 collective-permute-start.7
  17.1 1.0 %shard_map.82 = (f32[1152,128]{1,0:T(8,128)S(1)}, f32[832,128]{1,0:T(8,128)S(1)}, f32[320,128]{1,0:T(8,128)S(1)}, f32[448,128]{1,0:T(8,128)S(1)}) custom-call(f32[560,128]{1,0:T(8,128)S(1)} %get-tuple-element.41.block_ref, f32[408,128]{1,0:T(8,128)S(1)} %collective-permute-done.2.first_ref, f32[408,128]{1,0:T(8,128)S(1)} %collective-permute-done.3.second_ref, ...), custom_call_target="tpu_custom_call" | custom-call | flops 2200000000 | bytes 7200000 | tf_op jit(solution)/shard_map/pallas_call | solution.py:749
  18.0 0.5 %shard_map.83 = (f32[312,128]{1,0:T(8,128)S(1)}, f32[208,128]{1,0:T(8,128)S(1)}, f32[192,128]{1,0:T(8,128)S(1)}) custom-call(f32[1152,128]{1,0:T(8,128)S(1)} %get-tuple-element.47.cell.refs_0_, f32[832,128]{1,0:T(8,128)S(1)} %get-tuple-element.48.change.refs_1_, f32[320,128]{1,0:T(8,128)S(1)} %get-tuple-element.51.halo_wind_x.refs_5_, ...), custom_call_target="tpu_custom_call" | custom-call | flops 990000000 | bytes 3240000 | tf_op jit(solution)/shard_map/pallas_call | solution.py:749
  18.5 0.0 collective-permute-done.4.second_ref
  18.5 0.0 collective-permute-done.5.first_ref
  18.5 0.0 copy-start.3
  18.5 0.0 copy-start.4
  18.5 0.9 %shard_map.84 = (f32[832,128]{1,0:T(8,128)S(1)}, f32[448,128]{1,0:T(8,128)S(1)}, f32[320,128]{1,0:T(8,128)S(1)}, f32[320,128]{1,0:T(8,128)S(1)}) custom-call(f32[1152,128]{1,0:T(8,128)S(1)} %get-tuple-element.47.cell.refs_0_, f32[832,128]{1,0:T(8,128)S(1)} %get-tuple-element.48.change.refs_1_, f32[512,128]{1,0:T(8,128)S(1)} %get-tuple-element.49.wind_x.refs_2_, ...), custom_call_target="tpu_custom_call" | custom-call | flops 1870000000 | bytes 6120000 | tf_op jit(solution)/shard_map/pallas_call | solution.py:749
  19.4 0.5 %collective-permute-done.6.refs_14_ = f32[152,128]{1,0:T(8,128)S(1)} collective-permute-done((f32[152,128]{1,0:T(8,128)S(1)}, f32[152,128]{1,0:T(8,128)S(1)}, u32[]{:S(2)}, u32[]{:S(2)}) %collective-permute-start.6) | collective-permute-done | bytes 77856 | tf_op jit(solution)/shard_map/ppermute | solution.py:779
  19.9 0.0 collective-permute-done.7.refs_15_
  19.9 0.0 copy-done.3
  19.9 0.0 copy-done.4
  20.0 1.9 %shard_map.86 = (f32[1352,128]{1,0:T(8,128)S(1)}, f32[176,128]{1,0:T(8,128)S(1)}, f32[176,128]{1,0:T(8,128)S(1)}) custom-call(f32[1152,128]{1,0:T(8,128)S(1)} %get-tuple-element.47.cell.refs_0_, f32[832,128]{1,0:T(8,128)S(1)} %get-tuple-element.48.change.refs_1_, f32[512,128]{1,0:T(8,128)S(1)} %get-tuple-element.49.wind_x.refs_2_, ...), custom_call_target="tpu_custom_call" | custom-call | flops 2860000000 | bytes 9360000 | tf_op jit(solution)/shard_map/pallas_call | solution.py:749
  21.8 1.5 %collective-permute-start.9 = (f32[176,128]{1,0:T(8,128)S(1)}, f32[176,128]{1,0:T(8,128)S(1)}, u32[]{:S(2)}, u32[]{:S(2)}) collective-permute-start(f32[176,128]{1,0:T(8,128)S(1)} %get-tuple-element.71), channel_id=1, source_target_pairs={{0,1},{1,0},{2,3},{3,2},{4,5},{5,4},{6,7},{7,6},{8,9},{9,8},{10,11... | collective-permute-start | bytes 270344 | tf_op jit(solution)/shard_map/ppermute | solution.py:889
  23.3 1.0 %shard_map.87 = (f32[104,128]{1,0:T(8,128)S(1)}, f32[104,128]{1,0:T(8,128)S(1)}) custom-call(f32[1352,128]{1,0:T(8,128)S(1)} %get-tuple-element.65.one, f32[1152,128]{1,0:T(8,128)S(1)} %get-tuple-element.47.cell.refs_0_, f32[512,128]{1,0:T(8,128)S(1)} %get-tuple-element.49.wind_x.refs_2_, f32[448,128]{1,0:T(8,128)S(1)} %get-tuple-element.60.refs_11_.far_wind_x, ...), custom_call_target="tpu_custom_call" | custom-call | flops 770000000 | bytes 2520000 | tf_op jit(solution)/shard_map/pallas_call | solution.py:749
  24.4 0.7 %collective-permute-start.8 = (f32[104,128]{1,0:T(8,128)S(1)}, f32[104,128]{1,0:T(8,128)S(1)}, u32[]{:S(2)}, u32[]{:S(2)}) collective-permute-start(f32[104,128]{1,0:T(8,128)S(1)} %get-tuple-element.67), channel_id=1, source_target_pairs={{0,1},{1,0},{2,3},{3,2},{4,5},{5,4},{6,7},{7,6},{8,9},{9,8},{10,11... | collective-permute-start | bytes 159752 | tf_op jit(solution)/shard_map/ppermute | solution.py:902
  25.0 1.4 %collective-permute-done.9.got_ref = f32[176,128]{1,0:T(8,128)S(1)} collective-permute-done((f32[176,128]{1,0:T(8,128)S(1)}, f32[176,128]{1,0:T(8,128)S(1)}, u32[]{:S(2)}, u32[]{:S(2)}) %collective-permute-start.9) | collective-permute-done | bytes 90144 | tf_op jit(solution)/shard_map/ppermute | solution.py:889
  26.5 1.9 %shard_map.88 = (f32[5,8,16,64]{3,2,1,0:T(8,128)S(1)}, f32[5,4,64]{2,1,0:T(4,128)S(1)}) custom-call(f32[176,128]{1,0:T(8,128)S(1)} %get-tuple-element.70.keep_ref, f32[176,128]{1,0:T(8,128)S(1)} %collective-permute-done.9.got_ref, bf16[4224,128]{1,0:T(8,128)(2,1)S(1)} %get-tuple-element.68.pairs_ref, bf16[128,128]{1,0:T(8,128)(2,1)S(1)} %get-tuple-element.40.lost_ref, ...), custom_call_target="tpu_custom_call" | custom-call | flops 1980000000 | bytes 6480000 | tf_op jit(solution)/shard_map/pallas_call | solution.py:749
  28.4 0.2 collective-permute-done.8.got_ref
  28.6 2.1 %shard_map.89 = (f32[8,8,16,64]{3,2,1,0:T(8,128)}, f32[8,4,64]{2,1,0:T(4,128)}) custom-call(f32[104,128]{1,0:T(8,128)S(1)} %get-tuple-element.66.keep_ref, f32[104,128]{1,0:T(8,128)S(1)} %collective-permute-done.8.got_ref, bf16[4224,128]{1,0:T(8,128)(2,1)S(1)} %get-tuple-element.68.pairs_ref, bf16[128,128]{1,0:T(8,128)(2,1)S(1)} %get-tuple-element.40.lost_ref, ...), custom_call_target="tpu_custom_call" | custom-call | flops 1320000000 | bytes 4320000 | tf_op jit(solution)/shard_map/pallas_call | solution.py:749
  (1 shorter events, 0.0 us)
Async XLA Ops:
  0.6 1.0 %copy-start.1 = (f32[8,8,16,64]{3,2,1,0:T(8,128)S(1)}, f32[8,8,16,64]{3,2,1,0:T(8,128)}, u32[]{:S(2)}) copy-start(f32[8,8,16,64]{3,2,1,0:T(8,128)} %mass_ref.1) | copy-start | bytes 786436
  1.7 3.3 %copy-start.2 = (f32[3,8,8,16]{3,2,1,0:T(8,128)S(1)}, f32[3,8,8,16]{3,2,1,0:T(8,128)}, u32[]{:S(2)}) copy-start(f32[3,8,8,16]{3,2,1,0:T(8,128)} %wind_ref.1) | copy-start | bytes 36868
  1.7 4.0 %copy-start.5 = (bf16[4096,64]{0,1:T(8,128)(2,1)S(1)}, bf16[4096,64]{0,1:T(8,128)(2,1)}, u32[]{:S(2)}) copy-start(bf16[4096,64]{0,1:T(8,128)(2,1)} %param.10) | copy-start | bytes 1572868
  2.0 4.2 %copy-start = (bf16[64,64]{1,0:T(8,128)(2,1)S(1)}, bf16[64,64]{1,0:T(8,128)(2,1)}, u32[]{:S(2)}) copy-start(bf16[64,64]{1,0:T(8,128)(2,1)} %loss_ref.1) | copy-start | bytes 24580
  2.0 6.9 %collective-permute-start = (f32[256,128]{1,0:T(8,128)S(1)}, f32[256,128]{1,0:T(8,128)S(1)}, u32[]{:S(2)}, u32[]{:S(2)}) collective-permute-start(f32[256,128]{1,0:T(8,128)S(1)} %get-tuple-element.39), channel_id=1, source_target_pairs={{0,1},{1,0},{2,3},{3,2},{4,5},{5,4},{6,7},{7,6},{8,9},{9,8},{10,11... | collective-permute-start | bytes 393224 | tf_op jit(solution)/shard_map/ppermute | solution.py:809
  5.1 3.7 %collective-permute-start.1 = (f32[24,128]{1,0:T(8,128)S(1)}, f32[24,128]{1,0:T(8,128)S(1)}, u32[]{:S(2)}, u32[]{:S(2)}) collective-permute-start(f32[24,128]{1,0:T(8,128)S(1)} %shard_map.78.own_wind_ref), channel_id=1, source_target_pairs={{0,1},{1,0},{2,3},{3,2},{4,5},{5,4},{6,7},{7,6},{8,9},{9,8},{10,11... | collective-permute-start | bytes 36872 | tf_op jit(solution)/shard_map/ppermute | solution.py:811
  9.1 6.3 %collective-permute-start.2 = (f32[408,128]{1,0:T(8,128)S(1)}, f32[408,128]{1,0:T(8,128)S(1)}, u32[]{:S(2)}, u32[]{:S(2)}) collective-permute-start(f32[408,128]{1,0:T(8,128)S(1)} %get-tuple-element.42), channel_id=1, source_target_pairs={{0,2},{1,3},{2,0},{3,1},{4,6},{5,7},{6,4},{7,5},{8,10},{9,11},{10,... | collective-permute-start | bytes 626696 | tf_op jit(solution)/shard_map/ppermute | solution.py:779
  10.9 4.6 %collective-permute-start.3 = (f32[408,128]{1,0:T(8,128)S(1)}, f32[408,128]{1,0:T(8,128)S(1)}, u32[]{:S(2)}, u32[]{:S(2)}) collective-permute-start(f32[408,128]{1,0:T(8,128)S(1)} %get-tuple-element.43), channel_id=1, source_target_pairs={{0,8},{1,9},{2,4},{3,5},{4,2},{5,3},{6,14},{7,15},{8,0},{9,1},{10,... | collective-permute-start | bytes 626696 | tf_op jit(solution)/shard_map/ppermute | solution.py:779
  10.9 7.6 %collective-permute-start.4 = (f32[408,128]{1,0:T(8,128)S(1)}, f32[408,128]{1,0:T(8,128)S(1)}, u32[]{:S(2)}, u32[]{:S(2)}) collective-permute-start(f32[408,128]{1,0:T(8,128)S(1)} %get-tuple-element.57), channel_id=1, source_target_pairs={{0,1},{1,0},{2,3},{3,2},{4,5},{5,4},{6,7},{7,6},{8,16},{9,17},{10,... | collective-permute-start | bytes 626696 | tf_op jit(solution)/shard_map/ppermute | solution.py:779
  12.4 6.1 %collective-permute-start.5 = (f32[408,128]{1,0:T(8,128)S(1)}, f32[408,128]{1,0:T(8,128)S(1)}, u32[]{:S(2)}, u32[]{:S(2)}) collective-permute-start(f32[408,128]{1,0:T(8,128)S(1)} %get-tuple-element.58), channel_id=1, source_target_pairs={{0,8},{1,9},{2,10},{3,11},{4,12},{5,13},{6,14},{7,15},{8,0},{9,1},... | collective-permute-start | bytes 626696 | tf_op jit(solution)/shard_map/ppermute | solution.py:779
  15.5 4.5 %collective-permute-start.6 = (f32[152,128]{1,0:T(8,128)S(1)}, f32[152,128]{1,0:T(8,128)S(1)}, u32[]{:S(2)}, u32[]{:S(2)}) collective-permute-start(f32[152,128]{1,0:T(8,128)S(1)} %get-tuple-element.63), channel_id=1, source_target_pairs={{0,1},{1,0},{2,3},{3,2},{4,5},{5,4},{6,7},{7,6},{8,16},{9,17},{10,... | collective-permute-start | bytes 233480 | tf_op jit(solution)/shard_map/ppermute | solution.py:779
  17.0 3.0 %collective-permute-start.7 = (f32[152,128]{1,0:T(8,128)S(1)}, f32[152,128]{1,0:T(8,128)S(1)}, u32[]{:S(2)}, u32[]{:S(2)}) collective-permute-start(f32[152,128]{1,0:T(8,128)S(1)} %get-tuple-element.64), channel_id=1, source_target_pairs={{0,8},{1,9},{2,10},{3,11},{4,12},{5,13},{6,14},{7,15},{8,0},{9,1},... | collective-permute-start | bytes 233480 | tf_op jit(solution)/shard_map/ppermute | solution.py:779
  18.5 1.4 %copy-start.3 = (f32[64]{0:T(128)S(1)}, f32[64]{0:T(128)}, u32[]{:S(2)}) copy-start(f32[64]{0:T(128)} %param.8) | copy-start | bytes 772
  18.5 1.4 %copy-start.4 = (s32[64]{0:T(128)S(1)}, s32[64]{0:T(128)}, u32[]{:S(2)}) copy-start(s32[64]{0:T(128)} %param.9) | copy-start | bytes 772
  21.8 4.6 %collective-permute-start.9 = (f32[176,128]{1,0:T(8,128)S(1)}, f32[176,128]{1,0:T(8,128)S(1)}, u32[]{:S(2)}, u32[]{:S(2)}) collective-permute-start(f32[176,128]{1,0:T(8,128)S(1)} %get-tuple-element.71), channel_id=1, source_target_pairs={{0,1},{1,0},{2,3},{3,2},{4,5},{5,4},{6,7},{7,6},{8,9},{9,8},{10,11... | collective-permute-start | bytes 270344 | tf_op jit(solution)/shard_map/ppermute | solution.py:889
  24.4 4.2 %collective-permute-start.8 = (f32[104,128]{1,0:T(8,128)S(1)}, f32[104,128]{1,0:T(8,128)S(1)}, u32[]{:S(2)}, u32[]{:S(2)}) collective-permute-start(f32[104,128]{1,0:T(8,128)S(1)} %get-tuple-element.67), channel_id=1, source_target_pairs={{0,1},{1,0},{2,3},{3,2},{4,5},{5,4},{6,7},{7,6},{8,9},{9,8},{10,11... | collective-permute-start | bytes 159752 | tf_op jit(solution)/shard_map/ppermute | solution.py:902

commit v6 on v4

--- a/solution.py
+++ b/solution.py
@@ -279,7 +279,7 @@
         winds = [wind_z[eight(x * n, k)] for k in range(ROWS)]
         return [(change, eight(x * n, k), value) for k, value in enumerate(level_change(cells, winds, width))]
 
-    each(n, 2, along_z)
+    each(n, 4, along_z)
     begin, end = LO, n - HI
     for wind, edge, place in ((wind_x, edge_x, lambda i, k: k * n + i), (wind_y, edge_y, lambda i, k: i * n + k)):
 
@@ -325,7 +325,7 @@
         winds = [wind_z[eight(i * n, k)] for k in range(ROWS)]
         return [(halo_change, eight(i * n, k), value) for k, value in enumerate(level_change(cells, winds, width))]
 
-    each(LINES, 2, along_z)
+    each(LINES, LINES, along_z)
 
     def along_y(x):
         cells = [cell[rows_of(x * span + y)] for y in range(span)]
@@ -342,7 +342,7 @@
             stores.append((change, rows_of(x * reach + y + LO), own_change[rows_of(x * n + y)]))
         return stores
 
-    each(n, 2, along_y)
+    each(n, 4, along_y)
 
 
 def which(i, lower, upper):
@@ -405,7 +405,9 @@
     each(len(layers), len(layers), along_z)
 
 
-def x_kernel(n, parts, cell, change, wind_x, edge, second_ref, first_ref, mid, far_wind_x, side, side_wind_y, *scratch):
+def x_kernel(
+    n, parts, cell, change, wind_x, edge, second_ref, first_ref, mid, far_wind_x, side, side_wind_y, side_edge, *scratch
+):
     far, side_wind_z, side_change = scratch
     width, deep, tiles = groups(parts)
     half = tiles // 2
@@ -435,7 +437,17 @@
         winds = [side_wind_z[eight(i * n, k)] for k in range(ROWS)]
         return [(side_change, eight(i * n, k), value) for k, value in enumerate(level_change(cells, winds, width))]
 
-    each(LINES, 2, along_z)
+    each(LINES, LINES, along_z)
+    begin, end = LO, n - HI
+
+    def along_y(i):
+        cells = [side[rows_of(i * n + y)] for y in range(n)]
+        fluxes = line_fluxes(cells, [side_wind_y[rows_of(i * n + y)] for y in range(begin - 1, end + 1)])
+        at = [rows_of(i * n + y) for y in range(begin, end)]
+        stores = [(side_change, here, side_change[here] + value) for here, value in zip(at, changes(fluxes))]
+        return stores + [(side_edge, rows_of(i), fluxes[0]), (side_edge, rows_of(LINES + i), fluxes[-1])]
+
+    each(LINES, LINES, along_y)
 
     def along_x(y):
         outer = [far[rows_of(i * n + y)] for i in range(LINES)]
@@ -452,14 +464,14 @@
             stores.append((mid, rows_of((x + LO) * n + y), cells[PAD_LO + x] + value))
         return stores
 
-    each(n, 2, along_x)
+    each(n, 4, along_x)
 
 
 def main_kernel(n, parts, *refs):
     cell, change, wind_x, wind_y, wind_z, halo_wind_x, far_wind_y, inner, edge, inner_second = refs[:10]
-    mid, far_wind_x, side, side_wind_y, second_ref, first_ref, rate_ref, steps_ref = refs[10:18]
-    one, *out_refs = refs[18:21]
-    corner, corner_wind_x, edge_wind_y, second, fallen = refs[21:]
+    mid, far_wind_x, side, side_wind_y, side_edge, second_ref, first_ref, rate_ref, steps_ref = refs[10:19]
+    one, *out_refs = refs[19:22]
+    corner, corner_wind_x, edge_wind_y, second, fallen = refs[22:]
     deep, tiles = groups(parts)[1:]
     half = tiles // 2
     west, east = sides("gx", first_ref, second_ref)
@@ -495,11 +507,16 @@
         cells = corners[:LO] + [side[rows_of(i * n + y)] for y in range(n)] + corners[LO:]
         winds = [side_wind_y[rows_of(i * n + y)] for y in range(n)]
         winds = [edge_wind_y[rows_of(2 * i)]] + winds + [edge_wind_y[rows_of(2 * i + 1)]]
-        line = halo_line(i, n) + LO
-        return [
-            (one, rows_of(line * reach + LO + y), (mid[rows_of(line * n + y)] + value) * which(i, west_in, east_in))
-            for y, value in enumerate(line_change(cells, winds))
-        ]
+        low = line_fluxes(cells[: LO + begin + 1], winds[: begin + 1]) + [side_edge[rows_of(i)]]
+        high = [side_edge[rows_of(LINES + i)]] + line_fluxes(cells[LO + end - HI :], winds[end + 1 :])
+        values = dict(zip(range(begin), changes(low))) | dict(zip(range(end, n), changes(high)))
+        line, keep = halo_line(i, n) + LO, which(i, west_in, east_in)
+        stores = []
+        for y in range(n):
+            value = mid[rows_of(line * n + y)]
+            value = value + values[y] if y in values else value
+            stores.append((one, rows_of(line * reach + LO + y), value * keep))
+        return stores
 
     def along_x(i):
         line = halo_line(i, n) + LO
@@ -516,7 +533,7 @@
             stores.append((one, rows_of((x + LO) * reach + line), value))
         return stores
 
-    each(LINES, 2, along_y)
+    each(LINES, LINES, along_y)
     each(LINES, LINES, along_x)
     fall_layers(
         n, parts, 0, EARLY, one, cell, wind_x, far_wind_x, wind_y, far_wind_y, wind_z, inner_second, rate_ref, steps_ref,
@@ -840,9 +857,9 @@
         (cell, change, halo_wind_x, wind_y, far_wind_y, wind_z, edge_x),
         micros=0.9,
     )
-    mid, far_wind_x, side, side_wind_y = call(
+    mid, far_wind_x, side, side_wind_y, side_edge = call(
         functools.partial(x_kernel, n, parts),
-        [tiles_of(count) for count in (reach * n, (LINES + 2) * n, LINES * n, LINES * n)],
+        [tiles_of(count) for count in (reach * n, (LINES + 2) * n, LINES * n, LINES * n, 2 * LINES)],
         (cell, change, wind_x, near[1], *from_x),
         [tiles_of(LINES * n)] * 3,
         micros=1.7,
@@ -859,7 +876,7 @@
         [tiles_of(reach * reach)] + fallen(EARLY),
         (
             *(cell, change, wind_x, wind_y, wind_z, halo_wind_x, far_wind_y, *near),
-            *(mid, far_wind_x, side, side_wind_y, *corners, *fall),
+            *(mid, far_wind_x, side, side_wind_y, side_edge, *corners, *fall),
         ),
         [tiles_of(count) for count in (LINES * LINES, 2 * LINES, 2 * LINES, n * EARLY, n * EARLY)],
         micros=2.6,

time: 30.7 us -> 30.4 us (level)
  Pallas kernels: 12.5 us -> 11.9 us
    pallas_call x13, Pallas kernels: 12.5 us -> 11.9 us  [call(): pl.pallas_call(kernel, out_shape=outs, in_specs=[VMEM] * len(args), out_s...]
    ppermute x1, waiting for transfers between devices: 1.81 us -> 1.47 us  [per_device(): early_got = lax.ppermute(early[0], 'gz', [(0, 1), (1, 0)])]
    ppermute x6, waiting for transfers between devices: 1.73 us -> 2.06 us  [swap_neighbours(): return lax.ppermute(message, axes, pairs)]
  transfers between devices with their start and end apart: 10 -> 10, of which waited for: 4 -> 5; matrix products, arithmetic and copies ran while one was open for 2% -> 2% of each run, Pallas kernels for 27% -> 26%
where the time goes in v6:
time: 30.4 us; the launch traced here: 30.2 us
  Pallas kernels  11.9 us (39%)
  starting transfers between devices  10.7 us (35%)
  waiting for transfers between devices  5.36 us (18%)
  local copies, waits for them, and re-layouts  1.54 us (5%)
  between operations  0.77 us (3%)
    pallas_call x13, Pallas kernels, call(): pl.pallas_call(kernel, out_shape=outs, in_specs=[VMEM] * len(args), out_s...  11.9 us
    ppermute x6, starting transfers between devices, swap_neighbours(): return lax.ppermute(message, axes, pairs)  4.94 us
    ppermute x1, starting transfers between devices, per_device(): got = lax.ppermute(send, 'gz', [(0, 1), (1, 0)])  3.03 us
    ppermute x6, waiting for transfers between devices, swap_neighbours(): return lax.ppermute(message, axes, pairs)  2.06 us
    unnamed x13, local copies, waits for them, and re-layouts  1.54 us
    ppermute x1, starting transfers between devices, per_device(): early_got = lax.ppermute(early[0], 'gz', [(0, 1), (1, 0)])  1.49 us
    ppermute x1, waiting for transfers between devices, per_device(): early_got = lax.ppermute(early[0], 'gz', [(0, 1), (1, 0)])  1.47 us
    ppermute x1, waiting for transfers between devices, per_device(): got_wind = lax.ppermute(own_wind, 'gz', [(0, 1), (1, 0)])  1.31 us
  transfers between devices with their start and end apart: 10, of which 5 were waited for; matrix products, arithmetic and copies ran while one was open for 2% of the time, Pallas kernels for 26%

profile of v6, /device:TPU:0, one launch (start us, length us, event | category | flops | bytes accessed | tf_op | source)
XLA Modules:
  0.0 30.2 jit_solution(445368372998291254)
XLA Ops:
  0.6 0.0 copy-start.1
  0.6 1.0 %copy-done.1 = f32[8,8,16,64]{3,2,1,0:T(8,128)S(1)} copy-done((f32[8,8,16,64]{3,2,1,0:T(8,128)S(1)}, f32[8,8,16,64]{3,2,1,0:T(8,128)}, u32[]{:S(2)}) %copy-start.1) | copy-done | bytes 262168
  1.7 0.0 copy-start.2
  1.7 0.0 copy-start.5
  1.7 0.3 shard_map.77
  2.0 0.0 copy-start
  2.0 3.0 %collective-permute-start = (f32[256,128]{1,0:T(8,128)S(1)}, f32[256,128]{1,0:T(8,128)S(1)}, u32[]{:S(2)}, u32[]{:S(2)}) collective-permute-start(f32[256,128]{1,0:T(8,128)S(1)} %get-tuple-element.39), channel_id=1, source_target_pairs={{0,1},{1,0},{2,3},{3,2},{4,5},{5,4},{6,7},{7,6},{8,9},{9,8},{10,11... | collective-permute-start | bytes 393224 | tf_op jit(solution)/shard_map/ppermute | solution.py:805
  5.0 0.0 copy-done.2
  5.0 0.1 shard_map.78.own_wind_ref
  5.1 0.6 %collective-permute-start.1 = (f32[24,128]{1,0:T(8,128)S(1)}, f32[24,128]{1,0:T(8,128)S(1)}, u32[]{:S(2)}, u32[]{:S(2)}) collective-permute-start(f32[24,128]{1,0:T(8,128)S(1)} %shard_map.78.own_wind_ref), channel_id=1, source_target_pairs={{0,1},{1,0},{2,3},{3,2},{4,5},{5,4},{6,7},{7,6},{8,9},{9,8},{10,11... | collective-permute-start | bytes 36872 | tf_op jit(solution)/shard_map/ppermute | solution.py:807
  5.7 0.0 copy-done.5
  5.7 0.5 %copy.8.gain_ref = bf16[4096,64]{1,0:T(8,128)(2,1)S(1)} copy(bf16[4096,64]{0,1:T(8,128)(2,1)S(1)} %copy-done.5) | data formatting | bytes 1048576 | tf_op args[4]
  6.2 0.0 copy-done
  6.2 1.4 %shard_map.79 = (bf16[4224,128]{1,0:T(8,128)(2,1)S(1)}, bf16[128,128]{1,0:T(8,128)(2,1)S(1)}) custom-call(bf16[4096,64]{1,0:T(8,128)(2,1)S(1)} %copy.8.gain_ref, bf16[64,64]{1,0:T(8,128)(2,1)S(1)} %copy-done), custom_call_target="tpu_custom_call" | custom-call | flops 22000000 | bytes 72000 | tf_op jit(solution)/shard_map/pallas_call | solution.py:749
  7.5 1.3 %collective-permute-done.1.got_wind_ref = f32[24,128]{1,0:T(8,128)S(1)} collective-permute-done((f32[24,128]{1,0:T(8,128)S(1)}, f32[24,128]{1,0:T(8,128)S(1)}, u32[]{:S(2)}, u32[]{:S(2)}) %collective-permute-start.1) | collective-permute-done | bytes 12320 | tf_op jit(solution)/shard_map/ppermute | solution.py:807
  8.9 0.0 collective-permute-done.got_ref
  8.9 0.3 shard_map.80
  9.1 1.8 %collective-permute-start.2 = (f32[408,128]{1,0:T(8,128)S(1)}, f32[408,128]{1,0:T(8,128)S(1)}, u32[]{:S(2)}, u32[]{:S(2)}) collective-permute-start(f32[408,128]{1,0:T(8,128)S(1)} %get-tuple-element.42), channel_id=1, source_target_pairs={{0,2},{1,3},{2,0},{3,1},{4,6},{5,7},{6,4},{7,5},{8,10},{9,11},{10,... | collective-permute-start | bytes 626696 | tf_op jit(solution)/shard_map/ppermute | solution.py:779
  10.9 0.0 collective-permute-start.3
  10.9 1.5 %collective-permute-start.4 = (f32[408,128]{1,0:T(8,128)S(1)}, f32[408,128]{1,0:T(8,128)S(1)}, u32[]{:S(2)}, u32[]{:S(2)}) collective-permute-start(f32[408,128]{1,0:T(8,128)S(1)} %get-tuple-element.57), channel_id=1, source_target_pairs={{0,1},{1,0},{2,3},{3,2},{4,5},{5,4},{6,7},{7,6},{8,16},{9,17},{10,... | collective-permute-start | bytes 626696 | tf_op jit(solution)/shard_map/ppermute | solution.py:779
  12.4 0.1 collective-permute-start.5
  12.5 1.3 %shard_map.81 = (f32[512,128]{1,0:T(8,128)S(1)}, f32[512,128]{1,0:T(8,128)S(1)}, f32[512,128]{1,0:T(8,128)S(1)}, f32[512,128]{1,0:T(8,128)S(1)}, f32[128,128]{1,0:T(8,128)S(1)}, /*index=5*/f32[128,128]{1,0:T(8,128)S(1)}) custom-call(f32[560,128]{1,0:T(8,128)S(1)} %get-tuple-element.41.block_ref), custom_call_target="tpu_custom_call" | custom-call | flops 1760000000 | bytes 5760000 | tf_op jit(solution)/shard_map/pallas_call | solution.py:749
  13.8 1.7 %collective-permute-done.2.first_ref = f32[408,128]{1,0:T(8,128)S(1)} collective-permute-done((f32[408,128]{1,0:T(8,128)S(1)}, f32[408,128]{1,0:T(8,128)S(1)}, u32[]{:S(2)}, u32[]{:S(2)}) %collective-permute-start.2) | collective-permute-done | bytes 208928 | tf_op jit(solution)/shard_map/ppermute | solution.py:779
  15.4 0.0 collective-permute-done.3.second_ref
  15.5 1.5 %collective-permute-start.6 = (f32[152,128]{1,0:T(8,128)S(1)}, f32[152,128]{1,0:T(8,128)S(1)}, u32[]{:S(2)}, u32[]{:S(2)}) collective-permute-start(f32[152,128]{1,0:T(8,128)S(1)} %get-tuple-element.64), channel_id=1, source_target_pairs={{0,1},{1,0},{2,3},{3,2},{4,5},{5,4},{6,7},{7,6},{8,16},{9,17},{10,... | collective-permute-start | bytes 233480 | tf_op jit(solution)/shard_map/ppermute | solution.py:779
  17.0 0.1 collective-permute-start.7
  17.1 1.0 %shard_map.82 = (f32[1152,128]{1,0:T(8,128)S(1)}, f32[832,128]{1,0:T(8,128)S(1)}, f32[320,128]{1,0:T(8,128)S(1)}, f32[448,128]{1,0:T(8,128)S(1)}) custom-call(f32[560,128]{1,0:T(8,128)S(1)} %get-tuple-element.41.block_ref, f32[408,128]{1,0:T(8,128)S(1)} %collective-permute-done.2.first_ref, f32[408,128]{1,0:T(8,128)S(1)} %collective-permute-done.3.second_ref, ...), custom_call_target="tpu_custom_call" | custom-call | flops 2200000000 | bytes 7200000 | tf_op jit(solution)/shard_map/pallas_call | solution.py:749
  18.0 0.5 %shard_map.83 = (f32[312,128]{1,0:T(8,128)S(1)}, f32[208,128]{1,0:T(8,128)S(1)}, f32[192,128]{1,0:T(8,128)S(1)}) custom-call(f32[1152,128]{1,0:T(8,128)S(1)} %get-tuple-element.47.cell.refs_0_, f32[832,128]{1,0:T(8,128)S(1)} %get-tuple-element.48.change.refs_1_, f32[320,128]{1,0:T(8,128)S(1)} %get-tuple-element.51.halo_wind_x.refs_5_, ...), custom_call_target="tpu_custom_call" | custom-call | flops 990000000 | bytes 3240000 | tf_op jit(solution)/shard_map/pallas_call | solution.py:749
  18.5 0.0 collective-permute-done.4.second_ref
  18.5 0.0 collective-permute-done.5.first_ref
  18.5 0.0 copy-start.3
  18.5 0.0 copy-start.4
  18.5 1.0 %shard_map.84 = (f32[832,128]{1,0:T(8,128)S(1)}, f32[448,128]{1,0:T(8,128)S(1)}, f32[320,128]{1,0:T(8,128)S(1)}, f32[320,128]{1,0:T(8,128)S(1)}, f32[80,128]{1,0:T(8,128)S(1)}) custom-call(f32[1152,128]{1,0:T(8,128)S(1)} %get-tuple-element.47.cell.refs_0_, f32[832,128]{1,0:T(8,128)S(1)} %get-tuple-element.48.change.refs_1_, ...), custom_call_target="tpu_custom_call" | custom-call | flops 1870000000 | bytes 6120000 | tf_op jit(solution)/shard_map/pallas_call | solution.py:749
  19.6 0.4 %collective-permute-done.6.refs_15_ = f32[152,128]{1,0:T(8,128)S(1)} collective-permute-done((f32[152,128]{1,0:T(8,128)S(1)}, f32[152,128]{1,0:T(8,128)S(1)}, u32[]{:S(2)}, u32[]{:S(2)}) %collective-permute-start.6) | collective-permute-done | bytes 77856 | tf_op jit(solution)/shard_map/ppermute | solution.py:779
  19.9 0.0 collective-permute-done.7.refs_16_
  19.9 0.0 copy-done.3
  19.9 0.0 copy-done.4
  20.0 1.8 %shard_map.86 = (f32[1352,128]{1,0:T(8,128)S(1)}, f32[176,128]{1,0:T(8,128)S(1)}, f32[176,128]{1,0:T(8,128)S(1)}) custom-call(f32[1152,128]{1,0:T(8,128)S(1)} %get-tuple-element.47.cell.refs_0_, f32[832,128]{1,0:T(8,128)S(1)} %get-tuple-element.48.change.refs_1_, f32[512,128]{1,0:T(8,128)S(1)} %get-tuple-element.49.wind_x.refs_2_, ...), custom_call_target="tpu_custom_call" | custom-call | flops 2860000000 | bytes 9360000 | tf_op jit(solution)/shard_map/pallas_call | solution.py:749
  21.7 1.5 %collective-permute-start.9 = (f32[176,128]{1,0:T(8,128)S(1)}, f32[176,128]{1,0:T(8,128)S(1)}, u32[]{:S(2)}, u32[]{:S(2)}) collective-permute-start(f32[176,128]{1,0:T(8,128)S(1)} %get-tuple-element.71), channel_id=1, source_target_pairs={{0,1},{1,0},{2,3},{3,2},{4,5},{5,4},{6,7},{7,6},{8,9},{9,8},{10,11... | collective-permute-start | bytes 270344 | tf_op jit(solution)/shard_map/ppermute | solution.py:885
  23.2 1.0 %shard_map.87 = (f32[104,128]{1,0:T(8,128)S(1)}, f32[104,128]{1,0:T(8,128)S(1)}) custom-call(f32[1352,128]{1,0:T(8,128)S(1)} %get-tuple-element.66.one, f32[1152,128]{1,0:T(8,128)S(1)} %get-tuple-element.47.cell.refs_0_, f32[512,128]{1,0:T(8,128)S(1)} %get-tuple-element.49.wind_x.refs_2_, f32[448,128]{1,0:T(8,128)S(1)} %get-tuple-element.60.refs_11_.far_wind_x, ...), custom_call_target="tpu_custom_call" | custom-call | flops 770000000 | bytes 2520000 | tf_op jit(solution)/shard_map/pallas_call | solution.py:749
  24.3 0.7 %collective-permute-start.8 = (f32[104,128]{1,0:T(8,128)S(1)}, f32[104,128]{1,0:T(8,128)S(1)}, u32[]{:S(2)}, u32[]{:S(2)}) collective-permute-start(f32[104,128]{1,0:T(8,128)S(1)} %get-tuple-element.68), channel_id=1, source_target_pairs={{0,1},{1,0},{2,3},{3,2},{4,5},{5,4},{6,7},{7,6},{8,9},{9,8},{10,11... | collective-permute-start | bytes 159752 | tf_op jit(solution)/shard_map/ppermute | solution.py:898
  25.0 1.5 %collective-permute-done.9.got_ref = f32[176,128]{1,0:T(8,128)S(1)} collective-permute-done((f32[176,128]{1,0:T(8,128)S(1)}, f32[176,128]{1,0:T(8,128)S(1)}, u32[]{:S(2)}, u32[]{:S(2)}) %collective-permute-start.9) | collective-permute-done | bytes 90144 | tf_op jit(solution)/shard_map/ppermute | solution.py:885
  26.4 1.5 %shard_map.88 = (f32[5,8,16,64]{3,2,1,0:T(8,128)S(1)}, f32[5,4,64]{2,1,0:T(4,128)S(1)}) custom-call(f32[176,128]{1,0:T(8,128)S(1)} %get-tuple-element.70.keep_ref, f32[176,128]{1,0:T(8,128)S(1)} %collective-permute-done.9.got_ref, bf16[4224,128]{1,0:T(8,128)(2,1)S(1)} %get-tuple-element.69.pairs_ref, bf16[128,128]{1,0:T(8,128)(2,1)S(1)} %get-tuple-element.40.lost_ref), custom_call_target="tpu_custom_call" | custom-call | flops 1980000000 | bytes 6480000 | tf_op jit(solution)/shard_map/pallas_call | solution.py:749
  28.0 0.5 %collective-permute-done.8.got_ref = f32[104,128]{1,0:T(8,128)S(1)} collective-permute-done((f32[104,128]{1,0:T(8,128)S(1)}, f32[104,128]{1,0:T(8,128)S(1)}, u32[]{:S(2)}, u32[]{:S(2)}) %collective-permute-start.8) | collective-permute-done | bytes 53280 | tf_op jit(solution)/shard_map/ppermute | solution.py:898
  28.5 1.7 %shard_map.89 = (f32[8,8,16,64]{3,2,1,0:T(8,128)}, f32[8,4,64]{2,1,0:T(4,128)}) custom-call(f32[104,128]{1,0:T(8,128)S(1)} %get-tuple-element.67.keep_ref, f32[104,128]{1,0:T(8,128)S(1)} %collective-permute-done.8.got_ref, bf16[4224,128]{1,0:T(8,128)(2,1)S(1)} %get-tuple-element.69.pairs_ref, bf16[128,128]{1,0:T(8,128)(2,1)S(1)} %get-tuple-element.40.lost_ref, ...), custom_call_target="tpu_custom_call" | custom-call | flops 1320000000 | bytes 4320000 | tf_op jit(solution)/shard_map/pallas_call | solution.py:749
  (1 shorter events, 0.0 us)
Async XLA Ops:
  0.6 1.0 %copy-start.1 = (f32[8,8,16,64]{3,2,1,0:T(8,128)S(1)}, f32[8,8,16,64]{3,2,1,0:T(8,128)}, u32[]{:S(2)}) copy-start(f32[8,8,16,64]{3,2,1,0:T(8,128)} %mass_ref.1) | copy-start | bytes 786436
  1.7 3.3 %copy-start.2 = (f32[3,8,8,16]{3,2,1,0:T(8,128)S(1)}, f32[3,8,8,16]{3,2,1,0:T(8,128)}, u32[]{:S(2)}) copy-start(f32[3,8,8,16]{3,2,1,0:T(8,128)} %wind_ref.1) | copy-start | bytes 36868
  1.7 4.0 %copy-start.5 = (bf16[4096,64]{0,1:T(8,128)(2,1)S(1)}, bf16[4096,64]{0,1:T(8,128)(2,1)}, u32[]{:S(2)}) copy-start(bf16[4096,64]{0,1:T(8,128)(2,1)} %param.10) | copy-start | bytes 1572868
  2.0 4.2 %copy-start = (bf16[64,64]{1,0:T(8,128)(2,1)S(1)}, bf16[64,64]{1,0:T(8,128)(2,1)}, u32[]{:S(2)}) copy-start(bf16[64,64]{1,0:T(8,128)(2,1)} %loss_ref.1) | copy-start | bytes 24580
  2.0 6.9 %collective-permute-start = (f32[256,128]{1,0:T(8,128)S(1)}, f32[256,128]{1,0:T(8,128)S(1)}, u32[]{:S(2)}, u32[]{:S(2)}) collective-permute-start(f32[256,128]{1,0:T(8,128)S(1)} %get-tuple-element.39), channel_id=1, source_target_pairs={{0,1},{1,0},{2,3},{3,2},{4,5},{5,4},{6,7},{7,6},{8,9},{9,8},{10,11... | collective-permute-start | bytes 393224 | tf_op jit(solution)/shard_map/ppermute | solution.py:805
  5.1 3.7 %collective-permute-start.1 = (f32[24,128]{1,0:T(8,128)S(1)}, f32[24,128]{1,0:T(8,128)S(1)}, u32[]{:S(2)}, u32[]{:S(2)}) collective-permute-start(f32[24,128]{1,0:T(8,128)S(1)} %shard_map.78.own_wind_ref), channel_id=1, source_target_pairs={{0,1},{1,0},{2,3},{3,2},{4,5},{5,4},{6,7},{7,6},{8,9},{9,8},{10,11... | collective-permute-start | bytes 36872 | tf_op jit(solution)/shard_map/ppermute | solution.py:807
  9.1 6.3 %collective-permute-start.2 = (f32[408,128]{1,0:T(8,128)S(1)}, f32[408,128]{1,0:T(8,128)S(1)}, u32[]{:S(2)}, u32[]{:S(2)}) collective-permute-start(f32[408,128]{1,0:T(8,128)S(1)} %get-tuple-element.42), channel_id=1, source_target_pairs={{0,2},{1,3},{2,0},{3,1},{4,6},{5,7},{6,4},{7,5},{8,10},{9,11},{10,... | collective-permute-start | bytes 626696 | tf_op jit(solution)/shard_map/ppermute | solution.py:779
  10.9 4.6 %collective-permute-start.3 = (f32[408,128]{1,0:T(8,128)S(1)}, f32[408,128]{1,0:T(8,128)S(1)}, u32[]{:S(2)}, u32[]{:S(2)}) collective-permute-start(f32[408,128]{1,0:T(8,128)S(1)} %get-tuple-element.43), channel_id=1, source_target_pairs={{0,8},{1,9},{2,4},{3,5},{4,2},{5,3},{6,14},{7,15},{8,0},{9,1},{10,... | collective-permute-start | bytes 626696 | tf_op jit(solution)/shard_map/ppermute | solution.py:779
  10.9 7.6 %collective-permute-start.4 = (f32[408,128]{1,0:T(8,128)S(1)}, f32[408,128]{1,0:T(8,128)S(1)}, u32[]{:S(2)}, u32[]{:S(2)}) collective-permute-start(f32[408,128]{1,0:T(8,128)S(1)} %get-tuple-element.57), channel_id=1, source_target_pairs={{0,1},{1,0},{2,3},{3,2},{4,5},{5,4},{6,7},{7,6},{8,16},{9,17},{10,... | collective-permute-start | bytes 626696 | tf_op jit(solution)/shard_map/ppermute | solution.py:779
  12.4 6.1 %collective-permute-start.5 = (f32[408,128]{1,0:T(8,128)S(1)}, f32[408,128]{1,0:T(8,128)S(1)}, u32[]{:S(2)}, u32[]{:S(2)}) collective-permute-start(f32[408,128]{1,0:T(8,128)S(1)} %get-tuple-element.58), channel_id=1, source_target_pairs={{0,8},{1,9},{2,10},{3,11},{4,12},{5,13},{6,14},{7,15},{8,0},{9,1},... | collective-permute-start | bytes 626696 | tf_op jit(solution)/shard_map/ppermute | solution.py:779
  15.5 4.5 %collective-permute-start.6 = (f32[152,128]{1,0:T(8,128)S(1)}, f32[152,128]{1,0:T(8,128)S(1)}, u32[]{:S(2)}, u32[]{:S(2)}) collective-permute-start(f32[152,128]{1,0:T(8,128)S(1)} %get-tuple-element.64), channel_id=1, source_target_pairs={{0,1},{1,0},{2,3},{3,2},{4,5},{5,4},{6,7},{7,6},{8,16},{9,17},{10,... | collective-permute-start | bytes 233480 | tf_op jit(solution)/shard_map/ppermute | solution.py:779
  17.0 3.0 %collective-permute-start.7 = (f32[152,128]{1,0:T(8,128)S(1)}, f32[152,128]{1,0:T(8,128)S(1)}, u32[]{:S(2)}, u32[]{:S(2)}) collective-permute-start(f32[152,128]{1,0:T(8,128)S(1)} %get-tuple-element.65), channel_id=1, source_target_pairs={{0,8},{1,9},{2,10},{3,11},{4,12},{5,13},{6,14},{7,15},{8,0},{9,1},... | collective-permute-start | bytes 233480 | tf_op jit(solution)/shard_map/ppermute | solution.py:779
  18.5 1.4 %copy-start.3 = (f32[64]{0:T(128)S(1)}, f32[64]{0:T(128)}, u32[]{:S(2)}) copy-start(f32[64]{0:T(128)} %param.8) | copy-start | bytes 772
  18.5 1.4 %copy-start.4 = (s32[64]{0:T(128)S(1)}, s32[64]{0:T(128)}, u32[]{:S(2)}) copy-start(s32[64]{0:T(128)} %param.9) | copy-start | bytes 772
  21.7 4.7 %collective-permute-start.9 = (f32[176,128]{1,0:T(8,128)S(1)}, f32[176,128]{1,0:T(8,128)S(1)}, u32[]{:S(2)}, u32[]{:S(2)}) collective-permute-start(f32[176,128]{1,0:T(8,128)S(1)} %get-tuple-element.71), channel_id=1, source_target_pairs={{0,1},{1,0},{2,3},{3,2},{4,5},{5,4},{6,7},{7,6},{8,9},{9,8},{10,11... | collective-permute-start | bytes 270344 | tf_op jit(solution)/shard_map/ppermute | solution.py:885
  24.3 4.2 %collective-permute-start.8 = (f32[104,128]{1,0:T(8,128)S(1)}, f32[104,128]{1,0:T(8,128)S(1)}, u32[]{:S(2)}, u32[]{:S(2)}) collective-permute-start(f32[104,128]{1,0:T(8,128)S(1)} %get-tuple-element.68), channel_id=1, source_target_pairs={{0,1},{1,0},{2,3},{3,2},{4,5},{5,4},{6,7},{7,6},{8,9},{9,8},{10,11... | collective-permute-start | bytes 159752 | tf_op jit(solution)/shard_map/ppermute | solution.py:898

commit v7 on v6

--- a/solution.py
+++ b/solution.py
@@ -406,7 +406,8 @@
 
 
 def x_kernel(
-    n, parts, cell, change, wind_x, edge, second_ref, first_ref, mid, far_wind_x, side, side_wind_y, side_edge, *scratch
+    n, parts, cell, change, wind_x, inner, edge, inner_second, second_ref, first_ref,
+    mid, far_wind_x, side, side_wind_y, side_edge, ready_second, second_edge, *scratch
 ):
     far, side_wind_z, side_change = scratch
     width, deep, tiles = groups(parts)
@@ -466,12 +467,23 @@
 
     each(n, 4, along_x)
 
+    def second_x(y):
+        cells = [mid[rows_of((x + LO) * n + y)] for x in range(begin)]
+        cells += [inner[rows_of(i * reach + LO + y)] for i in range(end - begin)]
+        cells += [mid[rows_of((x + LO) * n + y)] for x in range(end, n)]
+        fluxes = line_fluxes(cells, [wind_x[rows_of(x * n + y)] for x in range(begin - 1, end + 1)])
+        at = [rows_of(i * n + y) for i in range(end - begin)]
+        stores = [(ready_second, here, inner_second[here] + value) for here, value in zip(at, changes(fluxes))]
+        return stores + [(second_edge, rows_of(y), fluxes[0]), (second_edge, rows_of(n + y), fluxes[-1])]
+
+    each(n, 4, second_x)
+
 
 def main_kernel(n, parts, *refs):
-    cell, change, wind_x, wind_y, wind_z, halo_wind_x, far_wind_y, inner, edge, inner_second = refs[:10]
-    mid, far_wind_x, side, side_wind_y, side_edge, second_ref, first_ref, rate_ref, steps_ref = refs[10:19]
-    one, *out_refs = refs[19:22]
-    corner, corner_wind_x, edge_wind_y, second, fallen = refs[22:]
+    cell, change, wind_x, wind_y, wind_z, halo_wind_x, far_wind_y, inner, edge = refs[:9]
+    mid, far_wind_x, side, side_wind_y, side_edge, inner_second, second_edge = refs[9:16]
+    second_ref, first_ref, rate_ref, steps_ref, one, *out_refs = refs[16:23]
+    corner, corner_wind_x, edge_wind_y, second, fallen = refs[23:]
     deep, tiles = groups(parts)[1:]
     half = tiles // 2
     west, east = sides("gx", first_ref, second_ref)
@@ -536,22 +548,22 @@
     each(LINES, LINES, along_y)
     each(LINES, LINES, along_x)
     fall_layers(
-        n, parts, 0, EARLY, one, cell, wind_x, far_wind_x, wind_y, far_wind_y, wind_z, inner_second, rate_ref, steps_ref,
+        n, parts, 0, EARLY, one, cell, wind_x, far_wind_x, wind_y, far_wind_y, wind_z, inner_second, second_edge, rate_ref, steps_ref,
         out_refs, second, fallen,
     )
 
 
 def late_kernel(
-    n, parts, one, cell, wind_x, far_wind_x, wind_y, far_wind_y, wind_z, inner_second, rate_ref, steps_ref, *refs
+    n, parts, one, cell, wind_x, far_wind_x, wind_y, far_wind_y, wind_z, inner_second, second_edge, rate_ref, steps_ref, *refs
 ):
     fall_layers(
-        n, parts, EARLY, n, one, cell, wind_x, far_wind_x, wind_y, far_wind_y, wind_z, inner_second, rate_ref, steps_ref,
+        n, parts, EARLY, n, one, cell, wind_x, far_wind_x, wind_y, far_wind_y, wind_z, inner_second, second_edge, rate_ref, steps_ref,
         refs[:2], *refs[2:],
     )
 
 
 def fall_layers(
-    n, parts, begin, end, one, cell, wind_x, far_wind_x, wind_y, far_wind_y, wind_z, inner_second, rate_ref, steps_ref,
+    n, parts, begin, end, one, cell, wind_x, far_wind_x, wind_y, far_wind_y, wind_z, inner_second, second_edge, rate_ref, steps_ref,
     out_refs, second, fallen,
 ):
     width = groups(parts)[0]
@@ -564,17 +576,24 @@
     second_y_z(n, width, left, begin, one, -LO, wind_y, far_wind_y, wind_z, second)
 
     def along_x(y):
-        cells = [one[rows_of(x * reach + LO + y)] for x in range(begin, end + LINES)]
-        winds = [wind_x[rows_of(x * n + y)] for x in range(max(begin - 1, 0), min(end + 1, n))]
+        values = {}
         if begin == 0:
-            winds = [far_wind_x[rows_of(LO * n + y)]] + winds
+            cells = [one[rows_of((x + LO) * reach + LO + y)] for x in range(-LO, LO + 1)]
+            winds = [far_wind_x[rows_of(LO * n + y)]] + [wind_x[rows_of(x * n + y)] for x in range(LO)]
+            fluxes = line_fluxes(cells, winds) + [second_edge[rows_of(y)]]
+            values |= zip(range(LO), changes(fluxes))
         if end == n:
-            winds = winds + [far_wind_x[rows_of((LO + 1) * n + y)]]
+            cells = [one[rows_of((x + LO) * reach + LO + y)] for x in range(n - 2 * HI, n + HI)]
+            winds = [wind_x[rows_of(x * n + y)] for x in range(n - HI, n)] + [far_wind_x[rows_of((LO + 1) * n + y)]]
+            fluxes = [second_edge[rows_of(n + y)]] + line_fluxes(cells, winds)
+            values |= zip(range(n - HI, n), changes(fluxes))
         stores = []
-        for i, value in enumerate(line_change(cells, winds)):
-            value = cells[i + LO] + (value + second[rows_of(i * n + y)])
-            value = 0.5 * cell[rows_of((begin + i) * span + PAD_LO + y)] + 0.5 * value
-            stores.append((fallen, rows_of(i * n + y), value))
+        for x in range(begin, end):
+            at = rows_of((x - begin) * n + y)
+            value = second[at] + values[x] if x in values else second[at]
+            value = one[rows_of((x + LO) * reach + LO + y)] + value
+            value = 0.5 * cell[rows_of(x * span + PAD_LO + y)] + 0.5 * value
+            stores.append((fallen, at, value))
         return stores
 
     each(n, 4, along_x)
@@ -857,10 +876,10 @@
         (cell, change, halo_wind_x, wind_y, far_wind_y, wind_z, edge_x),
         micros=0.9,
     )
-    mid, far_wind_x, side, side_wind_y, side_edge = call(
+    mid, far_wind_x, side, side_wind_y, side_edge, ready_second, second_edge = call(
         functools.partial(x_kernel, n, parts),
-        [tiles_of(count) for count in (reach * n, (LINES + 2) * n, LINES * n, LINES * n, 2 * LINES)],
-        (cell, change, wind_x, near[1], *from_x),
+        [tiles_of(count) for count in (reach * n, (LINES + 2) * n, LINES * n, LINES * n, 2 * LINES, inner * n, 2 * n)],
+        (cell, change, wind_x, *near, *from_x),
         [tiles_of(LINES * n)] * 3,
         micros=1.7,
     )
@@ -875,8 +894,8 @@
         functools.partial(main_kernel, n, parts),
         [tiles_of(reach * reach)] + fallen(EARLY),
         (
-            *(cell, change, wind_x, wind_y, wind_z, halo_wind_x, far_wind_y, *near),
-            *(mid, far_wind_x, side, side_wind_y, side_edge, *corners, *fall),
+            *(cell, change, wind_x, wind_y, wind_z, halo_wind_x, far_wind_y, *near[:2]),
+            *(mid, far_wind_x, side, side_wind_y, side_edge, ready_second, second_edge, *corners, *fall),
         ),
         [tiles_of(count) for count in (LINES * LINES, 2 * LINES, 2 * LINES, n * EARLY, n * EARLY)],
         micros=2.6,
@@ -886,7 +905,7 @@
     late = call(
         functools.partial(late_kernel, n, parts),
         fallen(n - EARLY),
-        (one, cell, wind_x, far_wind_x, wind_y, far_wind_y, wind_z, near[2], *fall),
+        (one, cell, wind_x, far_wind_x, wind_y, far_wind_y, wind_z, ready_second, second_edge, *fall),
         [tiles_of(n * (n - EARLY))] * 2,
         micros=0.7,
     )

time: 30.4 us -> 30.2 us (level)
    ppermute x1, waiting for transfers between devices: 0.52 us -> 0.18 us  [per_device(): late_got = lax.ppermute(late[0], 'gz', [(0, 1), (1, 0)])]
    ppermute x1, waiting for transfers between devices: 1.47 us -> 1.81 us  [per_device(): early_got = lax.ppermute(early[0], 'gz', [(0, 1), (1, 0)])]
where the time goes in v7:
time: 30.2 us; the launch traced here: 30 us
  Pallas kernels  11.9 us (39%)
  starting transfers between devices  10.7 us (35%)
  waiting for transfers between devices  5.15 us (17%)
  local copies, waits for them, and re-layouts  1.54 us (5%)
  between operations  0.77 us (3%)
    pallas_call x13, Pallas kernels, call(): pl.pallas_call(kernel, out_shape=outs, in_specs=[VMEM] * len(args), out_s...  11.9 us
    ppermute x6, starting transfers between devices, swap_neighbours(): return lax.ppermute(message, axes, pairs)  4.94 us
    ppermute x1, starting transfers between devices, per_device(): got = lax.ppermute(send, 'gz', [(0, 1), (1, 0)])  3.03 us
    ppermute x6, waiting for transfers between devices, swap_neighbours(): return lax.ppermute(message, axes, pairs)  1.86 us
    ppermute x1, waiting for transfers between devices, per_device(): early_got = lax.ppermute(early[0], 'gz', [(0, 1), (1, 0)])  1.81 us
    unnamed x13, local copies, waits for them, and re-layouts  1.54 us
    ppermute x1, starting transfers between devices, per_device(): early_got = lax.ppermute(early[0], 'gz', [(0, 1), (1, 0)])  1.49 us
    ppermute x1, waiting for transfers between devices, per_device(): got_wind = lax.ppermute(own_wind, 'gz', [(0, 1), (1, 0)])  1.31 us
  transfers between devices with their start and end apart: 10, of which 5 were waited for; matrix products, arithmetic and copies ran while one was open for 2% of the time, Pallas kernels for 26%

profile of v7, /device:TPU:0, one launch (start us, length us, event | category | flops | bytes accessed | tf_op | source)
XLA Modules:
  0.0 30.0 jit_solution(17303088191147249424)
XLA Ops:
  0.6 0.0 copy-start.1
  0.6 1.0 %copy-done.1 = f32[8,8,16,64]{3,2,1,0:T(8,128)S(1)} copy-done((f32[8,8,16,64]{3,2,1,0:T(8,128)S(1)}, f32[8,8,16,64]{3,2,1,0:T(8,128)}, u32[]{:S(2)}) %copy-start.1) | copy-done | bytes 262168
  1.7 0.0 copy-start.2
  1.7 0.0 copy-start.5
  1.7 0.3 shard_map.77
  2.0 0.0 copy-start
  2.0 3.0 %collective-permute-start = (f32[256,128]{1,0:T(8,128)S(1)}, f32[256,128]{1,0:T(8,128)S(1)}, u32[]{:S(2)}, u32[]{:S(2)}) collective-permute-start(f32[256,128]{1,0:T(8,128)S(1)} %get-tuple-element.41), channel_id=1, source_target_pairs={{0,1},{1,0},{2,3},{3,2},{4,5},{5,4},{6,7},{7,6},{8,9},{9,8},{10,11... | collective-permute-start | bytes 393224 | tf_op jit(solution)/shard_map/ppermute | solution.py:824
  5.0 0.0 copy-done.2
  5.0 0.1 shard_map.78.own_wind_ref
  5.1 0.6 %collective-permute-start.1 = (f32[24,128]{1,0:T(8,128)S(1)}, f32[24,128]{1,0:T(8,128)S(1)}, u32[]{:S(2)}, u32[]{:S(2)}) collective-permute-start(f32[24,128]{1,0:T(8,128)S(1)} %shard_map.78.own_wind_ref), channel_id=1, source_target_pairs={{0,1},{1,0},{2,3},{3,2},{4,5},{5,4},{6,7},{7,6},{8,9},{9,8},{10,11... | collective-permute-start | bytes 36872 | tf_op jit(solution)/shard_map/ppermute | solution.py:826
  5.7 0.0 copy-done.5
  5.7 0.5 %copy.8.gain_ref = bf16[4096,64]{1,0:T(8,128)(2,1)S(1)} copy(bf16[4096,64]{0,1:T(8,128)(2,1)S(1)} %copy-done.5) | data formatting | bytes 1048576 | tf_op args[4]
  6.2 0.0 copy-done
  6.2 1.4 %shard_map.79 = (bf16[4224,128]{1,0:T(8,128)(2,1)S(1)}, bf16[128,128]{1,0:T(8,128)(2,1)S(1)}) custom-call(bf16[4096,64]{1,0:T(8,128)(2,1)S(1)} %copy.8.gain_ref, bf16[64,64]{1,0:T(8,128)(2,1)S(1)} %copy-done), custom_call_target="tpu_custom_call" | custom-call | flops 22000000 | bytes 72000 | tf_op jit(solution)/shard_map/pallas_call | solution.py:768
  7.5 1.3 %collective-permute-done.1.got_wind_ref = f32[24,128]{1,0:T(8,128)S(1)} collective-permute-done((f32[24,128]{1,0:T(8,128)S(1)}, f32[24,128]{1,0:T(8,128)S(1)}, u32[]{:S(2)}, u32[]{:S(2)}) %collective-permute-start.1) | collective-permute-done | bytes 12320 | tf_op jit(solution)/shard_map/ppermute | solution.py:826
  8.9 0.0 collective-permute-done.got_ref
  8.9 0.3 shard_map.80
  9.1 1.8 %collective-permute-start.2 = (f32[408,128]{1,0:T(8,128)S(1)}, f32[408,128]{1,0:T(8,128)S(1)}, u32[]{:S(2)}, u32[]{:S(2)}) collective-permute-start(f32[408,128]{1,0:T(8,128)S(1)} %get-tuple-element.44), channel_id=1, source_target_pairs={{0,2},{1,3},{2,0},{3,1},{4,6},{5,7},{6,4},{7,5},{8,10},{9,11},{10,... | collective-permute-start | bytes 626696 | tf_op jit(solution)/shard_map/ppermute | solution.py:798
  10.9 0.0 collective-permute-start.3
  10.9 1.5 %collective-permute-start.4 = (f32[408,128]{1,0:T(8,128)S(1)}, f32[408,128]{1,0:T(8,128)S(1)}, u32[]{:S(2)}, u32[]{:S(2)}) collective-permute-start(f32[408,128]{1,0:T(8,128)S(1)} %get-tuple-element.59), channel_id=1, source_target_pairs={{0,1},{1,0},{2,3},{3,2},{4,5},{5,4},{6,7},{7,6},{8,16},{9,17},{10,... | collective-permute-start | bytes 626696 | tf_op jit(solution)/shard_map/ppermute | solution.py:798
  12.4 0.1 collective-permute-start.5
  12.5 1.3 %shard_map.81 = (f32[512,128]{1,0:T(8,128)S(1)}, f32[512,128]{1,0:T(8,128)S(1)}, f32[512,128]{1,0:T(8,128)S(1)}, f32[512,128]{1,0:T(8,128)S(1)}, f32[128,128]{1,0:T(8,128)S(1)}, /*index=5*/f32[128,128]{1,0:T(8,128)S(1)}) custom-call(f32[560,128]{1,0:T(8,128)S(1)} %get-tuple-element.43.block_ref), custom_call_target="tpu_custom_call" | custom-call | flops 1760000000 | bytes 5760000 | tf_op jit(solution)/shard_map/pallas_call | solution.py:768
  13.8 1.7 %collective-permute-done.2.first_ref = f32[408,128]{1,0:T(8,128)S(1)} collective-permute-done((f32[408,128]{1,0:T(8,128)S(1)}, f32[408,128]{1,0:T(8,128)S(1)}, u32[]{:S(2)}, u32[]{:S(2)}) %collective-permute-start.2) | collective-permute-done | bytes 208928 | tf_op jit(solution)/shard_map/ppermute | solution.py:798
  15.4 0.0 collective-permute-done.3.second_ref
  15.5 1.5 %collective-permute-start.6 = (f32[152,128]{1,0:T(8,128)S(1)}, f32[152,128]{1,0:T(8,128)S(1)}, u32[]{:S(2)}, u32[]{:S(2)}) collective-permute-start(f32[152,128]{1,0:T(8,128)S(1)} %get-tuple-element.68), channel_id=1, source_target_pairs={{0,1},{1,0},{2,3},{3,2},{4,5},{5,4},{6,7},{7,6},{8,16},{9,17},{10,... | collective-permute-start | bytes 233480 | tf_op jit(solution)/shard_map/ppermute | solution.py:798
  17.0 0.1 collective-permute-start.7
  17.1 1.0 %shard_map.82 = (f32[1152,128]{1,0:T(8,128)S(1)}, f32[832,128]{1,0:T(8,128)S(1)}, f32[320,128]{1,0:T(8,128)S(1)}, f32[448,128]{1,0:T(8,128)S(1)}) custom-call(f32[560,128]{1,0:T(8,128)S(1)} %get-tuple-element.43.block_ref, f32[408,128]{1,0:T(8,128)S(1)} %collective-permute-done.2.first_ref, f32[408,128]{1,0:T(8,128)S(1)} %collective-permute-done.3.second_ref, ...), custom_call_target="tpu_custom_call" | custom-call | flops 2200000000 | bytes 7200000 | tf_op jit(solution)/shard_map/pallas_call | solution.py:768
  18.0 0.5 %shard_map.83 = (f32[312,128]{1,0:T(8,128)S(1)}, f32[208,128]{1,0:T(8,128)S(1)}, f32[192,128]{1,0:T(8,128)S(1)}) custom-call(f32[1152,128]{1,0:T(8,128)S(1)} %get-tuple-element.49.cell.refs_0_, f32[832,128]{1,0:T(8,128)S(1)} %get-tuple-element.50.change.refs_1_, f32[320,128]{1,0:T(8,128)S(1)} %get-tuple-element.53.halo_wind_x.refs_5_, ...), custom_call_target="tpu_custom_call" | custom-call | flops 990000000 | bytes 3240000 | tf_op jit(solution)/shard_map/pallas_call | solution.py:768
  18.5 0.0 collective-permute-done.4.second_ref
  18.5 0.0 collective-permute-done.5.first_ref
  18.5 0.0 copy-start.3
  18.5 0.0 copy-start.4
  18.5 1.2 %shard_map.84 = (f32[832,128]{1,0:T(8,128)S(1)}, f32[448,128]{1,0:T(8,128)S(1)}, f32[320,128]{1,0:T(8,128)S(1)}, f32[320,128]{1,0:T(8,128)S(1)}, f32[80,128]{1,0...) custom-call(f32[1152,128]{1,0:T(8,128)S(1)} %get-tuple-element.49.cell.refs_0_, ...), custom_call_target="tpu_custom_call" | custom-call | flops 1870000000 | bytes 6120000 | tf_op jit(solution)/shard_map/pallas_call | solution.py:768
  19.8 0.2 collective-permute-done.6.refs_16_
  19.9 0.0 collective-permute-done.7.refs_17_
  19.9 0.0 copy-done.3
  19.9 0.0 copy-done.4
  20.0 1.7 %shard_map.86 = (f32[1352,128]{1,0:T(8,128)S(1)}, f32[176,128]{1,0:T(8,128)S(1)}, f32[176,128]{1,0:T(8,128)S(1)}) custom-call(f32[1152,128]{1,0:T(8,128)S(1)} %get-tuple-element.49.cell.refs_0_, f32[832,128]{1,0:T(8,128)S(1)} %get-tuple-element.50.change.refs_1_, f32[512,128]{1,0:T(8,128)S(1)} %get-tuple-element.51.wind_x.refs_2_, ...), custom_call_target="tpu_custom_call" | custom-call | flops 2860000000 | bytes 9360000 | tf_op jit(solution)/shard_map/pallas_call | solution.py:768
  21.6 1.5 %collective-permute-start.9 = (f32[176,128]{1,0:T(8,128)S(1)}, f32[176,128]{1,0:T(8,128)S(1)}, u32[]{:S(2)}, u32[]{:S(2)}) collective-permute-start(f32[176,128]{1,0:T(8,128)S(1)} %get-tuple-element.75), channel_id=1, source_target_pairs={{0,1},{1,0},{2,3},{3,2},{4,5},{5,4},{6,7},{7,6},{8,9},{9,8},{10,11... | collective-permute-start | bytes 270344 | tf_op jit(solution)/shard_map/ppermute | solution.py:904
  23.1 1.0 %shard_map.87 = (f32[104,128]{1,0:T(8,128)S(1)}, f32[104,128]{1,0:T(8,128)S(1)}) custom-call(f32[1352,128]{1,0:T(8,128)S(1)} %get-tuple-element.70.one, f32[1152,128]{1,0:T(8,128)S(1)} %get-tuple-element.49.cell.refs_0_, f32[512,128]{1,0:T(8,128)S(1)} %get-tuple-element.51.wind_x.refs_2_, f32[448,128]{1,0:T(8,128)S(1)} %get-tuple-element.62.refs_10_.far_wind_x, ...), custom_call_target="tpu_custom_call" | custom-call | flops 770000000 | bytes 2520000 | tf_op jit(solution)/shard_map/pallas_call | solution.py:768
  24.1 0.7 %collective-permute-start.8 = (f32[104,128]{1,0:T(8,128)S(1)}, f32[104,128]{1,0:T(8,128)S(1)}, u32[]{:S(2)}, u32[]{:S(2)}) collective-permute-start(f32[104,128]{1,0:T(8,128)S(1)} %get-tuple-element.72), channel_id=1, source_target_pairs={{0,1},{1,0},{2,3},{3,2},{4,5},{5,4},{6,7},{7,6},{8,9},{9,8},{10,11... | collective-permute-start | bytes 159752 | tf_op jit(solution)/shard_map/ppermute | solution.py:917
  24.8 1.8 %collective-permute-done.9.got_ref = f32[176,128]{1,0:T(8,128)S(1)} collective-permute-done((f32[176,128]{1,0:T(8,128)S(1)}, f32[176,128]{1,0:T(8,128)S(1)}, u32[]{:S(2)}, u32[]{:S(2)}) %collective-permute-start.9) | collective-permute-done | bytes 90144 | tf_op jit(solution)/shard_map/ppermute | solution.py:904
  26.6 1.5 %shard_map.88 = (f32[5,8,16,64]{3,2,1,0:T(8,128)S(1)}, f32[5,4,64]{2,1,0:T(4,128)S(1)}) custom-call(f32[176,128]{1,0:T(8,128)S(1)} %get-tuple-element.74.keep_ref, f32[176,128]{1,0:T(8,128)S(1)} %collective-permute-done.9.got_ref, bf16[4224,128]{1,0:T(8,128)(2,1)S(1)} %get-tuple-element.73.pairs_ref, bf16[128,128]{1,0:T(8,128)(2,1)S(1)} %get-tuple-element.42.lost_ref), custom_call_target="tpu_custom_call" | custom-call | flops 1980000000 | bytes 6480000 | tf_op jit(solution)/shard_map/pallas_call | solution.py:768
  28.1 0.2 collective-permute-done.8.got_ref
  28.3 1.7 %shard_map.89 = (f32[8,8,16,64]{3,2,1,0:T(8,128)}, f32[8,4,64]{2,1,0:T(4,128)}) custom-call(f32[104,128]{1,0:T(8,128)S(1)} %get-tuple-element.71.keep_ref, f32[104,128]{1,0:T(8,128)S(1)} %collective-permute-done.8.got_ref, bf16[4224,128]{1,0:T(8,128)(2,1)S(1)} %get-tuple-element.73.pairs_ref, bf16[128,128]{1,0:T(8,128)(2,1)S(1)} %get-tuple-element.42.lost_ref, ...), custom_call_target="tpu_custom_call" | custom-call | flops 1320000000 | bytes 4320000 | tf_op jit(solution)/shard_map/pallas_call | solution.py:768
  (1 shorter events, 0.0 us)
Async XLA Ops:
  0.6 1.0 %copy-start.1 = (f32[8,8,16,64]{3,2,1,0:T(8,128)S(1)}, f32[8,8,16,64]{3,2,1,0:T(8,128)}, u32[]{:S(2)}) copy-start(f32[8,8,16,64]{3,2,1,0:T(8,128)} %mass_ref.1) | copy-start | bytes 786436
  1.7 3.3 %copy-start.2 = (f32[3,8,8,16]{3,2,1,0:T(8,128)S(1)}, f32[3,8,8,16]{3,2,1,0:T(8,128)}, u32[]{:S(2)}) copy-start(f32[3,8,8,16]{3,2,1,0:T(8,128)} %wind_ref.1) | copy-start | bytes 36868
  1.7 4.0 %copy-start.5 = (bf16[4096,64]{0,1:T(8,128)(2,1)S(1)}, bf16[4096,64]{0,1:T(8,128)(2,1)}, u32[]{:S(2)}) copy-start(bf16[4096,64]{0,1:T(8,128)(2,1)} %param.10) | copy-start | bytes 1572868
  2.0 4.2 %copy-start = (bf16[64,64]{1,0:T(8,128)(2,1)S(1)}, bf16[64,64]{1,0:T(8,128)(2,1)}, u32[]{:S(2)}) copy-start(bf16[64,64]{1,0:T(8,128)(2,1)} %loss_ref.1) | copy-start | bytes 24580
  2.0 6.9 %collective-permute-start = (f32[256,128]{1,0:T(8,128)S(1)}, f32[256,128]{1,0:T(8,128)S(1)}, u32[]{:S(2)}, u32[]{:S(2)}) collective-permute-start(f32[256,128]{1,0:T(8,128)S(1)} %get-tuple-element.41), channel_id=1, source_target_pairs={{0,1},{1,0},{2,3},{3,2},{4,5},{5,4},{6,7},{7,6},{8,9},{9,8},{10,11... | collective-permute-start | bytes 393224 | tf_op jit(solution)/shard_map/ppermute | solution.py:824
  5.1 3.7 %collective-permute-start.1 = (f32[24,128]{1,0:T(8,128)S(1)}, f32[24,128]{1,0:T(8,128)S(1)}, u32[]{:S(2)}, u32[]{:S(2)}) collective-permute-start(f32[24,128]{1,0:T(8,128)S(1)} %shard_map.78.own_wind_ref), channel_id=1, source_target_pairs={{0,1},{1,0},{2,3},{3,2},{4,5},{5,4},{6,7},{7,6},{8,9},{9,8},{10,11... | collective-permute-start | bytes 36872 | tf_op jit(solution)/shard_map/ppermute | solution.py:826
  9.1 6.3 %collective-permute-start.2 = (f32[408,128]{1,0:T(8,128)S(1)}, f32[408,128]{1,0:T(8,128)S(1)}, u32[]{:S(2)}, u32[]{:S(2)}) collective-permute-start(f32[408,128]{1,0:T(8,128)S(1)} %get-tuple-element.44), channel_id=1, source_target_pairs={{0,2},{1,3},{2,0},{3,1},{4,6},{5,7},{6,4},{7,5},{8,10},{9,11},{10,... | collective-permute-start | bytes 626696 | tf_op jit(solution)/shard_map/ppermute | solution.py:798
  10.9 4.6 %collective-permute-start.3 = (f32[408,128]{1,0:T(8,128)S(1)}, f32[408,128]{1,0:T(8,128)S(1)}, u32[]{:S(2)}, u32[]{:S(2)}) collective-permute-start(f32[408,128]{1,0:T(8,128)S(1)} %get-tuple-element.45), channel_id=1, source_target_pairs={{0,8},{1,9},{2,4},{3,5},{4,2},{5,3},{6,14},{7,15},{8,0},{9,1},{10,... | collective-permute-start | bytes 626696 | tf_op jit(solution)/shard_map/ppermute | solution.py:798
  10.9 7.6 %collective-permute-start.4 = (f32[408,128]{1,0:T(8,128)S(1)}, f32[408,128]{1,0:T(8,128)S(1)}, u32[]{:S(2)}, u32[]{:S(2)}) collective-permute-start(f32[408,128]{1,0:T(8,128)S(1)} %get-tuple-element.59), channel_id=1, source_target_pairs={{0,1},{1,0},{2,3},{3,2},{4,5},{5,4},{6,7},{7,6},{8,16},{9,17},{10,... | collective-permute-start | bytes 626696 | tf_op jit(solution)/shard_map/ppermute | solution.py:798
  12.4 6.1 %collective-permute-start.5 = (f32[408,128]{1,0:T(8,128)S(1)}, f32[408,128]{1,0:T(8,128)S(1)}, u32[]{:S(2)}, u32[]{:S(2)}) collective-permute-start(f32[408,128]{1,0:T(8,128)S(1)} %get-tuple-element.60), channel_id=1, source_target_pairs={{0,8},{1,9},{2,10},{3,11},{4,12},{5,13},{6,14},{7,15},{8,0},{9,1},... | collective-permute-start | bytes 626696 | tf_op jit(solution)/shard_map/ppermute | solution.py:798
  15.5 4.5 %collective-permute-start.6 = (f32[152,128]{1,0:T(8,128)S(1)}, f32[152,128]{1,0:T(8,128)S(1)}, u32[]{:S(2)}, u32[]{:S(2)}) collective-permute-start(f32[152,128]{1,0:T(8,128)S(1)} %get-tuple-element.68), channel_id=1, source_target_pairs={{0,1},{1,0},{2,3},{3,2},{4,5},{5,4},{6,7},{7,6},{8,16},{9,17},{10,... | collective-permute-start | bytes 233480 | tf_op jit(solution)/shard_map/ppermute | solution.py:798
  17.0 3.0 %collective-permute-start.7 = (f32[152,128]{1,0:T(8,128)S(1)}, f32[152,128]{1,0:T(8,128)S(1)}, u32[]{:S(2)}, u32[]{:S(2)}) collective-permute-start(f32[152,128]{1,0:T(8,128)S(1)} %get-tuple-element.69), channel_id=1, source_target_pairs={{0,8},{1,9},{2,10},{3,11},{4,12},{5,13},{6,14},{7,15},{8,0},{9,1},... | collective-permute-start | bytes 233480 | tf_op jit(solution)/shard_map/ppermute | solution.py:798
  18.5 1.4 %copy-start.3 = (f32[64]{0:T(128)S(1)}, f32[64]{0:T(128)}, u32[]{:S(2)}) copy-start(f32[64]{0:T(128)} %param.8) | copy-start | bytes 772
  18.5 1.4 %copy-start.4 = (s32[64]{0:T(128)S(1)}, s32[64]{0:T(128)}, u32[]{:S(2)}) copy-start(s32[64]{0:T(128)} %param.9) | copy-start | bytes 772
  21.6 4.9 %collective-permute-start.9 = (f32[176,128]{1,0:T(8,128)S(1)}, f32[176,128]{1,0:T(8,128)S(1)}, u32[]{:S(2)}, u32[]{:S(2)}) collective-permute-start(f32[176,128]{1,0:T(8,128)S(1)} %get-tuple-element.75), channel_id=1, source_target_pairs={{0,1},{1,0},{2,3},{3,2},{4,5},{5,4},{6,7},{7,6},{8,9},{9,8},{10,11... | collective-permute-start | bytes 270344 | tf_op jit(solution)/shard_map/ppermute | solution.py:904
  24.1 4.2 %collective-permute-start.8 = (f32[104,128]{1,0:T(8,128)S(1)}, f32[104,128]{1,0:T(8,128)S(1)}, u32[]{:S(2)}, u32[]{:S(2)}) collective-permute-start(f32[104,128]{1,0:T(8,128)S(1)} %get-tuple-element.72), channel_id=1, source_target_pairs={{0,1},{1,0},{2,3},{3,2},{4,5},{5,4},{6,7},{7,6},{8,9},{9,8},{10,11... | collective-permute-start | bytes 159752 | tf_op jit(solution)/shard_map/ppermute | solution.py:917

commit v8 on v7

--- a/solution.py
+++ b/solution.py
@@ -14,7 +14,7 @@
 PAD_LO, PAD_HI = 2 * LO, 2 * HI
 LINES = LO + HI
 ROWS, LANES = 8, 128
-AHEAD = 4
+AHEAD = {3: 6, 5: 4}
 EARLY = 5
 F32 = jnp.float32
 VMEM = pl.BlockSpec(memory_space=pltpu.VMEM)
@@ -605,13 +605,14 @@
     ]
 
     rain = []
+    ahead = AHEAD[count]
     for some in [range(count)]:
         columns = [[fallen[eight(i * n, k)] for k in range(ROWS)] for i in some]
         drops = [jnp.zeros((ROWS, LANES), F32) for _ in some]
-        for block in range(SUBS // AHEAD):
-            columns = [column + [from_above(v, width) for v in column[:AHEAD]] for column in columns]
-            for s in range(AHEAD):
-                rate = jnp.where(block * AHEAD + s < steps, rates, 0.0)
+        for block in range(SUBS // ahead):
+            columns = [column + [from_above(v, width) for v in column[:ahead]] for column in columns]
+            for s in range(ahead):
+                rate = jnp.where(block * ahead + s < steps, rates, 0.0)
                 for i, column in enumerate(columns):
                     drops[i] = drops[i] + rate * column[0]
                     columns[i] = [v + rate * (u - v) for v, u in zip(column, column[1:])]

time: 30.2 us -> 30.2 us (level)
  no operation moved by 1% of the time
where the time goes in v8:
time: 30.2 us; the launch traced here: 30 us
  Pallas kernels  11.9 us (39%)
  starting transfers between devices  10.7 us (35%)
  waiting for transfers between devices  5.15 us (17%)
  local copies, waits for them, and re-layouts  1.54 us (5%)
  between operations  0.77 us (3%)
    pallas_call x13, Pallas kernels, call(): pl.pallas_call(kernel, out_shape=outs, in_specs=[VMEM] * len(args), out_s...  11.9 us
    ppermute x6, starting transfers between devices, swap_neighbours(): return lax.ppermute(message, axes, pairs)  4.94 us
    ppermute x1, starting transfers between devices, per_device(): got = lax.ppermute(send, 'gz', [(0, 1), (1, 0)])  3.03 us
    ppermute x6, waiting for transfers between devices, swap_neighbours(): return lax.ppermute(message, axes, pairs)  1.86 us
    ppermute x1, waiting for transfers between devices, per_device(): early_got = lax.ppermute(early[0], 'gz', [(0, 1), (1, 0)])  1.85 us
    unnamed x13, local copies, waits for them, and re-layouts  1.54 us
    ppermute x1, starting transfers between devices, per_device(): early_got = lax.ppermute(early[0], 'gz', [(0, 1), (1, 0)])  1.49 us
    ppermute x1, waiting for transfers between devices, per_device(): got_wind = lax.ppermute(own_wind, 'gz', [(0, 1), (1, 0)])  1.31 us
  transfers between devices with their start and end apart: 10, of which 5 were waited for; matrix products, arithmetic and copies ran while one was open for 2% of the time, Pallas kernels for 26%

profile of v8, /device:TPU:0, one launch (start us, length us, event | category | flops | bytes accessed | tf_op | source)
XLA Modules:
  0.0 30.0 jit_solution(3296862439430822311)
XLA Ops:
  0.6 0.0 copy-start.1
  0.6 1.0 %copy-done.1 = f32[8,8,16,64]{3,2,1,0:T(8,128)S(1)} copy-done((f32[8,8,16,64]{3,2,1,0:T(8,128)S(1)}, f32[8,8,16,64]{3,2,1,0:T(8,128)}, u32[]{:S(2)}) %copy-start.1) | copy-done | bytes 262168
  1.7 0.0 copy-start.2
  1.7 0.0 copy-start.5
  1.7 0.3 shard_map.77
  2.0 0.0 copy-start
  2.0 3.0 %collective-permute-start = (f32[256,128]{1,0:T(8,128)S(1)}, f32[256,128]{1,0:T(8,128)S(1)}, u32[]{:S(2)}, u32[]{:S(2)}) collective-permute-start(f32[256,128]{1,0:T(8,128)S(1)} %get-tuple-element.41), channel_id=1, source_target_pairs={{0,1},{1,0},{2,3},{3,2},{4,5},{5,4},{6,7},{7,6},{8,9},{9,8},{10,11... | collective-permute-start | bytes 393224 | tf_op jit(solution)/shard_map/ppermute | solution.py:825
  5.0 0.0 copy-done.2
  5.0 0.1 shard_map.78.own_wind_ref
  5.1 0.6 %collective-permute-start.1 = (f32[24,128]{1,0:T(8,128)S(1)}, f32[24,128]{1,0:T(8,128)S(1)}, u32[]{:S(2)}, u32[]{:S(2)}) collective-permute-start(f32[24,128]{1,0:T(8,128)S(1)} %shard_map.78.own_wind_ref), channel_id=1, source_target_pairs={{0,1},{1,0},{2,3},{3,2},{4,5},{5,4},{6,7},{7,6},{8,9},{9,8},{10,11... | collective-permute-start | bytes 36872 | tf_op jit(solution)/shard_map/ppermute | solution.py:827
  5.7 0.0 copy-done.5
  5.7 0.5 %copy.8.gain_ref = bf16[4096,64]{1,0:T(8,128)(2,1)S(1)} copy(bf16[4096,64]{0,1:T(8,128)(2,1)S(1)} %copy-done.5) | data formatting | bytes 1048576 | tf_op args[4]
  6.2 0.0 copy-done
  6.2 1.4 %shard_map.79 = (bf16[4224,128]{1,0:T(8,128)(2,1)S(1)}, bf16[128,128]{1,0:T(8,128)(2,1)S(1)}) custom-call(bf16[4096,64]{1,0:T(8,128)(2,1)S(1)} %copy.8.gain_ref, bf16[64,64]{1,0:T(8,128)(2,1)S(1)} %copy-done), custom_call_target="tpu_custom_call" | custom-call | flops 22000000 | bytes 72000 | tf_op jit(solution)/shard_map/pallas_call | solution.py:769
  7.5 1.3 %collective-permute-done.1.got_wind_ref = f32[24,128]{1,0:T(8,128)S(1)} collective-permute-done((f32[24,128]{1,0:T(8,128)S(1)}, f32[24,128]{1,0:T(8,128)S(1)}, u32[]{:S(2)}, u32[]{:S(2)}) %collective-permute-start.1) | collective-permute-done | bytes 12320 | tf_op jit(solution)/shard_map/ppermute | solution.py:827
  8.9 0.0 collective-permute-done.got_ref
  8.9 0.3 shard_map.80
  9.1 1.8 %collective-permute-start.2 = (f32[408,128]{1,0:T(8,128)S(1)}, f32[408,128]{1,0:T(8,128)S(1)}, u32[]{:S(2)}, u32[]{:S(2)}) collective-permute-start(f32[408,128]{1,0:T(8,128)S(1)} %get-tuple-element.44), channel_id=1, source_target_pairs={{0,2},{1,3},{2,0},{3,1},{4,6},{5,7},{6,4},{7,5},{8,10},{9,11},{10,... | collective-permute-start | bytes 626696 | tf_op jit(solution)/shard_map/ppermute | solution.py:799
  10.9 0.0 collective-permute-start.3
  10.9 1.5 %collective-permute-start.4 = (f32[408,128]{1,0:T(8,128)S(1)}, f32[408,128]{1,0:T(8,128)S(1)}, u32[]{:S(2)}, u32[]{:S(2)}) collective-permute-start(f32[408,128]{1,0:T(8,128)S(1)} %get-tuple-element.59), channel_id=1, source_target_pairs={{0,1},{1,0},{2,3},{3,2},{4,5},{5,4},{6,7},{7,6},{8,16},{9,17},{10,... | collective-permute-start | bytes 626696 | tf_op jit(solution)/shard_map/ppermute | solution.py:799
  12.4 0.1 collective-permute-start.5
  12.5 1.3 %shard_map.81 = (f32[512,128]{1,0:T(8,128)S(1)}, f32[512,128]{1,0:T(8,128)S(1)}, f32[512,128]{1,0:T(8,128)S(1)}, f32[512,128]{1,0:T(8,128)S(1)}, f32[128,128]{1,0:T(8,128)S(1)}, /*index=5*/f32[128,128]{1,0:T(8,128)S(1)}) custom-call(f32[560,128]{1,0:T(8,128)S(1)} %get-tuple-element.43.block_ref), custom_call_target="tpu_custom_call" | custom-call | flops 1760000000 | bytes 5760000 | tf_op jit(solution)/shard_map/pallas_call | solution.py:769
  13.8 1.7 %collective-permute-done.2.first_ref = f32[408,128]{1,0:T(8,128)S(1)} collective-permute-done((f32[408,128]{1,0:T(8,128)S(1)}, f32[408,128]{1,0:T(8,128)S(1)}, u32[]{:S(2)}, u32[]{:S(2)}) %collective-permute-start.2) | collective-permute-done | bytes 208928 | tf_op jit(solution)/shard_map/ppermute | solution.py:799
  15.4 0.0 collective-permute-done.3.second_ref
  15.5 1.5 %collective-permute-start.6 = (f32[152,128]{1,0:T(8,128)S(1)}, f32[152,128]{1,0:T(8,128)S(1)}, u32[]{:S(2)}, u32[]{:S(2)}) collective-permute-start(f32[152,128]{1,0:T(8,128)S(1)} %get-tuple-element.68), channel_id=1, source_target_pairs={{0,1},{1,0},{2,3},{3,2},{4,5},{5,4},{6,7},{7,6},{8,16},{9,17},{10,... | collective-permute-start | bytes 233480 | tf_op jit(solution)/shard_map/ppermute | solution.py:799
  17.0 0.1 collective-permute-start.7
  17.1 1.0 %shard_map.82 = (f32[1152,128]{1,0:T(8,128)S(1)}, f32[832,128]{1,0:T(8,128)S(1)}, f32[320,128]{1,0:T(8,128)S(1)}, f32[448,128]{1,0:T(8,128)S(1)}) custom-call(f32[560,128]{1,0:T(8,128)S(1)} %get-tuple-element.43.block_ref, f32[408,128]{1,0:T(8,128)S(1)} %collective-permute-done.2.first_ref, f32[408,128]{1,0:T(8,128)S(1)} %collective-permute-done.3.second_ref, ...), custom_call_target="tpu_custom_call" | custom-call | flops 2200000000 | bytes 7200000 | tf_op jit(solution)/shard_map/pallas_call | solution.py:769
  18.0 0.5 %shard_map.83 = (f32[312,128]{1,0:T(8,128)S(1)}, f32[208,128]{1,0:T(8,128)S(1)}, f32[192,128]{1,0:T(8,128)S(1)}) custom-call(f32[1152,128]{1,0:T(8,128)S(1)} %get-tuple-element.49.cell.refs_0_, f32[832,128]{1,0:T(8,128)S(1)} %get-tuple-element.50.change.refs_1_, f32[320,128]{1,0:T(8,128)S(1)} %get-tuple-element.53.halo_wind_x.refs_5_, ...), custom_call_target="tpu_custom_call" | custom-call | flops 990000000 | bytes 3240000 | tf_op jit(solution)/shard_map/pallas_call | solution.py:769
  18.5 0.0 collective-permute-done.4.second_ref
  18.5 0.0 collective-permute-done.5.first_ref
  18.5 0.0 copy-start.3
  18.5 0.0 copy-start.4
  18.5 1.2 %shard_map.84 = (f32[832,128]{1,0:T(8,128)S(1)}, f32[448,128]{1,0:T(8,128)S(1)}, f32[320,128]{1,0:T(8,128)S(1)}, f32[320,128]{1,0:T(8,128)S(1)}, f32[80,128]{1,0...) custom-call(f32[1152,128]{1,0:T(8,128)S(1)} %get-tuple-element.49.cell.refs_0_, ...), custom_call_target="tpu_custom_call" | custom-call | flops 1870000000 | bytes 6120000 | tf_op jit(solution)/shard_map/pallas_call | solution.py:769
  19.8 0.2 collective-permute-done.6.refs_16_
  19.9 0.0 collective-permute-done.7.refs_17_
  19.9 0.0 copy-done.3
  19.9 0.0 copy-done.4
  20.0 1.7 %shard_map.86 = (f32[1352,128]{1,0:T(8,128)S(1)}, f32[176,128]{1,0:T(8,128)S(1)}, f32[176,128]{1,0:T(8,128)S(1)}) custom-call(f32[1152,128]{1,0:T(8,128)S(1)} %get-tuple-element.49.cell.refs_0_, f32[832,128]{1,0:T(8,128)S(1)} %get-tuple-element.50.change.refs_1_, f32[512,128]{1,0:T(8,128)S(1)} %get-tuple-element.51.wind_x.refs_2_, ...), custom_call_target="tpu_custom_call" | custom-call | flops 2860000000 | bytes 9360000 | tf_op jit(solution)/shard_map/pallas_call | solution.py:769
  21.6 1.5 %collective-permute-start.9 = (f32[176,128]{1,0:T(8,128)S(1)}, f32[176,128]{1,0:T(8,128)S(1)}, u32[]{:S(2)}, u32[]{:S(2)}) collective-permute-start(f32[176,128]{1,0:T(8,128)S(1)} %get-tuple-element.75), channel_id=1, source_target_pairs={{0,1},{1,0},{2,3},{3,2},{4,5},{5,4},{6,7},{7,6},{8,9},{9,8},{10,11... | collective-permute-start | bytes 270344 | tf_op jit(solution)/shard_map/ppermute | solution.py:905
  23.1 0.9 %shard_map.87 = (f32[104,128]{1,0:T(8,128)S(1)}, f32[104,128]{1,0:T(8,128)S(1)}) custom-call(f32[1352,128]{1,0:T(8,128)S(1)} %get-tuple-element.70.one, f32[1152,128]{1,0:T(8,128)S(1)} %get-tuple-element.49.cell.refs_0_, f32[512,128]{1,0:T(8,128)S(1)} %get-tuple-element.51.wind_x.refs_2_, f32[448,128]{1,0:T(8,128)S(1)} %get-tuple-element.62.refs_10_.far_wind_x, ...), custom_call_target="tpu_custom_call" | custom-call | flops 770000000 | bytes 2520000 | tf_op jit(solution)/shard_map/pallas_call | solution.py:769
  24.1 0.7 %collective-permute-start.8 = (f32[104,128]{1,0:T(8,128)S(1)}, f32[104,128]{1,0:T(8,128)S(1)}, u32[]{:S(2)}, u32[]{:S(2)}) collective-permute-start(f32[104,128]{1,0:T(8,128)S(1)} %get-tuple-element.72), channel_id=1, source_target_pairs={{0,1},{1,0},{2,3},{3,2},{4,5},{5,4},{6,7},{7,6},{8,9},{9,8},{10,11... | collective-permute-start | bytes 159752 | tf_op jit(solution)/shard_map/ppermute | solution.py:918
  24.7 1.9 %collective-permute-done.9.got_ref = f32[176,128]{1,0:T(8,128)S(1)} collective-permute-done((f32[176,128]{1,0:T(8,128)S(1)}, f32[176,128]{1,0:T(8,128)S(1)}, u32[]{:S(2)}, u32[]{:S(2)}) %collective-permute-start.9) | collective-permute-done | bytes 90144 | tf_op jit(solution)/shard_map/ppermute | solution.py:905
  26.6 1.5 %shard_map.88 = (f32[5,8,16,64]{3,2,1,0:T(8,128)S(1)}, f32[5,4,64]{2,1,0:T(4,128)S(1)}) custom-call(f32[176,128]{1,0:T(8,128)S(1)} %get-tuple-element.74.keep_ref, f32[176,128]{1,0:T(8,128)S(1)} %collective-permute-done.9.got_ref, bf16[4224,128]{1,0:T(8,128)(2,1)S(1)} %get-tuple-element.73.pairs_ref, bf16[128,128]{1,0:T(8,128)(2,1)S(1)} %get-tuple-element.42.lost_ref), custom_call_target="tpu_custom_call" | custom-call | flops 1980000000 | bytes 6480000 | tf_op jit(solution)/shard_map/pallas_call | solution.py:769
  28.1 0.1 collective-permute-done.8.got_ref
  28.3 1.7 %shard_map.89 = (f32[8,8,16,64]{3,2,1,0:T(8,128)}, f32[8,4,64]{2,1,0:T(4,128)}) custom-call(f32[104,128]{1,0:T(8,128)S(1)} %get-tuple-element.71.keep_ref, f32[104,128]{1,0:T(8,128)S(1)} %collective-permute-done.8.got_ref, bf16[4224,128]{1,0:T(8,128)(2,1)S(1)} %get-tuple-element.73.pairs_ref, bf16[128,128]{1,0:T(8,128)(2,1)S(1)} %get-tuple-element.42.lost_ref, ...), custom_call_target="tpu_custom_call" | custom-call | flops 1320000000 | bytes 4320000 | tf_op jit(solution)/shard_map/pallas_call | solution.py:769
  (1 shorter events, 0.0 us)
Async XLA Ops:
  0.6 1.0 %copy-start.1 = (f32[8,8,16,64]{3,2,1,0:T(8,128)S(1)}, f32[8,8,16,64]{3,2,1,0:T(8,128)}, u32[]{:S(2)}) copy-start(f32[8,8,16,64]{3,2,1,0:T(8,128)} %mass_ref.1) | copy-start | bytes 786436
  1.7 3.3 %copy-start.2 = (f32[3,8,8,16]{3,2,1,0:T(8,128)S(1)}, f32[3,8,8,16]{3,2,1,0:T(8,128)}, u32[]{:S(2)}) copy-start(f32[3,8,8,16]{3,2,1,0:T(8,128)} %wind_ref.1) | copy-start | bytes 36868
  1.7 4.0 %copy-start.5 = (bf16[4096,64]{0,1:T(8,128)(2,1)S(1)}, bf16[4096,64]{0,1:T(8,128)(2,1)}, u32[]{:S(2)}) copy-start(bf16[4096,64]{0,1:T(8,128)(2,1)} %param.10) | copy-start | bytes 1572868
  2.0 4.2 %copy-start = (bf16[64,64]{1,0:T(8,128)(2,1)S(1)}, bf16[64,64]{1,0:T(8,128)(2,1)}, u32[]{:S(2)}) copy-start(bf16[64,64]{1,0:T(8,128)(2,1)} %loss_ref.1) | copy-start | bytes 24580
  2.0 6.9 %collective-permute-start = (f32[256,128]{1,0:T(8,128)S(1)}, f32[256,128]{1,0:T(8,128)S(1)}, u32[]{:S(2)}, u32[]{:S(2)}) collective-permute-start(f32[256,128]{1,0:T(8,128)S(1)} %get-tuple-element.41), channel_id=1, source_target_pairs={{0,1},{1,0},{2,3},{3,2},{4,5},{5,4},{6,7},{7,6},{8,9},{9,8},{10,11... | collective-permute-start | bytes 393224 | tf_op jit(solution)/shard_map/ppermute | solution.py:825
  5.1 3.7 %collective-permute-start.1 = (f32[24,128]{1,0:T(8,128)S(1)}, f32[24,128]{1,0:T(8,128)S(1)}, u32[]{:S(2)}, u32[]{:S(2)}) collective-permute-start(f32[24,128]{1,0:T(8,128)S(1)} %shard_map.78.own_wind_ref), channel_id=1, source_target_pairs={{0,1},{1,0},{2,3},{3,2},{4,5},{5,4},{6,7},{7,6},{8,9},{9,8},{10,11... | collective-permute-start | bytes 36872 | tf_op jit(solution)/shard_map/ppermute | solution.py:827
  9.1 6.3 %collective-permute-start.2 = (f32[408,128]{1,0:T(8,128)S(1)}, f32[408,128]{1,0:T(8,128)S(1)}, u32[]{:S(2)}, u32[]{:S(2)}) collective-permute-start(f32[408,128]{1,0:T(8,128)S(1)} %get-tuple-element.44), channel_id=1, source_target_pairs={{0,2},{1,3},{2,0},{3,1},{4,6},{5,7},{6,4},{7,5},{8,10},{9,11},{10,... | collective-permute-start | bytes 626696 | tf_op jit(solution)/shard_map/ppermute | solution.py:799
  10.9 4.6 %collective-permute-start.3 = (f32[408,128]{1,0:T(8,128)S(1)}, f32[408,128]{1,0:T(8,128)S(1)}, u32[]{:S(2)}, u32[]{:S(2)}) collective-permute-start(f32[408,128]{1,0:T(8,128)S(1)} %get-tuple-element.45), channel_id=1, source_target_pairs={{0,8},{1,9},{2,4},{3,5},{4,2},{5,3},{6,14},{7,15},{8,0},{9,1},{10,... | collective-permute-start | bytes 626696 | tf_op jit(solution)/shard_map/ppermute | solution.py:799
  10.9 7.6 %collective-permute-start.4 = (f32[408,128]{1,0:T(8,128)S(1)}, f32[408,128]{1,0:T(8,128)S(1)}, u32[]{:S(2)}, u32[]{:S(2)}) collective-permute-start(f32[408,128]{1,0:T(8,128)S(1)} %get-tuple-element.59), channel_id=1, source_target_pairs={{0,1},{1,0},{2,3},{3,2},{4,5},{5,4},{6,7},{7,6},{8,16},{9,17},{10,... | collective-permute-start | bytes 626696 | tf_op jit(solution)/shard_map/ppermute | solution.py:799
  12.4 6.1 %collective-permute-start.5 = (f32[408,128]{1,0:T(8,128)S(1)}, f32[408,128]{1,0:T(8,128)S(1)}, u32[]{:S(2)}, u32[]{:S(2)}) collective-permute-start(f32[408,128]{1,0:T(8,128)S(1)} %get-tuple-element.60), channel_id=1, source_target_pairs={{0,8},{1,9},{2,10},{3,11},{4,12},{5,13},{6,14},{7,15},{8,0},{9,1},... | collective-permute-start | bytes 626696 | tf_op jit(solution)/shard_map/ppermute | solution.py:799
  15.5 4.5 %collective-permute-start.6 = (f32[152,128]{1,0:T(8,128)S(1)}, f32[152,128]{1,0:T(8,128)S(1)}, u32[]{:S(2)}, u32[]{:S(2)}) collective-permute-start(f32[152,128]{1,0:T(8,128)S(1)} %get-tuple-element.68), channel_id=1, source_target_pairs={{0,1},{1,0},{2,3},{3,2},{4,5},{5,4},{6,7},{7,6},{8,16},{9,17},{10,... | collective-permute-start | bytes 233480 | tf_op jit(solution)/shard_map/ppermute | solution.py:799
  17.0 3.0 %collective-permute-start.7 = (f32[152,128]{1,0:T(8,128)S(1)}, f32[152,128]{1,0:T(8,128)S(1)}, u32[]{:S(2)}, u32[]{:S(2)}) collective-permute-start(f32[152,128]{1,0:T(8,128)S(1)} %get-tuple-element.69), channel_id=1, source_target_pairs={{0,8},{1,9},{2,10},{3,11},{4,12},{5,13},{6,14},{7,15},{8,0},{9,1},... | collective-permute-start | bytes 233480 | tf_op jit(solution)/shard_map/ppermute | solution.py:799
  18.5 1.4 %copy-start.3 = (f32[64]{0:T(128)S(1)}, f32[64]{0:T(128)}, u32[]{:S(2)}) copy-start(f32[64]{0:T(128)} %param.8) | copy-start | bytes 772
  18.5 1.4 %copy-start.4 = (s32[64]{0:T(128)S(1)}, s32[64]{0:T(128)}, u32[]{:S(2)}) copy-start(s32[64]{0:T(128)} %param.9) | copy-start | bytes 772
  21.6 5.0 %collective-permute-start.9 = (f32[176,128]{1,0:T(8,128)S(1)}, f32[176,128]{1,0:T(8,128)S(1)}, u32[]{:S(2)}, u32[]{:S(2)}) collective-permute-start(f32[176,128]{1,0:T(8,128)S(1)} %get-tuple-element.75), channel_id=1, source_target_pairs={{0,1},{1,0},{2,3},{3,2},{4,5},{5,4},{6,7},{7,6},{8,9},{9,8},{10,11... | collective-permute-start | bytes 270344 | tf_op jit(solution)/shard_map/ppermute | solution.py:905
  24.1 4.2 %collective-permute-start.8 = (f32[104,128]{1,0:T(8,128)S(1)}, f32[104,128]{1,0:T(8,128)S(1)}, u32[]{:S(2)}, u32[]{:S(2)}) collective-permute-start(f32[104,128]{1,0:T(8,128)S(1)} %get-tuple-element.72), channel_id=1, source_target_pairs={{0,1},{1,0},{2,3},{3,2},{4,5},{5,4},{6,7},{7,6},{8,9},{9,8},{10,11... | collective-permute-start | bytes 159752 | tf_op jit(solution)/shard_map/ppermute | solution.py:918
